TPU v7x, 128 devices: a whole 4x4x4 slice. The times are simulated.
128 devices in a mesh: row: 32 (over y, x, core), col: 4 (over z).
Axes of the slice: x: 4, y: 4, z: 4, core: 2. Of those that a mesh axis runs over, the one named last changes fastest.
Arguments:
- momentum: bfloat16 [16384, 26624], P(('row', 'col')), may hold values from -18 to 18
- gradient: bfloat16 [16384, 26624], P(('row', 'col')), may hold values from -9 to 9
- right_factor: bfloat16 [512, 26624], P('row', 'col'), may hold values from -0.0390625 to 0.0390625
Outputs:
- new_momentum: bfloat16 [16384, 26624], P('row', 'col')
- left_factor: float32 [16384, 512], P(('row', 'col'))
- new_right: float32 [512, 26624], P('row', 'col')
All inputs are finite; a program needn't handle non-finite values.
Results may differ from a plain program's by a relative error of at most 0.017.
Values may be sent and summed in bfloat16 or wider, within the bound.
No kernel may reach another device: no remote copies, remote signals or barrier semaphores. Data moves between devices by JAX's collectives and lax.ppermute only.
A program may use at most 128 MiB of HBM per device.

v0:
```python
import jax
import jax.numpy as jnp
from jax import lax
from jax.sharding import PartitionSpec as P

D = 16384


def orthonormalize(projected, gram_total):
    lower = jnp.linalg.cholesky(gram_total)
    identity = jnp.eye(gram_total.shape[0], dtype=gram_total.dtype)
    inverse = jax.scipy.linalg.solve_triangular(lower, identity, lower=True)
    return jnp.dot(projected, inverse.T, precision=lax.Precision.HIGHEST)


def per_device(momentum, gradient, right_factor):
    blend = (momentum.astype(jnp.float32) + gradient.astype(jnp.float32)).astype(jnp.bfloat16)
    regrouped = lax.all_to_all(blend, "col", split_axis=1, concat_axis=0, tiled=True)
    block_rows = regrouped.shape[0]
    ranks_dev = right_factor.shape[0]
    partial_proj = lax.dot_general(
        regrouped,
        lax.all_gather(right_factor, "row", axis=0, tiled=True),
        (((1,), (1,)), ((), ())),
        preferred_element_type=jnp.float32,
    )
    projected = lax.psum(partial_proj.astype(jnp.bfloat16), "col").astype(jnp.float32)
    gram_part = jnp.dot(projected.T, projected, precision=lax.Precision.HIGHEST)
    gram_total = lax.psum(gram_part.astype(jnp.bfloat16), "row").astype(jnp.float32)
    orthonormal = orthonormalize(projected, gram_total)
    orth_half = orthonormal.astype(jnp.bfloat16)
    share_rows = block_rows // lax.axis_size("col")
    left_local = lax.dynamic_slice_in_dim(
        orthonormal, lax.axis_index("col") * share_rows, share_rows, 0
    )
    partial_right = lax.dot_general(
        orth_half, regrouped, (((0,), (0,)), ((), ())), preferred_element_type=jnp.float32
    )
    right_totals = lax.psum(partial_right.astype(jnp.bfloat16), "row").astype(jnp.float32)
    right_raw = lax.dynamic_slice_in_dim(
        right_totals, lax.axis_index("row") * ranks_dev, ranks_dev, 0
    )
    right_rounded = right_totals.astype(jnp.bfloat16)
    squares = lax.psum(jnp.sum(right_raw * right_raw, axis=1), "col")
    new_right = right_raw / jnp.sqrt(squares + 1e-06)[:, None]
    feedback = jnp.dot(orth_half, right_rounded, preferred_element_type=jnp.float32)
    new_momentum = (regrouped.astype(jnp.float32) - 0.75 * feedback).astype(jnp.bfloat16)
    left_factor = left_local * float(D) ** 0.5
    return (new_momentum, left_factor, new_right)


def solution(mesh):
    in_specs = (P(("row", "col"), None), P(("row", "col"), None), P("row", "col"))
    out_specs = (P("row", "col"), P(("row", "col"), None), P("row", "col"))
    return jax.shard_map(
        per_device, mesh=mesh, in_specs=in_specs, out_specs=out_specs, check_vma=False
    )
```

profile of v0, /device:TPU:1, one launch (start us, length us, event | category | flops | bytes accessed | tf_op | source)
XLA Modules:
  0.0 573.2 jit_solution(9468540600345991133)
XLA Ops:
  7.9 9.3 %add_convert_fusion = bf16[128,26624]{1,0:T(8,128)(2,1)} fusion(bf16[128,26624]{1,0:T(8,128)(2,1)} %param.4, bf16[128,26624]{1,0:T(8,128)(2,1)} %param.3), kind=kLoop, calls=%fused_computation.3 | loop fusion | flops 13631488 | bytes 20447232 | tf_op jit(solution)/shard_map/convert_element_type | solution.py:17
  17.3 3.4 copy.12
  20.7 81.7 %all_to_all.19 = bf16[128,4,6656]{2,0,1:T(8,128)(2,1)} all-to-all(bf16[128,4,6656]{2,0,1:T(8,128)(2,1)S(1)} %bitcast.68), channel_id=1, replica_groups=mesh['row'=32,'col'=4] {'col'}, dimensions={1} | all-to-all | bytes 13631488 | tf_op jit(solution)/shard_map/all_to_all | solution.py:18
  102.5 9.4 %convolution_convert_fusion.2 = bf16[512,512]{1,0:T(8,128)(2,1)} fusion(bf16[512,6656]{1,0:T(8,128)(2,1)} %bitcast.62, bf16[512,6656]{1,0:T(8,128)(2,1)} %all-gather.2.cloned.1.call-done), kind=kOutput, calls=%fused_computation.7 | convolution fusion | flops 3489923072 | bytes 14155776 | tf_op jit(solution)/shard_map/dot_general | solution.py:21
  111.9 41.9 %all-reduce.5.cloned.1.call-done = bf16[512,512]{1,0:T(8,128)(2,1)} async-done(((bf16[512,512]{1,0:T(8,128)(2,1)}), bf16[512,512]{1,0:T(8,128)(2,1)}) %all-reduce.5.cloned.1.call-update) | async-done | bytes 524304 | tf_op jit(solution)/shard_map/psum | solution.py:27
  153.8 2.5 convolution_convert_fusion.1
  156.9 0.8 iota_compare_fusion
  157.7 1.1 fusion.18
  158.8 104.6 %all-reduce.7.cloned.1.call-done = bf16[512,512]{0,1:T(8,128)(2,1)} async-done(((bf16[512,512]{0,1:T(8,128)(2,1)}), bf16[512,512]{0,1:T(8,128)(2,1)}) %all-reduce.7.cloned.1.call-update) | async-done | bytes 524304 | tf_op jit(solution)/shard_map/psum | solution.py:29
  263.4 1.3 copy.8
  264.7 1.2 fusion.8
  265.9 11.7 %cholesky.104 = f32[128,128]{1,0:T(8,128)S(1)} custom-call(f32[128,128]{1,0:T(8,128)S(1)} %cholesky.266), custom_call_target="Cholesky" | custom-call | tf_op jit(solution)/shard_map/jit(cholesky)/cholesky | solution.py:10
  277.7 1.1 cholesky.224
  278.8 9.8 %custom-call.31 = f32[1,128,128]{1,2,0:T(8,128)S(1)} custom-call(f32[1,128,128]{2,1,0:T(8,128)S(1)} %get-tuple-element.30), custom_call_target="InvertDiagBlocksLowerTriangular" | custom-call | tf_op jit(solution)/shard_map/jit(cholesky)/cholesky | solution.py:10
  288.6 1.0 constant_dynamic-update-slice_fusion.2
  289.6 1.4 convolution_subtract_fusion.3
  291.0 11.7 %cholesky.217 = f32[128,128]{1,0:T(8,128)S(1)} custom-call(f32[128,128]{1,0:T(8,128)S(1)} %cholesky.270), custom_call_target="Cholesky" | custom-call | tf_op jit(solution)/shard_map/jit(cholesky)/cholesky | solution.py:10
  303.4 10.0 %custom-call.32 = f32[1,128,128]{1,2,0:T(8,128)S(1)} custom-call(f32[1,128,128]{2,1,0:T(8,128)S(1)} %get-tuple-element.27), custom_call_target="InvertDiagBlocksLowerTriangular" | custom-call | tf_op jit(solution)/shard_map/jit(cholesky)/cholesky | solution.py:10
  313.3 0.9 convolution_dynamic-update-slice_fusion
  314.3 1.4 convolution_subtract_fusion.4
  315.7 11.7 %cholesky.238 = f32[128,128]{1,0:T(8,128)S(1)} custom-call(f32[128,128]{1,0:T(8,128)S(1)} %cholesky.275), custom_call_target="Cholesky" | custom-call | tf_op jit(solution)/shard_map/jit(cholesky)/cholesky | solution.py:10
  328.1 9.8 %custom-call.33 = f32[1,128,128]{1,2,0:T(8,128)S(1)} custom-call(f32[1,128,128]{2,1,0:T(8,128)S(1)} %get-tuple-element.24), custom_call_target="InvertDiagBlocksLowerTriangular" | custom-call | tf_op jit(solution)/shard_map/jit(cholesky)/cholesky | solution.py:10
  337.9 0.8 convolution_dynamic-update-slice_fusion.1
  338.7 1.4 convolution_subtract_fusion.5
  340.1 11.7 %cholesky.255 = f32[128,128]{1,0:T(8,128)S(1)} custom-call(f32[128,128]{1,0:T(8,128)S(1)} %convolution_subtract_fusion.5), custom_call_target="Cholesky" | custom-call | tf_op jit(solution)/shard_map/jit(cholesky)/cholesky | solution.py:10
  352.5 0.7 compare_reduce_fusion.1
  353.8 0.7 compare_reduce_fusion.2
  357.2 2.3 select_select_fusion
  359.6 14.1 %while.1 = (s32[]{:T(128)}, f32[512,512]{1,0:T(8,128)}, s32[4,2]{0,1:T(2,128)S(1)}, f32[4,128,128]{2,1,0:T(8,128)}, s32[]{:T(128)}) while((s32[]{:T(128)}, f32[512,512]{1,0:T(8,128)}, s32[4,2]{0,1:T(2,128)S(1)}, f32[4,128,128]{2,1,0:T(8,128)}, s32[]{:T(128)}) %tuple.31), condition=%wide.while_cond, body=%wide.while_body.sunk | while | flops 2 | bytes 132205 | solution.py:12
  360.2 2.9 bitcast_dynamic-update-slice_fusion.2
  363.7 2.9 bitcast_dynamic-update-slice_fusion.2
  367.3 2.9 bitcast_dynamic-update-slice_fusion.2
  370.8 2.8 bitcast_dynamic-update-slice_fusion.2
  373.6 40.1 %custom-call.34 = f32[4,128,128]{1,2,0:T(8,128)S(1)} custom-call(f32[4,128,128]{2,1,0:T(8,128)} %get-tuple-element.10), custom_call_target="InvertDiagBlocksLowerTriangular" | custom-call | tf_op jit(solution)/shard_map/jit(_solve_triangular)/triangular_solve | solution.py:12
  413.8 1.1 fusion.22
  414.9 1.5 convolution_subtract_fusion.1
  416.8 1.4 convolution_subtract_fusion
  418.7 1.7 convolution_subtract_fusion.2
  420.8 1.1 fusion
  421.9 1.0 copy-done.2
  422.9 5.8 %convolution_convert_fusion = bf16[512,6656]{1,0:T(8,128)(2,1)} fusion(bf16[512,6656]{1,0:T(8,128)(2,1)S(1)} %bitcast.66, f32[512,512]{1,0:T(8,128)S(1)} %fusion), kind=kOutput, calls=%fused_computation.4 | convolution fusion | flops 3493330944 | bytes 14680064 | tf_op jit(solution)/shard_map/dot_general | solution.py:36
  428.7 1.2 copy-done.3
  429.9 0.7 dynamic-slice_multiply_fusion
  430.6 114.6 %all-reduce.9.cloned.1.call-done = bf16[512,6656]{1,0:T(8,128)(2,1)} async-done(((bf16[512,6656]{1,0:T(8,128)(2,1)}), bf16[512,6656]{1,0:T(8,128)(2,1)}) %all-reduce.9.cloned.1.call-update) | async-done | bytes 6815760 | tf_op jit(solution)/shard_map/psum | solution.py:39
  545.2 1.1 fusion.17
  546.3 8.7 %psum.31 = f32[16]{0:T(128)S(1)} all-reduce(f32[16]{0:T(128)S(1)} %fusion.17), channel_id=1, replica_groups=mesh['row'=32,'col'=4] {'col'}, use_global_device_ids=true, to_apply=%region_12.13 | all-reduce | flops 16 | bytes 128 | tf_op jit(solution)/shard_map/psum | solution.py:44
  555.0 9.6 %subtract_convert_fusion = bf16[512,6656]{1,0:T(8,128)(2,1)} fusion(bf16[512,6656]{1,0:T(8,128)(2,1)} %bitcast.63, bf16[512,6656]{1,0:T(8,128)(2,1)} %all-reduce.9.cloned.1.call-done, f32[512,512]{1,0:T(8,128)S(1)} %copy-done.3), kind=kOutput, calls=%fused_computation.2 | convolution fusion | flops 3503554560 | bytes 21495808 | tf_op jit(solution)/shard_map/dot_general | solution.py:46
  564.6 1.8 convert_divide_fusion
  (43 shorter events, 7.9 us)
Async XLA Ops:
  7.2 95.3 %all-gather.2.cloned.1.call-start = ((), (), s32[]{:S(2)}) async-start(), calls=%async_computation.1 | async-start | bytes 7028736 | tf_op jit(solution)/shard_map/all_gather | solution.py:23
  7.9 145.9 %all-reduce.5.cloned.1.call-start = ((), (), s32[]{:S(2)}) async-start(), calls=%async_computation.2 | async-start | bytes 1048576 | tf_op jit(solution)/shard_map/psum | solution.py:27
  111.9 151.5 %all-reduce.7.cloned.1.call-start = ((), (), s32[]{:S(2)}) async-start(), calls=%async_computation.3 | async-start | bytes 1048576 | tf_op jit(solution)/shard_map/psum | solution.py:29
  156.4 388.8 %all-reduce.9.cloned.1.call-start = ((), (), s32[]{:S(2)}) async-start(), calls=%async_computation.4 | async-start | bytes 13631488 | tf_op jit(solution)/shard_map/psum | solution.py:39
  265.9 22.7 %copy-start = (f32[512,512]{1,0:T(8,128)}, f32[512,512]{1,0:T(8,128)S(1)}, u32[]{:S(2)}) copy-start(f32[512,512]{1,0:T(8,128)S(1)} %fusion.8) | copy-start | bytes 3145732
  265.9 154.9 %copy-start.1 = (bf16[512,512]{1,0:T(8,128)(2,1)S(1)}, bf16[512,512]{1,0:T(8,128)(2,1)}, u32[]{:S(2)}) copy-start(bf16[512,512]{1,0:T(8,128)(2,1)} %all-reduce.5.cloned.1.call-done) | copy-start | bytes 1572868
  289.6 133.3 %slice-start = ((s8[6815744]{0:T(1024)(128)(4,1)}), s8[2621440]{0:T(1024)(128)(4,1)S(1)}, s32[]{:S(2)}) async-start(s8[6815744]{0:T(1024)(128)(4,1)} %bitcast.64), calls=%async_computation.5 | async-start | bytes 5242880
  414.9 8.0 %slice-start.1 = ((s8[6815744]{0:T(1024)(128)(4,1)}), s8[4194304]{0:T(1024)(128)(4,1)S(1)}, s32[]{:S(2)}) async-start(s8[6815744]{0:T(1024)(128)(4,1)} %bitcast.64), calls=%async_computation.6 | async-start | bytes 8388608
  421.9 1.0 copy-start.2
  428.6 1.2 copy-start.3
Sparse Core Ops, SparseCore 0:
  10.2 53.4 all-gather.1
  112.0 41.7 all-reduce.4
  157.6 105.7 all-reduce.6
  428.8 116.3 all-reduce.8
where the time goes:
time: 580 us; the launch traced here: 573 us
  waiting for transfers between devices  262 us (45%)
  other arithmetic  139 us (24%)
  blocking collectives  90.4 us (16%)
  matrix products  42.3 us (7%)
  local copies, waits for them, and re-layouts  22.1 us (4%)
  between operations  16.9 us (3%)
    psum x1, waiting for transfers between devices, per_device(): lax.psum(partial_right.astype(jnp.bfloat16), 'row').astype(jnp.float32)  115 us
    psum x1, waiting for transfers between devices, per_device(): lax.psum(gram_part.astype(jnp.bfloat16), 'row').astype(jnp.float32)  105 us
    all_to_all x1, blocking collectives, per_device(): lax.all_to_all(blend, 'col', split_axis=1, concat_axis=0, tiled=True)  81.7 us
    another operation x14, other arithmetic, orthonormalize(): lower = jnp.linalg.cholesky(gram_total)  80.4 us
    another operation x3, other arithmetic, orthonormalize(): inverse = jax.scipy.linalg.solve_triangular(lower, identity, lower=True)  42.5 us
    psum x1, waiting for transfers between devices, per_device(): lax.psum(partial_proj.astype(jnp.bfloat16), 'col').astype(jnp.float32)  41.9 us
    another operation x12, local copies, waits for them, and re-layouts  14.1 us
  transfers between devices with their start and end apart: 4, of which 3 were waited for; matrix products, arithmetic and copies ran while one was open for 3% of the time, Pallas kernels for 0%

commit v1 on v0

v1 whole, which is shorter than its diff:
```python
import jax
import jax.numpy as jnp
from jax import lax
from jax.experimental import pallas as pl
from jax.experimental.pallas import tpu as pltpu
from jax.sharding import PartitionSpec as P

D = 16384
HI=lax.Precision.HIGHEST
B=128
PANEL=8

def diagonal_inverse(a_ref, x_ref):
    row = lax.broadcasted_iota(jnp.int32, (B, B), 0)
    col = lax.broadcasted_iota(jnp.int32, (B, B), 1)
    x_ref[...] = jnp.where(row == col, 1.0, 0.0)
    panels = B // PANEL
    full = (PANEL, B)
    for p in range(panels):
        at = p * PANEL
        mine = a_ref[at:at + PANEL, :]
        xmine = x_ref[at:at + PANEL, :]
        cols = [jnp.broadcast_to(mine[:, at + j:at + j + 1], full) for j in range(PANEL)]
        a = {(i, j): jnp.broadcast_to(cols[j][i:i + 1, :], full) for j in range(PANEL) for i in range(j, PANEL)}
        inv = []
        for k in range(PANEL):
            inv.append(lax.rsqrt(a[k, k]))
            for i in range(k + 1, PANEL):
                a[i, k] = a[i, k] * inv[k]
            for j in range(k + 1, PANEL):
                for i in range(j, PANEL):
                    a[i, j] = a[i, j] - a[i, k] * a[j, k]
        def forward(block):
            y = []
            for i in range(PANEL):
                r = jnp.broadcast_to(block[i:i + 1, :], full)
                for j in range(i):
                    r = r - a[i, j] * y[j]
                y.append(r * inv[i])
            return y
        def backward(y):
            z = [None] * PANEL
            for i in range(PANEL - 1, -1, -1):
                r = y[i]
                for j in range(i + 1, PANEL):
                    r = r - a[j, i] * z[j]
                z[i] = r * inv[i]
            return z
        yx = forward(xmine)
        sub = lax.broadcasted_iota(jnp.int32, full, 0)
        out = yx[0]
        for i in range(1, PANEL):
            out = jnp.where(sub == i, yx[i], out)
        x_ref[at:at + PANEL, :] = out
        if p + 1 < panels:
            za = backward(forward(mine))
            zx = backward(yx)
            for q in range(p + 1, panels):
                s = slice(q * PANEL, (q + 1) * PANEL)
                block = a_ref[s, :]
                da = 0.0
                dx = 0.0
                for j in range(PANEL):
                    m = jnp.broadcast_to(block[:, at + j:at + j + 1], full)
                    da = da + m * za[j]
                    dx = dx + m * zx[j]
                a_ref[s, :] = block - da
                x_ref[s, :] = x_ref[s, :] - dx

def chol_kernel(g_ref, x_ref, a_s, d_s, i_s):
    n = g_ref.shape[0]
    nb = n // B
    a_s[...] = g_ref[...].astype(jnp.float32)
    x_ref[...] = jnp.zeros_like(x_ref)
    def dot(u, v, dims):
        return lax.dot_general(u, v, (dims, ((), ())), precision=HI, preferred_element_type=jnp.float32)
    def step(b, _):
        at = pl.multiple_of(b * B, B)
        here = pl.ds(at, B)
        d_s[...] = a_s[here, here]
        diagonal_inverse(d_s, i_s)
        inv = i_s[...]
        x_ref[here, here] = inv
        left = dot(inv, x_ref[here, :], ((1,), (0,)))
        lane = lax.broadcasted_iota(jnp.int32, (B, n), 1)
        own = (lane >= at) & (lane < at + B)
        wide = jnp.concatenate([inv] * nb, axis=1)
        y_x = jnp.where(own, wide, left)
        x_ref[here, :] = y_x
        @pl.when(b < nb - 1)
        def _():
            y_a = dot(inv, a_s[here, :], ((1,), (0,)))
            y_a = jnp.where(lane >= at + B, y_a, 0.0)
            a_s[...] = a_s[...] - dot(y_a, y_a, ((0,), (0,)))
            x_ref[...] = x_ref[...] - dot(y_a, y_x, ((0,), (0,)))
        return 0
    lax.fori_loop(0, nb, step, 0)

def cholesky_inverse(gram):
    n = gram.shape[0]
    return pl.pallas_call(
        chol_kernel,
        out_shape=jax.ShapeDtypeStruct((n, n), jnp.float32),
        in_specs=[pl.BlockSpec(memory_space=pltpu.VMEM)],
        out_specs=pl.BlockSpec(memory_space=pltpu.VMEM),
        scratch_shapes=[pltpu.VMEM((n, n), jnp.float32), pltpu.VMEM((B, B), jnp.float32), pltpu.VMEM((B, B), jnp.float32)],
        compiler_params=pltpu.CompilerParams(vmem_limit_bytes=16 * 2**20),
        cost_estimate=pl.CostEstimate(flops=2 * 10**9, bytes_accessed=2 * 2**20, transcendentals=0),
        name="cholesky_inverse",
    )(gram)


def per_device(momentum, gradient, right_factor):
    f32, half = jnp.float32, jnp.bfloat16
    ranks_dev = right_factor.shape[0]
    rows = lax.axis_size("row")
    cols = lax.axis_size("col")
    right_all = lax.all_gather(right_factor, "row", axis=0, tiled=True)
    blend = (momentum.astype(f32) + gradient.astype(f32)).astype(half)
    regrouped = lax.all_to_all(blend, "col", split_axis=1, concat_axis=0, tiled=True)
    block_rows = regrouped.shape[0]
    share = block_rows // cols
    ranks = right_all.shape[0]
    partial = lax.dot_general(
        regrouped, right_all, (((1,), (1,)), ((), ())), preferred_element_type=f32
    ).astype(half)
    pieces = lax.all_to_all(partial, "col", split_axis=0, concat_axis=0, tiled=True)
    mine = jnp.sum(pieces.reshape(cols, share, ranks).astype(f32), axis=0).astype(half)
    projected = lax.all_gather(mine, "col", axis=0, tiled=True)
    cross = lax.dot_general(
        projected, regrouped, (((0,), (0,)), ((), ())), preferred_element_type=f32
    ).astype(half)
    cross_total = lax.psum(cross, "row")
    gram_part = lax.dot_general(
        projected, projected, (((0,), (0,)), ((), ())), preferred_element_type=f32
    ).astype(half)
    gram_pieces = lax.all_to_all(gram_part, "row", split_axis=0, concat_axis=0, tiled=True)
    gram_mine = jnp.sum(gram_pieces.reshape(rows, ranks // rows, ranks).astype(f32), axis=0)
    gram = lax.all_gather(gram_mine.astype(half), "row", axis=0, tiled=True).astype(f32)
    inverse = cholesky_inverse(gram)
    left_local = jnp.dot(mine.astype(f32), inverse.T, precision=HI)
    left_factor = left_local * float(D) ** 0.5
    orthonormal = jnp.dot(projected.astype(f32), inverse.T, precision=HI)
    weights = (0.75 * jnp.dot(orthonormal, inverse, precision=HI)).astype(half)
    own = lax.dynamic_slice_in_dim(inverse, lax.axis_index("row") * ranks_dev, ranks_dev, 0)
    high = own.astype(half)
    low = (own - high.astype(f32)).astype(half)
    both = jnp.dot(
        jnp.concatenate([high, low], axis=0), cross_total, preferred_element_type=f32
    )
    right_raw = both[:ranks_dev] + both[ranks_dev:]
    squares = lax.psum(jnp.sum(right_raw * right_raw, axis=1), "col")
    feedback = jnp.dot(weights, cross_total, preferred_element_type=f32)
    new_momentum = (regrouped.astype(f32) - feedback).astype(half)
    new_right = right_raw / jnp.sqrt(squares + 1e-06)[:, None]
    return (new_momentum, left_factor, new_right)


def solution(mesh):
    in_specs = (P(("row", "col"), None), P(("row", "col"), None), P("row", "col"))
    out_specs = (P("row", "col"), P(("row", "col"), None), P("row", "col"))
    return jax.shard_map(
        per_device, mesh=mesh, in_specs=in_specs, out_specs=out_specs, check_vma=False
    )
```

time: 580 us -> 299 us (0.52)
  waiting for transfers between devices: 262 us -> 53.9 us
  other arithmetic: 139 us -> 10.7 us
  blocking collectives: 90.4 us -> 135 us
  Pallas kernels: 0 us -> 30.9 us
  local copies, waits for them, and re-layouts: 22.1 us -> 3.45 us
  starting transfers between devices: 0.62 us -> 12.2 us
    psum x3 -> x1, waiting for transfers between devices: 261 us -> 39.9 us  [per_device(): cross_total = lax.psum(cross, 'row')]
    another operation x17 -> x0, other arithmetic: 123 us -> none  [the longest x14 80.4 us: orthonormalize(): lower = jnp.linalg.cholesky(gram_total)]
    all_gather x0 -> x2, blocking collectives: none -> 34.5 us  [the longest x1 23.9 us: per_device(): lax.all_gather(gram_mine.astype(half), 'row', axis=0, tiled=True)]
    pallas_call x0 -> x1, Pallas kernels: none -> 30.9 us  [cholesky_inverse(): pl.pallas_call(chol_kernel, out_shape=jax.ShapeDtypeStruct((n, n), jnp.fl...]
    another operation x17 -> x0, local copies, waits for them, and re-layouts: 15.2 us -> none
    another operation x13 -> x0, matrix products: 14 us -> none  [the longest x7 6.99 us: orthonormalize(): inverse = jax.scipy.linalg.solve_triangular(lower, identity, lower=True)]
    all_to_all x0 -> x1, waiting for transfers between devices: none -> 13.3 us  [per_device(): lax.all_to_all(gram_part, 'row', split_axis=0, concat_axis=0, tiled=True)]
    all_to_all x0 -> x1, starting transfers between devices: none -> 12.1 us  [per_device(): lax.all_to_all(gram_part, 'row', split_axis=0, concat_axis=0, tiled=True)]
  transfers between devices with their start and end apart: 4 -> 3, of which waited for: 3 -> 2; matrix products, arithmetic and copies ran while one was open for 3% -> 6% of each run, Pallas kernels for 0% -> 10%
where the time goes in v1:
time: 299 us; the launch traced here: 297 us
  blocking collectives  135 us (45%)
  waiting for transfers between devices  53.9 us (18%)
  matrix products  36.6 us (12%)
  Pallas kernels  30.9 us (10%)
  between operations  14.1 us (5%)
  starting transfers between devices  12.2 us (4%)
  other arithmetic  10.7 us (4%)
  local copies, waits for them, and re-layouts  3.45 us (1%)
    all_to_all x1, blocking collectives, per_device(): lax.all_to_all(blend, 'col', split_axis=1, concat_axis=0, tiled=True)  81.7 us
    psum x1, waiting for transfers between devices, per_device(): cross_total = lax.psum(cross, 'row')  39.9 us
    pallas_call x1, Pallas kernels, cholesky_inverse(): pl.pallas_call(chol_kernel, out_shape=jax.ShapeDtypeStruct((n, n), jnp.fl...  30.9 us
    all_gather x1, blocking collectives, per_device(): lax.all_gather(gram_mine.astype(half), 'row', axis=0, tiled=True)  23.9 us
    all_to_all x1, waiting for transfers between devices, per_device(): lax.all_to_all(gram_part, 'row', split_axis=0, concat_axis=0, tiled=True)  13.3 us
    all_to_all x1, starting transfers between devices, per_device(): lax.all_to_all(gram_part, 'row', split_axis=0, concat_axis=0, tiled=True)  12.1 us
    all_gather x1, blocking collectives, per_device(): projected = lax.all_gather(mine, 'col', axis=0, tiled=True)  10.6 us
    all_to_all x1, blocking collectives, per_device(): lax.all_to_all(partial, 'col', split_axis=0, concat_axis=0, tiled=True)  10 us
  transfers between devices with their start and end apart: 3, of which 2 were waited for; matrix products, arithmetic and copies ran while one was open for 6% of the time, Pallas kernels for 10%

profile of v1, /device:TPU:1, one launch (start us, length us, event | category | flops | bytes accessed | tf_op | source)
XLA Modules:
  0.0 296.7 jit_solution(17583923710375515583)
XLA Ops:
  7.2 0.0 all-gather.2.cloned.1.call-start
  7.2 0.7 all-gather.2.cloned.1.call-update
  7.9 0.0 all-reduce.2.cloned.1.call-start
  7.9 9.3 %add_convert_fusion = bf16[128,26624]{1,0:T(8,128)(2,1)} fusion(bf16[128,26624]{1,0:T(8,128)(2,1)} %param.4, bf16[128,26624]{1,0:T(8,128)(2,1)} %param.3), kind=kLoop, calls=%fused_computation.1 | loop fusion | flops 13631488 | bytes 20447232 | tf_op jit(solution)/shard_map/convert_element_type | solution.py:119
  17.3 3.4 %copy.9 = bf16[16,4,8,6656]{3,2,0,1:T(8,128)(2,1)S(1)} copy(bf16[16,4,8,6656]{3,2,1,0:T(8,128)(2,1)} %bitcast.24) | data formatting | bytes 13631488 | tf_op jit(solution)/shard_map/all_to_all | solution.py:120
  20.7 81.7 %all_to_all.37 = bf16[128,4,6656]{2,0,1:T(8,128)(2,1)} all-to-all(bf16[128,4,6656]{2,0,1:T(8,128)(2,1)S(1)} %bitcast.28), channel_id=1, replica_groups=mesh['row'=32,'col'=4] {'col'}, dimensions={1} | all-to-all | bytes 13631488 | tf_op jit(solution)/shard_map/all_to_all | solution.py:120
  102.5 0.0 all-gather.2.cloned.1.call-done
  102.5 8.6 %convolution_convert_fusion.2 = bf16[512,512]{1,0:T(8,128)(2,1)S(1)} fusion(bf16[512,6656]{1,0:T(8,128)(2,1)} %bitcast.25, bf16[512,6656]{1,0:T(8,128)(2,1)} %all-gather.2.cloned.1.call-done), kind=kOutput, calls=%fused_computation.7 | convolution fusion | flops 3489923072 | bytes 14155776 | tf_op jit(solution)/shard_map/dot_general | solution.py:124
  111.1 10.0 %all_to_all.38 = bf16[4,128,512]{2,1,0:T(8,128)(2,1)S(1)} all-to-all(bf16[4,128,512]{2,1,0:T(8,128)(2,1)S(1)} %bitcast.29), channel_id=1, replica_groups=mesh['row'=32,'col'=4] {'col'}, dimensions={0} | all-to-all | bytes 1048576 | tf_op jit(solution)/shard_map/all_to_all | solution.py:127
  121.1 0.1 reduce_sum.33
  121.2 10.6 %all_gather.10 = bf16[512,512]{1,0:T(8,128)(2,1)S(1)} all-gather(bf16[128,512]{1,0:T(8,128)(2,1)S(1)} %reduce_sum.33), channel_id=1, replica_groups=mesh['row'=32,'col'=4] {'col'}, dimensions={0}, use_global_device_ids=true | all-gather | bytes 655360 | tf_op jit(solution)/shard_map/all_gather | solution.py:129
  131.7 8.6 %convolution_convert_fusion = bf16[512,6656]{1,0:T(8,128)(2,1)} fusion(bf16[512,512]{1,0:T(8,128)(2,1)S(1)} %all_gather.10, bf16[512,6656]{1,0:T(8,128)(2,1)} %bitcast.26), kind=kOutput, calls=%fused_computation.2 | convolution fusion | flops 3493068800 | bytes 14155776 | tf_op jit(solution)/shard_map/dot_general | solution.py:130
  140.4 0.0 all-reduce.2.cloned.1.call-update
  140.4 1.3 convolution_convert_fusion.1
  141.7 12.1 %all-to-all-start.2 = ((bf16[32,16,512]{2,1,0:T(8,128)(2,1)}), bf16[32,16,512]{2,1,0:T(8,128)(2,1)S(1)}, u32[]{:S(2)}, u32[]{:S(2)}) async-start(bf16[32,16,512]{2,1,0:T(8,128)(2,1)} %bitcast.4), calls=%async_computation.2 | async-start | bytes 1048576 | tf_op jit(solution)/shard_map/all_to_all | solution.py:137
  153.8 13.3 %all-to-all-done.2 = bf16[32,16,512]{2,1,0:T(8,128)(2,1)S(1)} async-done(((bf16[32,16,512]{2,1,0:T(8,128)(2,1)}), bf16[32,16,512]{2,1,0:T(8,128)(2,1)S(1)}, u32[]{:S(2)}, u32[]{:S(2)}) %all-to-all-start.2) | async-done | bytes 524320 | tf_op jit(solution)/shard_map/all_to_all | solution.py:137
  167.1 0.1 reduce_sum.34
  167.2 23.9 %all_gather.11 = bf16[512,512]{1,0:T(8,128)(2,1)S(1)} all-gather(bf16[16,512]{1,0:T(8,128)(2,1)S(1)} %reduce_sum.34), channel_id=1, replica_groups=mesh['row'=32,'col'=4] {'row'}, dimensions={0}, use_global_device_ids=true | all-gather | bytes 540672 | tf_op jit(solution)/shard_map/all_gather | solution.py:139
  191.1 0.1 convert_element_type.51.g_ref
  191.2 30.9 %cholesky_inverse.1 = f32[512,512]{1,0:T(8,128)S(1)} custom-call(f32[512,512]{1,0:T(8,128)S(1)} %convert_element_type.51.g_ref), custom_call_target="tpu_custom_call" | custom-call | flops 2000000000 | bytes 2097152 | tf_op jit(solution)/shard_map/cholesky_inverse/pallas_call | solution.py:101
  222.1 1.4 convolution_multiply_fusion.1
  223.5 1.1 fusion.6
  224.6 1.8 fusion
  226.5 39.9 %all-reduce.2.cloned.1.call-done = bf16[512,6656]{1,0:T(8,128)(2,1)} async-done(((bf16[512,6656]{1,0:T(8,128)(2,1)}), bf16[512,6656]{1,0:T(8,128)(2,1)}) %all-reduce.2.cloned.1.call-update) | async-done | bytes 6815760 | tf_op jit(solution)/shard_map/psum | solution.py:133
  266.3 4.2 %fusion.1 = f32[32,6656]{1,0:T(8,128)S(1)} fusion(bf16[512,6656]{1,0:T(8,128)(2,1)} %all-reduce.2.cloned.1.call-done, bf16[16,512]{1,0:T(8,128)(2,1)S(1)} %get-tuple-element.3, bf16[16,512]{1,0:T(8,128)(2,1)S(1)} %get-tuple-element.4), kind=kOutput, calls=%fused_computation.12 | convolution fusion | flops 218169344 | bytes 7700480 | tf_op jit(solution)/shard_map/dot_general | solution.py:148
  270.5 0.2 multiply_reduce_fusion
  270.7 8.7 %psum.15 = f32[16]{0:T(128)S(1)} all-reduce(f32[16]{0:T(128)S(1)} %multiply_reduce_fusion), channel_id=1, replica_groups=mesh['row'=32,'col'=4] {'col'}, use_global_device_ids=true, to_apply=%region_4.0 | all-reduce | flops 16 | bytes 128 | tf_op jit(solution)/shard_map/psum | solution.py:152
  279.4 0.9 broadcast_divide_fusion
  280.3 9.6 %subtract_convert_fusion = bf16[512,6656]{1,0:T(8,128)(2,1)} fusion(bf16[512,6656]{1,0:T(8,128)(2,1)} %bitcast.27, bf16[512,512]{1,0:T(8,128)(2,1)S(1)} %fusion, bf16[512,6656]{1,0:T(8,128)(2,1)} %all-reduce.2.cloned.1.call-done), kind=kOutput, calls=%fused_computation | convolution fusion | flops 3499884544 | bytes 20971520 | tf_op jit(solution)/shard_map/dot_general | solution.py:153
  (2 shorter events, 0.0 us)
Async XLA Ops:
  7.2 95.3 %all-gather.2.cloned.1.call-start = ((), (), s32[]{:S(2)}) async-start(), calls=%async_computation.3 | async-start | bytes 7028736 | tf_op jit(solution)/shard_map/all_gather | solution.py:118
  7.9 258.4 %all-reduce.2.cloned.1.call-start = ((), (), s32[]{:S(2)}) async-start(), calls=%async_computation.4 | async-start | bytes 13631488 | tf_op jit(solution)/shard_map/psum | solution.py:133
  141.7 25.5 %all-to-all-start.2 = ((bf16[32,16,512]{2,1,0:T(8,128)(2,1)}), bf16[32,16,512]{2,1,0:T(8,128)(2,1)S(1)}, u32[]{:S(2)}, u32[]{:S(2)}) async-start(bf16[32,16,512]{2,1,0:T(8,128)(2,1)} %bitcast.4), calls=%async_computation.2 | async-start | bytes 1048576 | tf_op jit(solution)/shard_map/all_to_all | solution.py:137
Sparse Core Ops, SparseCore 0:
  10.2 53.4 all-gather.1
  140.5 125.7 all-reduce.1

commit v2 on v0

v2 whole, which is shorter than its diff:
```python
import functools
import math

import jax
import jax.numpy as jnp
from jax import lax
from jax.experimental import pallas as pl
from jax.experimental.pallas import tpu as pltpu
from jax.sharding import Mesh, PartitionSpec as P

D = 16384
HI=lax.Precision.HIGHEST
B=128
PANEL=8

def total(terms):
    while len(terms) > 1:
        terms = [sum(terms[i:i + 2][1:], terms[i]) for i in range(0, len(terms), 2)]
    return terms[0]


def diagonal_inverse(a_ref, x_ref):
    row = lax.broadcasted_iota(jnp.int32, (B, B), 0)
    col = lax.broadcasted_iota(jnp.int32, (B, B), 1)
    x_ref[...] = jnp.where(row == col, 1.0, 0.0)
    panels = B // PANEL
    full = (PANEL, B)
    for p in range(panels):
        at = p * PANEL
        mine = a_ref[at:at + PANEL, :]
        xmine = x_ref[at:at + PANEL, :]
        cols = [jnp.broadcast_to(mine[:, at + j:at + j + 1], full) for j in range(PANEL)]
        a = {(i, j): jnp.broadcast_to(cols[j][i:i + 1, :], full) for j in range(PANEL) for i in range(j, PANEL)}
        low = {}
        for k in range(PANEL):
            root = lax.rsqrt(a[k, k])
            for i in range(k + 1, PANEL):
                a[i, k] = a[i, k] * root
            for j in range(k + 1, PANEL):
                for i in range(j, PANEL):
                    a[i, j] = a[i, j] - a[i, k] * a[j, k]
            for j in range(k):
                low[k, j] = -root * total([a[k, i] * low[i, j] for i in range(j, k)])
            low[k, k] = root

        def forward(block):
            r = [jnp.broadcast_to(block[i:i + 1, :], full) for i in range(PANEL)]
            return [total([low[i, j] * r[j] for j in range(i + 1)]) for i in range(PANEL)]

        def backward(y):
            return [total([low[j, i] * y[j] for j in range(i, PANEL)]) for i in range(PANEL)]

        yx = forward(xmine)
        sub = lax.broadcasted_iota(jnp.int32, full, 0)
        out = yx[0]
        for i in range(1, PANEL):
            out = jnp.where(sub == i, yx[i], out)
        x_ref[at:at + PANEL, :] = out
        if p + 1 < panels:
            za = backward(forward(mine))
            zx = backward(yx)
            for q in range(p + 1, panels):
                s = slice(q * PANEL, (q + 1) * PANEL)
                block = a_ref[s, :]
                m = [jnp.broadcast_to(block[:, at + j:at + j + 1], full) for j in range(PANEL)]
                a_ref[s, :] = block - total([m[j] * za[j] for j in range(PANEL)])
                x_ref[s, :] = x_ref[s, :] - total([m[j] * zx[j] for j in range(PANEL)])

def factor_kernel(at_ref, g_ref, *refs):
    factors, outs, scratch = refs[:4], refs[4:7], refs[7:]
    own_ref, weights_ref, left_ref, a_s, x_ref, d_s, i_s, sems = scratch
    copies = [
        pltpu.make_async_copy(ref, out, sems.at[i])
        for i, (ref, out) in enumerate(zip((own_ref, weights_ref, left_ref), outs))
    ]
    n = g_ref.shape[0]
    nb = n // B
    a_s[...] = g_ref[...].astype(jnp.float32)
    x_ref[...] = jnp.zeros_like(x_ref)

    def split(value):
        high = value.astype(jnp.bfloat16)
        return high, (value - high.astype(jnp.float32)).astype(jnp.bfloat16)

    def half_dot(u, v, dims):
        return lax.dot_general(u, v, (dims, ((), ())), preferred_element_type=jnp.float32)

    def dot(u, v, dims):
        (u_high, u_low), (v_high, v_low) = u, v
        return half_dot(u_high, v_high, dims) + (half_dot(u_high, v_low, dims) + half_dot(u_low, v_high, dims))

    def step(b, _):
        at = pl.multiple_of(b * B, B)
        here = pl.ds(at, B)
        d_s[...] = a_s[here, here]
        diagonal_inverse(d_s, i_s)
        for k in range(nb):
            @pl.when(b == k)
            def _(here=slice(k * B, (k + 1) * B), before=k * B, rest=slice((k + 1) * B, n)):
                inv = split(i_s[...])
                x_ref[here, here] = i_s[...]
                if before:
                    x_ref[here, :before] = dot(inv, split(x_ref[here, :before]), ((1,), (0,)))
                if rest.start < n:
                    y_x = split(x_ref[here, :here.stop])
                    y_a = split(dot(inv, split(a_s[here, rest]), ((1,), (0,))))
                    a_s[rest, rest] = a_s[rest, rest] - dot(y_a, y_a, ((0,), (0,)))
                    x_ref[rest, :here.stop] = x_ref[rest, :here.stop] - dot(y_a, y_x, ((0,), (0,)))
        return 0

    lax.fori_loop(0, nb, step, 0)

    count = own_ref.shape[0] // 2
    own = x_ref[pl.ds(pl.multiple_of(at_ref[0] * count, count), count), :]
    own_ref[:count, :], own_ref[count:, :] = split(own)
    copies[0].start()
    high, low = split(x_ref[...])
    factor = jnp.concatenate([f[...] for f in factors], axis=1)
    turned = half_dot(high, factor, ((1,), (0,))) + half_dot(low, factor, ((1,), (0,)))
    rows = left_ref.shape[0]
    left_ref[...] = turned[:, :rows].T * float(D) ** 0.5
    copies[2].start()
    turned_high, turned_low = split(turned)
    weights = half_dot(turned_high, high, ((0,), (0,)))
    weights += half_dot(turned_low, high, ((0,), (0,)))
    weights += half_dot(turned_high, low, ((0,), (0,)))
    weights_ref[...] = (0.75 * weights).astype(jnp.bfloat16)
    copies[1].start()
    for copy in copies:
        copy.wait()


def factorize(gram, factors, place, count):
    n = gram.shape[0]
    rows = factors[0].shape[1]
    vmem = pl.BlockSpec(memory_space=pltpu.VMEM)
    outs = [((2 * count, n), jnp.bfloat16), ((4 * rows, n), jnp.bfloat16), ((rows, n), jnp.float32)]
    return pl.pallas_call(
        factor_kernel,
        out_shape=[pltpu.HBM(*out) for out in outs],
        in_specs=[pl.BlockSpec(memory_space=pltpu.SMEM)] + [vmem] * 5,
        out_specs=[pl.BlockSpec(memory_space=pltpu.HBM)] * 3,
        scratch_shapes=[pltpu.VMEM(*out) for out in outs]
        + [pltpu.VMEM((n, n), jnp.float32)] * 2
        + [pltpu.VMEM((B, B), jnp.float32)] * 2
        + [pltpu.SemaphoreType.DMA((3,))],
        compiler_params=pltpu.CompilerParams(vmem_limit_bytes=16 * 2**20),
        cost_estimate=pl.CostEstimate(flops=2 * 10**10, bytes_accessed=4 * 2**20, transcendentals=0),
        name="factorize",
    )(jnp.full((1,), place, jnp.int32), gram, *factors)


TILE = 1664
CHUNK = 512
QUARTER = 128
EIGHTH = 32
F32 = jnp.float32
HALF = jnp.bfloat16
VMEM = pl.BlockSpec(memory_space=pltpu.VMEM)
SMEM = pl.BlockSpec(memory_space=pltpu.SMEM)
HBM = pl.BlockSpec(memory_space=pltpu.HBM)


def ring(value, axis, shift):
    size = lax.axis_size(axis)
    return lax.ppermute(value, axis, [(i, (i + shift) % size) for i in range(size)])


def swap_cores(value):
    return lax.ppermute(value, "core", [(0, 1), (1, 0)])


def in_hbm(values):
    return [pltpu.with_memory_space_constraint(value, pltpu.HBM) for value in values]


def call(kernel, name, operands, out_shape, scratch=(), in_specs=None, out_specs=None, flops=0):
    shapes = out_shape if isinstance(out_shape, list) else [out_shape]
    moved = sum(math.prod(v.shape) * v.dtype.itemsize for v in list(operands) + shapes)
    return pl.pallas_call(
        kernel,
        in_specs=in_specs or [VMEM] * len(operands),
        out_specs=out_specs or ([VMEM] * len(shapes) if isinstance(out_shape, list) else VMEM),
        out_shape=out_shape,
        scratch_shapes=list(scratch),
        compiler_params=pltpu.CompilerParams(vmem_limit_bytes=16 * 2**20),
        cost_estimate=pl.CostEstimate(flops=int(flops), bytes_accessed=int(moved), transcendentals=0),
        name=name,
    )(*operands)


def project_kernel(half, *refs):
    blocks, right = refs[:4], refs[4]
    rows, width = blocks[0].shape
    total = refs[5][...] if half else 0.0
    for at in range(0, width, TILE):
        block = jnp.concatenate([b[:, at:at + TILE] for b in blocks], axis=0)
        total += lax.dot_general(
            block,
            right[:, half * width + at:half * width + at + TILE],
            (((1,), (1,)), ((), ())),
            preferred_element_type=F32,
        )
    if half:
        for i, out in enumerate(refs[6:]):
            out[...] = total[i * rows:(i + 1) * rows].astype(HALF)
    else:
        refs[5][...] = total


def project(blocks, right, half, before=None):
    rows, width = blocks[0].shape
    ranks = right.shape[0]
    if half:
        out_shape = [jax.ShapeDtypeStruct((rows, ranks), HALF)] * 4
    else:
        out_shape = jax.ShapeDtypeStruct((4 * rows, ranks), F32)
    return call(
        functools.partial(project_kernel, half),
        "project",
        [*blocks, right] + ([before] if half else []),
        out_shape,
        flops=8 * rows * width * ranks,
    )


def settle_kernel(*refs):
    terms, out, turned = refs[:4], refs[4], refs[5]
    total = terms[0][...].astype(F32)
    for term in terms[1:]:
        total += term[...].astype(F32)
    out[...] = total.astype(HALF)
    turned[...] = total.T.astype(HALF)


def settle(terms):
    rows, ranks = terms[0].shape
    return call(
        settle_kernel,
        "settle",
        terms,
        [jax.ShapeDtypeStruct((rows, ranks), HALF), jax.ShapeDtypeStruct((ranks, rows), HALF)],
        flops=4 * rows * ranks,
    )


def gram_kernel(*refs):
    total = 0.0
    for factor in refs[:4]:
        total += lax.dot_general(
            factor[...], factor[...], (((1,), (1,)), ((), ())), preferred_element_type=F32
        )
    refs[4][...] = total.astype(HALF)


def gram_of(factors):
    ranks, rows = factors[0].shape
    return call(
        gram_kernel,
        "gram",
        factors,
        jax.ShapeDtypeStruct((ranks, ranks), HALF),
        flops=8 * rows * ranks * ranks,
    )


def spread_kernel(pieces_ref, out_ref):
    total = pieces_ref[0].astype(F32)
    for i in range(1, pieces_ref.shape[0]):
        total += pieces_ref[i].astype(F32)
    out_ref[...] = jnp.broadcast_to(total.astype(HALF)[None], out_ref.shape)


def spread(pieces):
    return call(spread_kernel, "spread", [pieces], jax.ShapeDtypeStruct(pieces.shape, HALF), flops=pieces.size)


def cross_kernel(half, adds, at_ref, *refs):
    factors, blocks = refs[:4], refs[4:8]
    extra = refs[8] if adds else None
    outs, (mixed, held, sems) = refs[8 + adds:-3], refs[-3:]
    rows = blocks[0].shape[0]
    base = pl.multiple_of(at_ref[0] * TILE, 128)
    copies = []
    for turn in range(4):
        quarter = lax.rem(at_ref[1] + turn, 4)
        for part in range(4):
            at = part * QUARTER + quarter * EIGHTH if half == 0 else quarter * QUARTER + part * EIGHTH
            to = turn * QUARTER + part * EIGHTH
            for i in range(4):
                mixed[to:to + EIGHTH, i * rows:(i + 1) * rows] = factors[i][
                    pl.ds(pl.multiple_of(at, EIGHTH), EIGHTH), :
                ]
    factor = mixed[...]
    for at in range(0, TILE, 512):
        size = min(512, TILE - at)
        block = jnp.concatenate([b[:, pl.ds(pl.multiple_of(base + at, 128), size)] for b in blocks], axis=0)
        total = jnp.dot(factor, block, preferred_element_type=F32)
        here = slice(at, at + size)
        for turn in range(4):
            value = total[turn * QUARTER:(turn + 1) * QUARTER]
            if adds:
                value = value + extra[turn, :, here].astype(F32)
            held[turn, :, here] = value.astype(HALF)
            out = outs[turn] if adds else outs[0].at[turn]
            copies.append(
                pltpu.make_async_copy(held.at[turn, :, here], out.at[:, here], sems.at[len(copies)])
            )
            copies[-1].start()
    for copy in copies:
        copy.wait()


def cross(factors, blocks, tile, half, at, extra=None):
    rows, width = blocks[0].shape
    ranks = factors[0].shape[0]
    adds = extra is not None
    if adds:
        out_shape = [pltpu.HBM((QUARTER, TILE), HALF)] * 4
    else:
        out_shape = pltpu.HBM((4, QUARTER, TILE), HALF)
    return call(
        functools.partial(cross_kernel, half, adds),
        "cross_add" if adds else "cross",
        [jnp.stack([tile, at]).astype(jnp.int32), *factors, *blocks] + ([extra] if adds else []),
        out_shape,
        in_specs=[SMEM] + [VMEM] * (8 + adds),
        out_specs=[HBM] * 4 if adds else HBM,
        scratch=[
            pltpu.VMEM((ranks, 4 * rows), HALF),
            pltpu.VMEM((4, QUARTER, TILE), HALF),
            pltpu.SemaphoreType.DMA((16,)),
        ],
        flops=8 * rows * TILE * ranks,
    )


def fold_kernel(at_ref, *refs):
    terms, outs, (taken, held, in_sems, out_sems) = refs[:4], refs[4:8], refs[8:]
    loads = [pltpu.make_async_copy(terms[i], taken.at[i], in_sems.at[i]) for i in range(4)]
    stores = [pltpu.make_async_copy(held.at[i], outs[i], out_sems.at[i]) for i in range(4)]
    for load in loads:
        load.start()
    for load in loads:
        load.wait()
    for turn in range(4):
        at = lax.rem(at_ref[0] + turn, 4) * EIGHTH
        here = pl.ds(pl.multiple_of(at, EIGHTH), EIGHTH)
        total = taken[0, here, :].astype(F32)
        for i in range(1, 4):
            total += taken[i, here, :].astype(F32)
        held[turn] = total.astype(HALF)
        stores[turn].start()
    for store in stores:
        store.wait()


def fold(terms, at):
    return call(
        fold_kernel,
        "fold",
        [jnp.full((1,), at, jnp.int32), *in_hbm(terms)],
        [pltpu.HBM((EIGHTH, TILE), HALF)] * 4,
        in_specs=[SMEM] + [HBM] * 4,
        out_specs=[HBM] * 4,
        scratch=[
            pltpu.VMEM((4, QUARTER, TILE), HALF),
            pltpu.VMEM((4, EIGHTH, TILE), HALF),
            pltpu.SemaphoreType.DMA((4,)),
            pltpu.SemaphoreType.DMA((4,)),
        ],
        flops=4 * QUARTER * TILE,
    )


def finish_kernel(*refs):
    terms, out, (taken, held, in_sems, out_sem) = refs[:8], refs[8], refs[9:]
    loads = [pltpu.make_async_copy(terms[i], taken.at[i], in_sems.at[i]) for i in range(8)]
    for load in loads:
        load.start()
    for side in range(2):
        for load in loads[4 * side:4 * side + 4]:
            load.wait()
        total = taken[4 * side].astype(F32)
        for i in range(1, 4):
            total += taken[4 * side + i].astype(F32)
        held[side * EIGHTH:(side + 1) * EIGHTH, :] = total.astype(HALF)
    store = pltpu.make_async_copy(held, out, out_sem)
    store.start()
    store.wait()


def finish(first, second):
    return call(
        finish_kernel,
        "finish",
        in_hbm([*first, *second]),
        pltpu.HBM((2 * EIGHTH, TILE), HALF),
        in_specs=[HBM] * 8,
        out_specs=HBM,
        scratch=[
            pltpu.VMEM((8, EIGHTH, TILE), HALF),
            pltpu.VMEM((2 * EIGHTH, TILE), HALF),
            pltpu.SemaphoreType.DMA((8,)),
            pltpu.SemaphoreType.DMA,
        ],
        flops=8 * EIGHTH * TILE,
    )


def tile_of(total, tile):
    ranks = 16 * EIGHTH
    return total[:, tile % 2, tile // 2].reshape(ranks, TILE)


def right_kernel(rows_hbm, weights_hbm, total_hbm, raw_ref, squares_ref, weights_ref, total_ref, rows_ref, sems):
    count = raw_ref.shape[0]
    loads = [pltpu.make_async_copy(rows_hbm, rows_ref, sems.at[4])]
    for tile in range(4):
        here = (slice(None), tile % 2, tile // 2)
        loads.append(pltpu.make_async_copy(total_hbm.at[here], total_ref.at[here], sems.at[tile]))
    loads.append(pltpu.make_async_copy(weights_hbm, weights_ref, sems.at[5]))
    for load in loads:
        load.start()
    loads[0].wait()
    squares = 0.0
    for tile in range(4):
        loads[1 + tile].wait()
        both = jnp.dot(rows_ref[...], tile_of(total_ref, tile), preferred_element_type=F32)
        raw = both[:count] + both[count:]
        raw_ref[:, tile * TILE:(tile + 1) * TILE] = raw
        squares += jnp.sum(raw * raw, axis=1, keepdims=True)
    squares_ref[...] = jnp.broadcast_to(squares, squares_ref.shape)
    loads[5].wait()


def right_rows(rows, weights, total):
    count = rows.shape[0] // 2
    return call(
        right_kernel,
        "right_rows",
        in_hbm([rows, weights, total]),
        [
            jax.ShapeDtypeStruct((count, 4 * TILE), F32),
            jax.ShapeDtypeStruct((count, 128), F32),
            pltpu.VMEM(weights.shape, weights.dtype),
            pltpu.VMEM(total.shape, total.dtype),
        ],
        in_specs=[HBM] * 3,
        scratch=[pltpu.VMEM(rows.shape, rows.dtype), pltpu.SemaphoreType.DMA((6,))],
        flops=2 * rows.size * 4 * TILE,
    )


def feedback_kernel(at_ref, weights_ref, total_ref, *refs):
    blocks, out, (held, sems) = refs[:8], refs[8], refs[9:]
    rows = blocks[0].shape[0]
    ranks = 16 * EIGHTH
    copies = []
    for tile in range(4):
        for start in range(0, TILE, CHUNK):
            size = min(CHUNK, TILE - start)
            total = total_ref[:, tile % 2, tile // 2, :, start:start + size].reshape(ranks, size)
            here = (tile % 2) * TILE + start
            to = slice(tile * TILE + start, tile * TILE + start + size)
            for turn in range(4):
                part = jnp.dot(
                    weights_ref[turn * rows:(turn + 1) * rows, :], total, preferred_element_type=F32
                )
                at = lax.rem(at_ref[0] - turn + 4, 4) * rows
                held[pl.ds(pl.multiple_of(at, rows), rows), to] = (
                    blocks[4 * (tile // 2) + turn][:, here:here + size].astype(F32) - part
                ).astype(HALF)
            copies.append(pltpu.make_async_copy(held.at[:, to], out.at[:, to], sems.at[len(copies)]))
            copies[-1].start()
    for copy in copies:
        copy.wait()


def apply_feedback(weights, total, blocks, place):
    rows = blocks[0].shape[0]
    ranks = weights.shape[1]
    shape = (4 * rows, 4 * TILE)
    return call(
        feedback_kernel,
        "feedback",
        [jnp.full((1,), place, jnp.int32), weights, total, *blocks],
        pltpu.HBM(shape, HALF),
        in_specs=[SMEM] + [VMEM] * 10,
        out_specs=HBM,
        scratch=[pltpu.VMEM(shape, HALF), pltpu.SemaphoreType.DMA((4 * -(-TILE // CHUNK),))],
        flops=32 * rows * TILE * ranks,
    )


def after(value, *others):
    return lax.optimization_barrier((value,) + others)[0]


def per_device(momentum, gradient, right_factor):
    ranks_dev, width = right_factor.shape
    half_width = width // 2
    at_y, at_x, core, place = (lax.axis_index(name) for name in ("y", "x", "core", "col"))
    row = ("y", "x", "core")
    right_all = lax.all_gather(right_factor, row, axis=0, tiled=True)
    ranks = right_all.shape[0]
    blocks = [[None] * 4, [None] * 4]
    last = place
    for half in range(2):
        for turn in (2, 1, 3, 0):
            block = lax.rem(place + turn, 4) * 2 + half
            start = after(block, last) * half_width
            pair = [lax.dynamic_slice_in_dim(v, start, half_width, 1).astype(F32) for v in (momentum, gradient)]
            last = (pair[0] + pair[1]).astype(HALF)
            blocks[half][turn] = ring(last, "col", turn) if turn else last
    partial = project(blocks[0], right_all, 0)
    parts = project(blocks[1], right_all, 1, partial)
    terms = [parts[0]] + [ring(parts[turn], "col", -turn) for turn in (2, 1, 3)]
    mine, turned = settle(terms)
    factors = [turned] + [ring(turned, "col", turn) for turn in (1, 2, 3)]

    places = (at_x, at_y)
    sent = [cross(factors, blocks[half], 1 - core, half, places[half]) for half in range(2)]
    got = [swap_cores(value) for value in sent]
    first = list(cross(factors, blocks[0], after(core, sent[1]), 0, at_x, got[0]))
    second = list(cross(factors, blocks[1], after(core, first[0]), 1, at_y, got[1]))
    for turn in (2, 1, 3):
        first[turn] = ring(after(first[turn], second[0]), "x", turn)
        second[turn] = ring(second[turn], "y", turn)

    gram_part = gram_of([after(factors[0], first[2])] + factors[1:])
    rows = ranks // ranks_dev
    gram_pieces = lax.all_to_all(gram_part, row, split_axis=0, concat_axis=0, tiled=True)
    copies = spread(gram_pieces.reshape(rows, ranks_dev, ranks))

    first = list(fold(first, at_y))
    for turn in (2, 1, 3):
        first[turn] = ring(first[turn], "y", turn)
    second = list(fold(second, at_x))
    gram = lax.all_to_all(copies.reshape(ranks, ranks), row, split_axis=0, concat_axis=0, tiled=True)
    for turn in (2, 1, 3):
        second[turn] = ring(second[turn], "x", turn)
    done = finish([after(first[0], copies)] + first[1:], second)
    total = lax.all_gather(done, row, axis=0, tiled=True)
    total = total.reshape(16, 2, 2, EIGHTH, TILE)

    at_row = (at_y * 4 + at_x) * 2 + core
    own, weights, left_factor = factorize(after(gram, done), factors, at_row, ranks_dev)

    right_raw, squares, weights, total = right_rows(own, weights, total)
    squares = squares + sum(ring(squares, "col", turn) for turn in (1, 2, 3))
    new_momentum = apply_feedback(weights, total, blocks[0] + blocks[1], place)
    new_right = right_raw / jnp.sqrt(squares[:, :1] + 1e-06)
    return (new_momentum, left_factor, new_right)


def solution(mesh):
    fine = Mesh(mesh.devices.reshape(4, 4, 2, 4), ("y", "x", "core", "col"))
    every = ("y", "x", "core", "col")
    row = ("y", "x", "core")
    in_specs = (P(every, None), P(every, None), P(row, "col"))
    out_specs = (P(row, "col"), P(every, None), P(row, "col"))
    return jax.shard_map(
        per_device, mesh=fine, in_specs=in_specs, out_specs=out_specs, check_vma=False
    )
```

time: 580 us -> 250 us (0.43); the launches traced: 573 us -> 249 us
  waiting for transfers between devices: 262 us -> 80.9 us
  other arithmetic: 139 us -> 19.9 us
  blocking collectives: 90.4 us -> 0 us
  Pallas kernels: 0 us -> 65.3 us
  starting transfers between devices: 0.62 us -> 60.3 us
  matrix products: 42.3 us -> 0 us
  local copies, waits for them, and re-layouts: 22.1 us -> 8.54 us
    psum x3 -> x0, waiting for transfers between devices: 261 us -> none  [the longest x1 115 us: per_device(): lax.psum(partial_right.astype(jnp.bfloat16), 'row').astype(jnp.float32)]
    another operation x17 -> x4, other arithmetic: 123 us -> 0.3 us  [cross(): jnp.stack([tile, at]).astype(jnp.int32)]
    all_to_all x1 -> x0, blocking collectives: 81.7 us -> none  [per_device(): lax.all_to_all(blend, 'col', split_axis=1, concat_axis=0, tiled=True)]
    pallas_call x0 -> x15, Pallas kernels: none -> 65.3 us  [the longest x14 40.7 us: call(): pl.pallas_call(kernel, in_specs=in_specs or [VMEM] * len(operands), out_s...]
    ppermute x0 -> x29, waiting for transfers between devices: none -> 54 us  [the longest x27 54 us: ring(): lax.ppermute(value, axis, [(i, (i + shift) % size) for i in range(size)])]
    ppermute x0 -> x29, starting transfers between devices: none -> 47 us  [the longest x27 44.6 us: ring(): lax.ppermute(value, axis, [(i, (i + shift) % size) for i in range(size)])]
    dot_general x5 -> x0, matrix products: 28.3 us -> none  [the longest x1 9.63 us: per_device(): jnp.dot(orth_half, right_rounded, preferred_element_type=jnp.float32)]
    another operation x17 -> x0, local copies, waits for them, and re-layouts: 15.2 us -> none
  transfers between devices with their start and end apart: 4 -> 33, of which waited for: 3 -> 16; matrix products, arithmetic and copies ran while one was open for 3% -> 8% of each run, Pallas kernels for 0% -> 19%
where the time goes in v2:
time: 250 us; the launch traced here: 249 us
  waiting for transfers between devices  80.9 us (32%)
  Pallas kernels  65.3 us (26%)
  starting transfers between devices  60.3 us (24%)
  other arithmetic  19.9 us (8%)
  between operations  14.3 us (6%)
  local copies, waits for them, and re-layouts  8.54 us (3%)
    ppermute x27, waiting for transfers between devices, ring(): lax.ppermute(value, axis, [(i, (i + shift) % size) for i in range(size)])  54 us
    ppermute x27, starting transfers between devices, ring(): lax.ppermute(value, axis, [(i, (i + shift) % size) for i in range(size)])  44.6 us
    pallas_call x14, Pallas kernels, call(): pl.pallas_call(kernel, in_specs=in_specs or [VMEM] * len(operands), out_s...  40.7 us
    pallas_call x1, Pallas kernels, factorize(): pl.pallas_call(factor_kernel, out_shape=[pltpu.HBM(*out) for out in outs]...  24.6 us
    convert_element_type x8, other arithmetic, per_device(): last = (pair[0] + pair[1]).astype(HALF)  18.6 us
    all_to_all x1, waiting for transfers between devices, per_device(): lax.all_to_all(copies.reshape(ranks, ranks), row, split_axis=0, concat_ax...  13.7 us
    unnamed x22, local copies, waits for them, and re-layouts  8.54 us
    all_gather x1, waiting for transfers between devices, per_device(): right_all = lax.all_gather(right_factor, row, axis=0, tiled=True)  7.65 us
  transfers between devices with their start and end apart: 33, of which 16 were waited for; matrix products, arithmetic and copies ran while one was open for 8% of the time, Pallas kernels for 19%

profile of v2, /device:TPU:1, one launch (start us, length us, event | category | flops | bytes accessed | tf_op | source)
XLA Modules:
  0.0 249.2 jit_solution(13088831619745709415)
XLA Ops:
  7.9 2.5 %add_convert_fusion.7 = bf16[128,3328]{1,0:T(8,128)(2,1)} fusion(bf16[128,26624]{1,0:T(8,128)(2,1)} %param.4, s32[]{:T(128)S(6)} %select_n.32, bf16[128,26624]{1,0:T(8,128)(2,1)} %param.3), kind=kLoop, calls=%fused_computation.7 | loop fusion | flops 1703936 | bytes 2555908 | tf_op jit(solution)/shard_map/convert_element_type | solution.py:514
  10.4 4.4 %collective-permute-start.4 = (bf16[128,3328]{1,0:T(8,128)(2,1)}, bf16[128,3328]{1,0:T(8,128)(2,1)S(1)}, u32[]{:S(2)}, u32[]{:S(2)}) collective-permute-start(bf16[128,3328]{1,0:T(8,128)(2,1)} %add_convert_fusion.7), channel_id=1, source_target_pairs={{0,2},{1,3},{2,0},{3,1},{4,6},{5,7},{6,4},{7,5},{8,10},{9,11},{10,... | collective-permute-start | bytes 2555912 | tf_op jit(solution)/shard_map/ppermute | solution.py:166
  14.9 2.6 %add_convert_fusion.6 = bf16[128,3328]{1,0:T(8,128)(2,1)} fusion(bf16[128,26624]{1,0:T(8,128)(2,1)} %param.4, s32[]{:T(128)S(6)} %select_n.33, bf16[128,26624]{1,0:T(8,128)(2,1)} %param.3), kind=kLoop, calls=%fused_computation.6 | loop fusion | flops 1703936 | bytes 2555908 | tf_op jit(solution)/shard_map/convert_element_type | solution.py:514
  18.2 2.5 %add_convert_fusion.5 = bf16[128,3328]{1,0:T(8,128)(2,1)} fusion(bf16[128,26624]{1,0:T(8,128)(2,1)} %param.4, s32[]{:T(128)S(6)} %select_n.34, bf16[128,26624]{1,0:T(8,128)(2,1)} %param.3), kind=kLoop, calls=%fused_computation.5 | loop fusion | flops 1703936 | bytes 2555908 | tf_op jit(solution)/shard_map/convert_element_type | solution.py:514
  20.7 1.9 collective-permute-start.5
  22.6 1.7 add_convert_fusion.4.refs_0_.refs_4_
  24.3 2.5 %add_convert_fusion.3 = bf16[128,3328]{1,0:T(8,128)(2,1)} fusion(bf16[128,26624]{1,0:T(8,128)(2,1)} %param.4, s32[]{:T(128)S(6)} %select_n.36, bf16[128,26624]{1,0:T(8,128)(2,1)} %param.3), kind=kLoop, calls=%fused_computation.3 | loop fusion | flops 1703936 | bytes 2555908 | tf_op jit(solution)/shard_map/convert_element_type | solution.py:514
  26.8 2.5 %add_convert_fusion.2 = bf16[128,3328]{1,0:T(8,128)(2,1)} fusion(bf16[128,26624]{1,0:T(8,128)(2,1)} %param.4, s32[]{:T(128)S(6)} %select_n.37, bf16[128,26624]{1,0:T(8,128)(2,1)} %param.3), kind=kLoop, calls=%fused_computation.2 | loop fusion | flops 1703936 | bytes 2555908 | tf_op jit(solution)/shard_map/convert_element_type | solution.py:514
  29.3 2.5 %add_convert_fusion.1 = bf16[128,3328]{1,0:T(8,128)(2,1)} fusion(bf16[128,26624]{1,0:T(8,128)(2,1)} %param.4, s32[]{:T(128)S(6)} %select_n.38, bf16[128,26624]{1,0:T(8,128)(2,1)} %param.3), kind=kLoop, calls=%fused_computation.1 | loop fusion | flops 1703936 | bytes 2555908 | tf_op jit(solution)/shard_map/convert_element_type | solution.py:514
  31.9 2.7 %collective-permute-start.2 = (bf16[128,3328]{1,0:T(8,128)(2,1)}, bf16[128,3328]{1,0:T(8,128)(2,1)}, u32[]{:S(2)}, u32[]{:S(2)}) collective-permute-start(bf16[128,3328]{1,0:T(8,128)(2,1)} %add_convert_fusion.1), channel_id=1, source_target_pairs={{0,3},{1,0},{2,1},{3,2},{4,7},{5,4},{6,5},{7,6},{8,11},{9,8},{10,9... | collective-permute-start | bytes 2555912 | tf_op jit(solution)/shard_map/ppermute | solution.py:166
  34.5 18.0 %collective-permute-done.5.refs_3_.refs_7_ = bf16[128,3328]{1,0:T(8,128)(2,1)S(1)} collective-permute-done((bf16[128,3328]{1,0:T(8,128)(2,1)}, bf16[128,3328]{1,0:T(8,128)(2,1)S(1)}, u32[]{:S(2)}, u32[]{:S(2)}) %collective-permute-start.5) | collective-permute-done | bytes 852000 | tf_op jit(solution)/shard_map/ppermute | solution.py:166
  54.4 1.7 add_convert_fusion.refs_0_.refs_4_
  56.1 7.7 %all-gather.3.cloned.1.call-done.refs_4_ = bf16[512,6656]{1,0:T(8,128)(2,1)} async-done(((bf16[16,6656]{1,0:T(8,128)(2,1)}), bf16[512,6656]{1,0:T(8,128)(2,1)}) %all-gather.3.cloned.1.call-update) | async-done | bytes 6815760 | tf_op jit(solution)/shard_map/all_gather | solution.py:505
  63.8 2.9 %copy-done = bf16[512,6656]{1,0:T(8,128)(2,1)S(1)} copy-done((bf16[512,6656]{1,0:T(8,128)(2,1)S(1)}, bf16[512,6656]{1,0:T(8,128)(2,1)}, u32[]{:S(2)}) %copy-start) | copy-done | bytes 6815768
  67.9 2.1 project.2.refs_5_
  70.0 1.4 collective-permute-done.2.refs_3_.refs_7_
  71.8 16.9 %collective-permute-done.1.refs_2_.refs_6_ = bf16[128,3328]{1,0:T(8,128)(2,1)} collective-permute-done((bf16[128,3328]{1,0:T(8,128)(2,1)}, bf16[128,3328]{1,0:T(8,128)(2,1)}, u32[]{:S(2)}, u32[]{:S(2)}) %collective-permute-start.1) | collective-permute-done | bytes 852000 | tf_op jit(solution)/shard_map/ppermute | solution.py:166
  88.7 3.8 %project.3 = (bf16[128,512]{1,0:T(8,128)(2,1)S(1)}, bf16[128,512]{1,0:T(8,128)(2,1)S(1)}, bf16[128,512]{1,0:T(8,128)(2,1)S(1)}, bf16[128,512]{1,0:T(8,128)(2,1)S(1)}) custom-call(bf16[128,3328]{1,0:T(8,128)(2,1)S(1)} %add_convert_fusion.refs_0_.refs_4_, bf16[128,3328]{1,0:T(8,128)(2,1)} %collective-permute-done.refs_1_.refs_5_, ...), custom_call_target="tpu_custom_call" | custom-call | flops 1744830464 | bytes 11796480 | tf_op jit(solution)/shard_map/project/pallas_call | solution.py:180
  92.4 2.7 %collective-permute-start.6 = (bf16[128,512]{1,0:T(8,128)(2,1)S(1)}, bf16[128,512]{1,0:T(8,128)(2,1)S(1)}, u32[]{:S(2)}, u32[]{:S(2)}) collective-permute-start(bf16[128,512]{1,0:T(8,128)(2,1)S(1)} %get-tuple-element.56), channel_id=1, source_target_pairs={{0,2},{1,3},{2,0},{3,1},{4,6},{5,7},{6,4},{7,5},{8,10},{9,11},{10,... | collective-permute-start | bytes 393224 | tf_op jit(solution)/shard_map/ppermute | solution.py:166
  97.8 2.9 %collective-permute-done.7.refs_2_ = bf16[128,512]{1,0:T(8,128)(2,1)S(1)} collective-permute-done((bf16[128,512]{1,0:T(8,128)(2,1)S(1)}, bf16[128,512]{1,0:T(8,128)(2,1)S(1)}, u32[]{:S(2)}, u32[]{:S(2)}) %collective-permute-start.7) | collective-permute-done | bytes 131104 | tf_op jit(solution)/shard_map/ppermute | solution.py:166
  102.0 3.0 %collective-permute-start.11 = (bf16[512,128]{1,0:T(8,128)(2,1)S(1)}, bf16[512,128]{1,0:T(8,128)(2,1)}, u32[]{:S(2)}, u32[]{:S(2)}) collective-permute-start(bf16[512,128]{1,0:T(8,128)(2,1)S(1)} %get-tuple-element.66.refs_0_), channel_id=1, source_target_pairs={{0,3},{1,0},{2,1},{3,2},{4,7},{5,4},{6,5},{7,6},{8,11},{9,8},{10,9... | collective-permute-start | bytes 393224 | tf_op jit(solution)/shard_map/ppermute | solution.py:166
  105.7 4.7 %collective-permute-done.11.refs_3_ = bf16[512,128]{1,0:T(8,128)(2,1)} collective-permute-done((bf16[512,128]{1,0:T(8,128)(2,1)S(1)}, bf16[512,128]{1,0:T(8,128)(2,1)}, u32[]{:S(2)}, u32[]{:S(2)}) %collective-permute-start.11) | collective-permute-done | bytes 131104 | tf_op jit(solution)/shard_map/ppermute | solution.py:166
  110.5 2.5 %collective-permute-done.9.refs_1_ = bf16[512,128]{1,0:T(8,128)(2,1)} collective-permute-done((bf16[512,128]{1,0:T(8,128)(2,1)S(1)}, bf16[512,128]{1,0:T(8,128)(2,1)}, u32[]{:S(2)}, u32[]{:S(2)}) %collective-permute-start.9) | collective-permute-done | bytes 131104 | tf_op jit(solution)/shard_map/ppermute | solution.py:166
  114.2 3.0 %cross.3 = bf16[4,128,1664]{2,1,0:T(8,128)(2,1)} custom-call(s32[2]{0:T(128)S(1)} %pad_add_fusion.3.at_ref, bf16[512,128]{1,0:T(8,128)(2,1)S(1)} %get-tuple-element.66.refs_0_, bf16[512,128]{1,0:T(8,128)(2,1)} %collective-permute-done.9.refs_1_, bf16[512,128]{1,0:T(8,128)(2,1)} %collective-permute-done.10.refs_2_, ...), custom_call_target="tpu_custom_call" | custom-call | flops 872415232 | bytes 5636104 | tf_op jit(solution)/shard_map/cross/pallas_call | solution.py:180
  117.2 2.1 collective-permute-start.12
  119.4 3.9 %cross.2 = bf16[4,128,1664]{2,1,0:T(8,128)(2,1)} custom-call(s32[2]{0:T(128)S(1)} %pad_add_fusion.2.at_ref, bf16[512,128]{1,0:T(8,128)(2,1)S(1)} %get-tuple-element.66.refs_0_, bf16[512,128]{1,0:T(8,128)(2,1)} %collective-permute-done.9.refs_1_, bf16[512,128]{1,0:T(8,128)(2,1)} %collective-permute-done.10.refs_2_, ...), custom_call_target="tpu_custom_call" | custom-call | flops 872415232 | bytes 5636104 | tf_op jit(solution)/shard_map/cross/pallas_call | solution.py:180
  123.8 3.6 %cross_add.2 = (bf16[128,1664]{1,0:T(8,128)(2,1)}, bf16[128,1664]{1,0:T(8,128)(2,1)}, bf16[128,1664]{1,0:T(8,128)(2,1)}, bf16[128,1664]{1,0:T(8,128)(2,1)}) custom-call(s32[2]{0:T(128)S(1)} %pad_add_fusion.at_ref, bf16[512,128]{1,0:T(8,128)(2,1)S(1)} %get-tuple-element.66.refs_0_, bf16[512,128]{1,0:T(8,128)(2,1)} %collective-permute-done.9.refs_1_, ...), custom_call_target="tpu_custom_call" | custom-call | flops 872415232 | bytes 7340040 | tf_op jit(solution)/shard_map/cross_add/pallas_call | solution.py:180
  127.4 3.8 %cross_add.3 = (bf16[128,1664]{1,0:T(8,128)(2,1)}, bf16[128,1664]{1,0:T(8,128)(2,1)}, bf16[128,1664]{1,0:T(8,128)(2,1)}, bf16[128,1664]{1,0:T(8,128)(2,1)}) custom-call(s32[2]{0:T(128)S(1)} %pad_add_fusion.1.at_ref, bf16[512,128]{1,0:T(8,128)(2,1)S(1)} %get-tuple-element.66.refs_0_, bf16[512,128]{1,0:T(8,128)(2,1)} %collective-permute-done.9.refs_1_, ...), custom_call_target="tpu_custom_call" | custom-call | flops 872415232 | bytes 7340040 | tf_op jit(solution)/shard_map/cross_add/pallas_call | solution.py:180
  131.3 2.8 %collective-permute-start.14 = (bf16[128,1664]{1,0:T(8,128)(2,1)S(1)}, bf16[128,1664]{1,0:T(8,128)(2,1)S(1)}, u32[]{:S(2)}, u32[]{:S(2)}) collective-permute-start(bf16[128,1664]{1,0:T(8,128)(2,1)S(1)} %copy-done.10), channel_id=1, source_target_pairs={{0,16},{8,24},{16,0},{24,8},{1,17},{9,25},{17,1},{25,9},{2,18},{10... | collective-permute-start | bytes 1277960 | tf_op jit(solution)/shard_map/ppermute | solution.py:166
  134.4 2.4 collective-permute-start.16
  138.1 2.6 %collective-permute-start.21 = (bf16[128,1664]{1,0:T(8,128)(2,1)}, bf16[128,1664]{1,0:T(8,128)(2,1)}, u32[]{:S(2)}, u32[]{:S(2)}) collective-permute-start(bf16[128,1664]{1,0:T(8,128)(2,1)} %get-tuple-element.77), channel_id=1, source_target_pairs={{0,64},{32,96},{64,0},{96,32},{1,65},{33,97},{65,1},{97,33},{2,66}... | collective-permute-start | bytes 1277960 | tf_op jit(solution)/shard_map/ppermute | solution.py:166
  140.7 3.2 %collective-permute-done.14.refs_2_ = bf16[128,1664]{1,0:T(8,128)(2,1)S(1)} collective-permute-done((bf16[128,1664]{1,0:T(8,128)(2,1)S(1)}, bf16[128,1664]{1,0:T(8,128)(2,1)S(1)}, u32[]{:S(2)}, u32[]{:S(2)}) %collective-permute-start.14) | collective-permute-done | bytes 426016 | tf_op jit(solution)/shard_map/ppermute | solution.py:166
  144.7 2.9 %collective-permute-start.22 = (bf16[128,1664]{1,0:T(8,128)(2,1)}, bf16[128,1664]{1,0:T(8,128)(2,1)}, u32[]{:S(2)}, u32[]{:S(2)}) collective-permute-start(bf16[128,1664]{1,0:T(8,128)(2,1)} %get-tuple-element.78), channel_id=1, source_target_pairs={{0,96},{32,0},{64,32},{96,64},{1,97},{33,1},{65,33},{97,65},{2,98}... | collective-permute-start | bytes 1277960 | tf_op jit(solution)/shard_map/ppermute | solution.py:166
  147.5 1.7 gram.1
  150.0 7.0 %all-to-all-start = ((bf16[32,16,512]{2,1,0:T(8,128)(2,1)}), bf16[32,16,512]{2,1,0:T(8,128)(2,1)}, u32[]{:S(2)}, u32[]{:S(2)}) async-start(bf16[32,16,512]{2,1,0:T(8,128)(2,1)} %bitcast.10), calls=%async_computation | async-start | bytes 1048576 | tf_op jit(solution)/shard_map/all_to_all | solution.py:533
  157.1 2.3 fold.2
  159.4 1.5 collective-permute-start.17
  160.9 2.4 collective-permute-start.18
  164.5 2.3 fold.3
  168.1 2.4 collective-permute-start.24
  175.7 2.0 finish.1
  177.7 6.3 %all-to-all-start.1 = ((bf16[32,16,512]{2,1,0:T(8,128)(2,1)}), bf16[32,16,512]{2,1,0:T(8,128)(2,1)}, u32[]{:S(2)}, u32[]{:S(2)}) async-start(bf16[32,16,512]{2,1,0:T(8,128)(2,1)} %copy-done.8), calls=%async_computation.1 | async-start | bytes 1048576 | tf_op jit(solution)/shard_map/all_to_all | solution.py:540
  184.0 13.7 %all-to-all-done.1 = bf16[32,16,512]{2,1,0:T(8,128)(2,1)} async-done(((bf16[32,16,512]{2,1,0:T(8,128)(2,1)}), bf16[32,16,512]{2,1,0:T(8,128)(2,1)}, u32[]{:S(2)}, u32[]{:S(2)}) %all-to-all-start.1) | async-done | bytes 524320 | tf_op jit(solution)/shard_map/all_to_all | solution.py:540
  197.6 24.6 %factorize.1 = (bf16[32,512]{1,0:T(8,128)(2,1)}, bf16[512,512]{1,0:T(8,128)(2,1)}, f32[128,512]{1,0:T(8,128)}) custom-call(s32[1]{0:T(128)} %bitcast.1.at_ref, bf16[512,512]{1,0:T(8,128)(2,1)} %bitcast.8.g_ref, bf16[512,128]{1,0:T(8,128)(2,1)S(1)} %get-tuple-element.66.refs_0_, bf16[512,128]{1,0:T(8,128)(2,1)} %collective-permute-done.9.refs_1_, ...), custom_call_target="tpu_custom_call" | custom-call | flops 20000000000 | bytes 4194304 | tf_op jit(solution)/shard_map/factorize/pallas_call | solution.py:138
  222.2 5.0 %all-gather.5.cloned.1.call-done = bf16[2048,1664]{1,0:T(8,128)(2,1)} async-done(((bf16[64,1664]{1,0:T(8,128)(2,1)}), bf16[2048,1664]{1,0:T(8,128)(2,1)}) %all-gather.5.cloned.1.call-update) | async-done | bytes 6815760 | tf_op jit(solution)/shard_map/all_gather | solution.py:544
  227.2 3.6 %right_rows.1 = (f32[16,6656]{1,0:T(8,128)S(1)}, f32[16,128]{1,0:T(8,128)S(1)}, bf16[512,512]{1,0:T(8,128)(2,1)S(1)}, bf16[16,2,2,32,1664]{4,3,2,1,0:T(8,128)(2,1)S(1)}) custom-call(bf16[32,512]{1,0:T(8,128)(2,1)} %get-tuple-element.84.rows_hbm, bf16[512,512]{1,0:T(8,128)(2,1)} %get-tuple-element.85.weights_hbm, bf16[16,2,2,32,1664]{4,3,2,1,0:T(8,128)(2,1)} %bitcast.11), custom_call_target="tpu_custom_call" | custom-call | flops 218103808 | bytes 15147008 | tf_op jit(solution)/shard_map/right_rows/pallas_call | solution.py:180
  230.8 2.7 %collective-permute-start.28 = (f32[16,128]{1,0:T(8,128)S(1)}, f32[16,128]{1,0:T(8,128)S(1)}, u32[]{:S(2)}, u32[]{:S(2)}) collective-permute-start(f32[16,128]{1,0:T(8,128)S(1)} %get-tuple-element.90), channel_id=1, source_target_pairs={{0,3},{1,0},{2,1},{3,2},{4,7},{5,4},{6,5},{7,6},{8,11},{9,8},{10,9... | collective-permute-start | bytes 24584 | tf_op jit(solution)/shard_map/ppermute | solution.py:166
  234.8 6.6 %feedback.1 = bf16[512,6656]{1,0:T(8,128)(2,1)} custom-call(s32[1]{0:T(128)} %bitcast.at_ref, bf16[512,512]{1,0:T(8,128)(2,1)S(1)} %get-tuple-element.86.weights_ref, bf16[16,2,2,32,1664]{4,3,2,1,0:T(8,128)(2,1)S(1)} %get-tuple-element.87.total_ref, bf16[128,3328]{1,0:T(8,128)(2,1)S(1)} %add_convert_fusion.4.refs_0_.refs_4_, ...), custom_call_target="tpu_custom_call" | custom-call | flops 3489660928 | bytes 20971524 | tf_op jit(solution)/shard_map/feedback/pallas_call | solution.py:180
  (71 shorter events, 24.3 us)
Async XLA Ops:
  7.2 56.6 %all-gather.3.cloned.1.call-start = ((), (), s32[]{:S(2)}) async-start(), calls=%async_computation.2 | async-start | bytes 7028736 | tf_op jit(solution)/shard_map/all_gather | solution.py:505
  10.4 45.7 %collective-permute-start.4 = (bf16[128,3328]{1,0:T(8,128)(2,1)}, bf16[128,3328]{1,0:T(8,128)(2,1)S(1)}, u32[]{:S(2)}, u32[]{:S(2)}) collective-permute-start(bf16[128,3328]{1,0:T(8,128)(2,1)} %add_convert_fusion.7), channel_id=1, source_target_pairs={{0,2},{1,3},{2,0},{3,1},{4,6},{5,7},{6,4},{7,5},{8,10},{9,11},{10,... | collective-permute-start | bytes 2555912 | tf_op jit(solution)/shard_map/ppermute | solution.py:166
  17.4 38.7 %collective-permute-start.3 = (bf16[128,3328]{1,0:T(8,128)(2,1)}, bf16[128,3328]{1,0:T(8,128)(2,1)S(1)}, u32[]{:S(2)}, u32[]{:S(2)}) collective-permute-start(bf16[128,3328]{1,0:T(8,128)(2,1)} %add_convert_fusion.6), channel_id=1, source_target_pairs={{0,1},{1,2},{2,3},{3,0},{4,5},{5,6},{6,7},{7,4},{8,9},{9,10},{10,1... | collective-permute-start | bytes 2555912 | tf_op jit(solution)/shard_map/ppermute | solution.py:166
  20.7 31.9 %collective-permute-start.5 = (bf16[128,3328]{1,0:T(8,128)(2,1)}, bf16[128,3328]{1,0:T(8,128)(2,1)S(1)}, u32[]{:S(2)}, u32[]{:S(2)}) collective-permute-start(bf16[128,3328]{1,0:T(8,128)(2,1)} %add_convert_fusion.5), channel_id=1, source_target_pairs={{0,3},{1,0},{2,1},{3,2},{4,7},{5,4},{6,5},{7,6},{8,11},{9,8},{10,9... | collective-permute-start | bytes 2555912 | tf_op jit(solution)/shard_map/ppermute | solution.py:166
  29.3 42.4 %collective-permute-start = (bf16[128,3328]{1,0:T(8,128)(2,1)}, bf16[128,3328]{1,0:T(8,128)(2,1)}, u32[]{:S(2)}, u32[]{:S(2)}) collective-permute-start(bf16[128,3328]{1,0:T(8,128)(2,1)} %add_convert_fusion.2), channel_id=1, source_target_pairs={{0,1},{1,2},{2,3},{3,0},{4,5},{5,6},{6,7},{7,4},{8,9},{9,10},{10,1... | collective-permute-start | bytes 2555912 | tf_op jit(solution)/shard_map/ppermute | solution.py:166
  31.9 39.4 %collective-permute-start.2 = (bf16[128,3328]{1,0:T(8,128)(2,1)}, bf16[128,3328]{1,0:T(8,128)(2,1)}, u32[]{:S(2)}, u32[]{:S(2)}) collective-permute-start(bf16[128,3328]{1,0:T(8,128)(2,1)} %add_convert_fusion.1), channel_id=1, source_target_pairs={{0,3},{1,0},{2,1},{3,2},{4,7},{5,4},{6,5},{7,6},{8,11},{9,8},{10,9... | collective-permute-start | bytes 2555912 | tf_op jit(solution)/shard_map/ppermute | solution.py:166
  52.6 0.9 copy-start.2
  53.5 35.2 %collective-permute-start.1 = (bf16[128,3328]{1,0:T(8,128)(2,1)}, bf16[128,3328]{1,0:T(8,128)(2,1)}, u32[]{:S(2)}, u32[]{:S(2)}) collective-permute-start(bf16[128,3328]{1,0:T(8,128)(2,1)} %add_convert_fusion.3), channel_id=1, source_target_pairs={{0,2},{1,3},{2,0},{3,1},{4,6},{5,7},{6,4},{7,5},{8,10},{9,11},{10,... | collective-permute-start | bytes 2555912 | tf_op jit(solution)/shard_map/ppermute | solution.py:166
  63.8 2.9 %copy-start = (bf16[512,6656]{1,0:T(8,128)(2,1)S(1)}, bf16[512,6656]{1,0:T(8,128)(2,1)}, u32[]{:S(2)}) copy-start(bf16[512,6656]{1,0:T(8,128)(2,1)} %all-gather.3.cloned.1.call-done.refs_4_) | copy-start | bytes 20447236
  66.7 1.2 copy-start.3
  67.9 20.8 %copy-start.1 = (bf16[512,6656]{1,0:T(8,128)(2,1)S(1)}, bf16[512,6656]{1,0:T(8,128)(2,1)}, u32[]{:S(2)}) copy-start(bf16[512,6656]{1,0:T(8,128)(2,1)} %all-gather.3.cloned.1.call-done.refs_4_) | copy-start | bytes 20447236
  92.4 5.4 %collective-permute-start.6 = (bf16[128,512]{1,0:T(8,128)(2,1)S(1)}, bf16[128,512]{1,0:T(8,128)(2,1)S(1)}, u32[]{:S(2)}, u32[]{:S(2)}) collective-permute-start(bf16[128,512]{1,0:T(8,128)(2,1)S(1)} %get-tuple-element.56), channel_id=1, source_target_pairs={{0,2},{1,3},{2,0},{3,1},{4,6},{5,7},{6,4},{7,5},{8,10},{9,11},{10,... | collective-permute-start | bytes 393224 | tf_op jit(solution)/shard_map/ppermute | solution.py:166
  95.1 5.6 %collective-permute-start.7 = (bf16[128,512]{1,0:T(8,128)(2,1)S(1)}, bf16[128,512]{1,0:T(8,128)(2,1)S(1)}, u32[]{:S(2)}, u32[]{:S(2)}) collective-permute-start(bf16[128,512]{1,0:T(8,128)(2,1)S(1)} %get-tuple-element.57), channel_id=1, source_target_pairs={{0,3},{1,0},{2,1},{3,2},{4,7},{5,4},{6,5},{7,6},{8,11},{9,8},{10,9... | collective-permute-start | bytes 393224 | tf_op jit(solution)/shard_map/ppermute | solution.py:166
  95.6 5.7 %collective-permute-start.8 = (bf16[128,512]{1,0:T(8,128)(2,1)S(1)}, bf16[128,512]{1,0:T(8,128)(2,1)S(1)}, u32[]{:S(2)}, u32[]{:S(2)}) collective-permute-start(bf16[128,512]{1,0:T(8,128)(2,1)S(1)} %get-tuple-element.58), channel_id=1, source_target_pairs={{0,1},{1,2},{2,3},{3,0},{4,5},{5,6},{6,7},{7,4},{8,9},{9,10},{10,1... | collective-permute-start | bytes 393224 | tf_op jit(solution)/shard_map/ppermute | solution.py:166
  102.0 8.4 %collective-permute-start.11 = (bf16[512,128]{1,0:T(8,128)(2,1)S(1)}, bf16[512,128]{1,0:T(8,128)(2,1)}, u32[]{:S(2)}, u32[]{:S(2)}) collective-permute-start(bf16[512,128]{1,0:T(8,128)(2,1)S(1)} %get-tuple-element.66.refs_0_), channel_id=1, source_target_pairs={{0,3},{1,0},{2,1},{3,2},{4,7},{5,4},{6,5},{7,6},{8,11},{9,8},{10,9... | collective-permute-start | bytes 393224 | tf_op jit(solution)/shard_map/ppermute | solution.py:166
  105.0 5.5 %collective-permute-start.10 = (bf16[512,128]{1,0:T(8,128)(2,1)S(1)}, bf16[512,128]{1,0:T(8,128)(2,1)}, u32[]{:S(2)}, u32[]{:S(2)}) collective-permute-start(bf16[512,128]{1,0:T(8,128)(2,1)S(1)} %get-tuple-element.66.refs_0_), channel_id=1, source_target_pairs={{0,2},{1,3},{2,0},{3,1},{4,6},{5,7},{6,4},{7,5},{8,10},{9,11},{10,... | collective-permute-start | bytes 393224 | tf_op jit(solution)/shard_map/ppermute | solution.py:166
  105.0 8.0 %collective-permute-start.9 = (bf16[512,128]{1,0:T(8,128)(2,1)S(1)}, bf16[512,128]{1,0:T(8,128)(2,1)}, u32[]{:S(2)}, u32[]{:S(2)}) collective-permute-start(bf16[512,128]{1,0:T(8,128)(2,1)S(1)} %get-tuple-element.66.refs_0_), channel_id=1, source_target_pairs={{0,1},{1,2},{2,3},{3,0},{4,5},{5,6},{6,7},{7,4},{8,9},{9,10},{10,1... | collective-permute-start | bytes 393224 | tf_op jit(solution)/shard_map/ppermute | solution.py:166
  113.0 1.2 copy-start.4
  117.2 6.5 %collective-permute-start.12 = (bf16[4,128,1664]{2,1,0:T(8,128)(2,1)}, bf16[4,128,1664]{2,1,0:T(8,128)(2,1)}, u32[]{:S(2)}, u32[]{:S(2)}) collective-permute-start(bf16[4,128,1664]{2,1,0:T(8,128)(2,1)} %cross.3), channel_id=1, source_target_pairs={{0,4},{4,0},{1,5},{5,1},{2,6},{6,2},{3,7},{7,3},{8,12},{12,8},{9,1... | collective-permute-start | bytes 5111816 | tf_op jit(solution)/shard_map/ppermute | solution.py:170
  119.4 4.3 %copy-start.5 = (bf16[128,3328]{1,0:T(8,128)(2,1)S(1)}, bf16[128,3328]{1,0:T(8,128)(2,1)}, u32[]{:S(2)}) copy-start(bf16[128,3328]{1,0:T(8,128)(2,1)} %copy-done.2) | copy-start | bytes 2555908
  123.4 4.1 %collective-permute-start.13 = (bf16[4,128,1664]{2,1,0:T(8,128)(2,1)}, bf16[4,128,1664]{2,1,0:T(8,128)(2,1)S(1)}, u32[]{:S(2)}, u32[]{:S(2)}) collective-permute-start(bf16[4,128,1664]{2,1,0:T(8,128)(2,1)} %cross.2), channel_id=1, source_target_pairs={{0,4},{4,0},{1,5},{5,1},{2,6},{6,2},{3,7},{7,3},{8,12},{12,8},{9,1... | collective-permute-start | bytes 5111816 | tf_op jit(solution)/shard_map/ppermute | solution.py:170
  127.4 3.8 %copy-start.10 = (bf16[128,1664]{1,0:T(8,128)(2,1)S(1)}, bf16[128,1664]{1,0:T(8,128)(2,1)}, u32[]{:S(2)}) copy-start(bf16[128,1664]{1,0:T(8,128)(2,1)} %get-tuple-element.65) | copy-start | bytes 1277956
  131.3 12.6 %collective-permute-start.14 = (bf16[128,1664]{1,0:T(8,128)(2,1)S(1)}, bf16[128,1664]{1,0:T(8,128)(2,1)S(1)}, u32[]{:S(2)}, u32[]{:S(2)}) collective-permute-start(bf16[128,1664]{1,0:T(8,128)(2,1)S(1)} %copy-done.10), channel_id=1, source_target_pairs={{0,16},{8,24},{16,0},{24,8},{1,17},{9,25},{17,1},{25,9},{2,18},{10... | collective-permute-start | bytes 1277960 | tf_op jit(solution)/shard_map/ppermute | solution.py:166
  134.1 23.0 %collective-permute-start.15 = (bf16[128,1664]{1,0:T(8,128)(2,1)}, bf16[128,1664]{1,0:T(8,128)(2,1)}, u32[]{:S(2)}, u32[]{:S(2)}) collective-permute-start(bf16[128,1664]{1,0:T(8,128)(2,1)} %get-tuple-element.68), channel_id=1, source_target_pairs={{0,8},{8,16},{16,24},{24,0},{1,9},{9,17},{17,25},{25,1},{2,10},{10... | collective-permute-start | bytes 1277960 | tf_op jit(solution)/shard_map/ppermute | solution.py:166
  134.4 22.7 %collective-permute-start.16 = (bf16[128,1664]{1,0:T(8,128)(2,1)}, bf16[128,1664]{1,0:T(8,128)(2,1)}, u32[]{:S(2)}, u32[]{:S(2)}) collective-permute-start(bf16[128,1664]{1,0:T(8,128)(2,1)} %get-tuple-element.70), channel_id=1, source_target_pairs={{0,24},{8,0},{16,8},{24,16},{1,25},{9,1},{17,9},{25,17},{2,26},{10... | collective-permute-start | bytes 1277960 | tf_op jit(solution)/shard_map/ppermute | solution.py:166
  136.8 26.5 %collective-permute-start.20 = (bf16[128,1664]{1,0:T(8,128)(2,1)}, bf16[128,1664]{1,0:T(8,128)(2,1)}, u32[]{:S(2)}, u32[]{:S(2)}) collective-permute-start(bf16[128,1664]{1,0:T(8,128)(2,1)} %get-tuple-element.76), channel_id=1, source_target_pairs={{0,32},{32,64},{64,96},{96,0},{1,33},{33,65},{65,97},{97,1},{2,34}... | collective-permute-start | bytes 1277960 | tf_op jit(solution)/shard_map/ppermute | solution.py:166
  138.1 26.4 %collective-permute-start.21 = (bf16[128,1664]{1,0:T(8,128)(2,1)}, bf16[128,1664]{1,0:T(8,128)(2,1)}, u32[]{:S(2)}, u32[]{:S(2)}) collective-permute-start(bf16[128,1664]{1,0:T(8,128)(2,1)} %get-tuple-element.77), channel_id=1, source_target_pairs={{0,64},{32,96},{64,0},{96,32},{1,65},{33,97},{65,1},{97,33},{2,66}... | collective-permute-start | bytes 1277960 | tf_op jit(solution)/shard_map/ppermute | solution.py:166
  143.9 0.8 copy-start.9
  144.7 19.8 %collective-permute-start.22 = (bf16[128,1664]{1,0:T(8,128)(2,1)}, bf16[128,1664]{1,0:T(8,128)(2,1)}, u32[]{:S(2)}, u32[]{:S(2)}) collective-permute-start(bf16[128,1664]{1,0:T(8,128)(2,1)} %get-tuple-element.78), channel_id=1, source_target_pairs={{0,96},{32,0},{64,32},{96,64},{1,97},{33,1},{65,33},{97,65},{2,98}... | collective-permute-start | bytes 1277960 | tf_op jit(solution)/shard_map/ppermute | solution.py:166
  149.2 0.8 copy-start.7
  150.0 21.6 %all-to-all-start = ((bf16[32,16,512]{2,1,0:T(8,128)(2,1)}), bf16[32,16,512]{2,1,0:T(8,128)(2,1)}, u32[]{:S(2)}, u32[]{:S(2)}) async-start(bf16[32,16,512]{2,1,0:T(8,128)(2,1)} %bitcast.10), calls=%async_computation | async-start | bytes 1048576 | tf_op jit(solution)/shard_map/all_to_all | solution.py:533
  157.0 70.2 %all-gather.5.cloned.1.call-start = ((), (), s32[]{:S(2)}) async-start(), calls=%async_computation.3 | async-start | bytes 7028736 | tf_op jit(solution)/shard_map/all_gather | solution.py:544
  159.4 11.0 %collective-permute-start.17 = (bf16[32,1664]{1,0:T(8,128)(2,1)}, bf16[32,1664]{1,0:T(8,128)(2,1)}, u32[]{:S(2)}, u32[]{:S(2)}) collective-permute-start(bf16[32,1664]{1,0:T(8,128)(2,1)} %get-tuple-element.73), channel_id=1, source_target_pairs={{0,32},{32,64},{64,96},{96,0},{1,33},{33,65},{65,97},{97,1},{2,34}... | collective-permute-start | bytes 319496 | tf_op jit(solution)/shard_map/ppermute | solution.py:166
  160.9 12.7 %collective-permute-start.18 = (bf16[32,1664]{1,0:T(8,128)(2,1)}, bf16[32,1664]{1,0:T(8,128)(2,1)}, u32[]{:S(2)}, u32[]{:S(2)}) collective-permute-start(bf16[32,1664]{1,0:T(8,128)(2,1)} %get-tuple-element.74), channel_id=1, source_target_pairs={{0,64},{32,96},{64,0},{96,32},{1,65},{33,97},{65,1},{97,33},{2,66}... | collective-permute-start | bytes 319496 | tf_op jit(solution)/shard_map/ppermute | solution.py:166
  163.3 10.3 %collective-permute-start.19 = (bf16[32,1664]{1,0:T(8,128)(2,1)}, bf16[32,1664]{1,0:T(8,128)(2,1)}, u32[]{:S(2)}, u32[]{:S(2)}) collective-permute-start(bf16[32,1664]{1,0:T(8,128)(2,1)} %get-tuple-element.75), channel_id=1, source_target_pairs={{0,96},{32,0},{64,32},{96,64},{1,97},{33,1},{65,33},{97,65},{2,98}... | collective-permute-start | bytes 319496 | tf_op jit(solution)/shard_map/ppermute | solution.py:166
  166.8 6.8 %collective-permute-start.23 = (bf16[32,1664]{1,0:T(8,128)(2,1)}, bf16[32,1664]{1,0:T(8,128)(2,1)}, u32[]{:S(2)}, u32[]{:S(2)}) collective-permute-start(bf16[32,1664]{1,0:T(8,128)(2,1)} %get-tuple-element.80), channel_id=1, source_target_pairs={{0,8},{8,16},{16,24},{24,0},{1,9},{9,17},{17,25},{25,1},{2,10},{10... | collective-permute-start | bytes 319496 | tf_op jit(solution)/shard_map/ppermute | solution.py:166
  168.1 6.5 %collective-permute-start.24 = (bf16[32,1664]{1,0:T(8,128)(2,1)}, bf16[32,1664]{1,0:T(8,128)(2,1)}, u32[]{:S(2)}, u32[]{:S(2)}) collective-permute-start(bf16[32,1664]{1,0:T(8,128)(2,1)} %get-tuple-element.81), channel_id=1, source_target_pairs={{0,16},{8,24},{16,0},{24,8},{1,17},{9,25},{17,1},{25,9},{2,18},{10... | collective-permute-start | bytes 319496 | tf_op jit(solution)/shard_map/ppermute | solution.py:166
  170.5 5.2 %collective-permute-start.25 = (bf16[32,1664]{1,0:T(8,128)(2,1)}, bf16[32,1664]{1,0:T(8,128)(2,1)}, u32[]{:S(2)}, u32[]{:S(2)}) collective-permute-start(bf16[32,1664]{1,0:T(8,128)(2,1)} %get-tuple-element.82), channel_id=1, source_target_pairs={{0,24},{8,0},{16,8},{24,16},{1,25},{9,1},{17,9},{25,17},{2,26},{10... | collective-permute-start | bytes 319496 | tf_op jit(solution)/shard_map/ppermute | solution.py:166
  172.8 0.8 copy-start.8
  177.7 19.9 %all-to-all-start.1 = ((bf16[32,16,512]{2,1,0:T(8,128)(2,1)}), bf16[32,16,512]{2,1,0:T(8,128)(2,1)}, u32[]{:S(2)}, u32[]{:S(2)}) async-start(bf16[32,16,512]{2,1,0:T(8,128)(2,1)} %copy-done.8), calls=%async_computation.1 | async-start | bytes 1048576 | tf_op jit(solution)/shard_map/all_to_all | solution.py:540
  227.2 7.6 %copy-start.6 = (bf16[128,3328]{1,0:T(8,128)(2,1)S(1)}, bf16[128,3328]{1,0:T(8,128)(2,1)}, u32[]{:S(2)}) copy-start(bf16[128,3328]{1,0:T(8,128)(2,1)} %copy-done.2) | copy-start | bytes 2555908
  230.8 10.5 %collective-permute-start.28 = (f32[16,128]{1,0:T(8,128)S(1)}, f32[16,128]{1,0:T(8,128)S(1)}, u32[]{:S(2)}, u32[]{:S(2)}) collective-permute-start(f32[16,128]{1,0:T(8,128)S(1)} %get-tuple-element.90), channel_id=1, source_target_pairs={{0,3},{1,0},{2,1},{3,2},{4,7},{5,4},{6,5},{7,6},{8,11},{9,8},{10,9... | collective-permute-start | bytes 24584 | tf_op jit(solution)/shard_map/ppermute | solution.py:166
  233.6 7.8 %collective-permute-start.27 = (f32[16,128]{1,0:T(8,128)S(1)}, f32[16,128]{1,0:T(8,128)S(1)}, u32[]{:S(2)}, u32[]{:S(2)}) collective-permute-start(f32[16,128]{1,0:T(8,128)S(1)} %get-tuple-element.90), channel_id=1, source_target_pairs={{0,2},{1,3},{2,0},{3,1},{4,6},{5,7},{6,4},{7,5},{8,10},{9,11},{10,... | collective-permute-start | bytes 24584 | tf_op jit(solution)/shard_map/ppermute | solution.py:166
  234.0 7.4 %collective-permute-start.26 = (f32[16,128]{1,0:T(8,128)S(1)}, f32[16,128]{1,0:T(8,128)S(1)}, u32[]{:S(2)}, u32[]{:S(2)}) collective-permute-start(f32[16,128]{1,0:T(8,128)S(1)} %get-tuple-element.90), channel_id=1, source_target_pairs={{0,1},{1,2},{2,3},{3,0},{4,5},{5,6},{6,7},{7,4},{8,9},{9,10},{10,1... | collective-permute-start | bytes 24584 | tf_op jit(solution)/shard_map/ppermute | solution.py:166
Sparse Core Ops, SparseCore 0:
  10.2 53.4 all-gather.2
  177.8 49.3 all-gather.4

commit v3 on v2

--- a/solution.py
+++ b/solution.py
@@ -174,9 +174,10 @@
     return [pltpu.with_memory_space_constraint(value, pltpu.HBM) for value in values]
 
 
-def call(kernel, name, operands, out_shape, scratch=(), in_specs=None, out_specs=None, flops=0):
+def call(kernel, name, operands, out_shape, scratch=(), in_specs=None, out_specs=None, flops=0, moved=None):
     shapes = out_shape if isinstance(out_shape, list) else [out_shape]
-    moved = sum(math.prod(v.shape) * v.dtype.itemsize for v in list(operands) + shapes)
+    if moved is None:
+        moved = sum(math.prod(v.shape) * v.dtype.itemsize for v in list(operands) + shapes)
     return pl.pallas_call(
         kernel,
         in_specs=in_specs or [VMEM] * len(operands),
@@ -187,6 +188,36 @@
         cost_estimate=pl.CostEstimate(flops=int(flops), bytes_accessed=int(moved), transcendentals=0),
         name=name,
     )(*operands)
+
+
+def blend_kernel(at_ref, momentum, gradient, out, held, sems):
+    width = out.shape[1]
+    loads = []
+    for start in range(0, width, TILE):
+        here = pl.ds(pl.multiple_of(at_ref[0] * width + start, 128), TILE)
+        for i, source in enumerate((momentum, gradient)):
+            target = held.at[i, :, start:start + TILE]
+            loads.append(pltpu.make_async_copy(source.at[:, here], target, sems.at[len(loads)]))
+            loads[-1].start()
+    for start in range(0, width, TILE):
+        for load in loads[2 * start // TILE:2 * start // TILE + 2]:
+            load.wait()
+        here = slice(start, start + TILE)
+        out[:, here] = (held[0, :, here].astype(F32) + held[1, :, here].astype(F32)).astype(HALF)
+
+
+def blend_block(momentum, gradient, block, width):
+    rows = momentum.shape[0]
+    return call(
+        blend_kernel,
+        "blend",
+        [jnp.full((1,), block, jnp.int32), *in_hbm([momentum, gradient])],
+        jax.ShapeDtypeStruct((rows, width), HALF),
+        in_specs=[SMEM, HBM, HBM],
+        scratch=[pltpu.VMEM((2, rows, width), HALF), pltpu.SemaphoreType.DMA((2 * width // TILE,))],
+        flops=rows * width,
+        moved=rows * width,
+    )
 
 
 def project_kernel(half, *refs):
@@ -505,14 +536,11 @@
     right_all = lax.all_gather(right_factor, row, axis=0, tiled=True)
     ranks = right_all.shape[0]
     blocks = [[None] * 4, [None] * 4]
-    last = place
     for half in range(2):
         for turn in (2, 1, 3, 0):
             block = lax.rem(place + turn, 4) * 2 + half
-            start = after(block, last) * half_width
-            pair = [lax.dynamic_slice_in_dim(v, start, half_width, 1).astype(F32) for v in (momentum, gradient)]
-            last = (pair[0] + pair[1]).astype(HALF)
-            blocks[half][turn] = ring(last, "col", turn) if turn else last
+            mine = blend_block(momentum, gradient, after(block, blocks[0][0]) if half else block, half_width)
+            blocks[half][turn] = ring(mine, "col", turn) if turn else mine
     partial = project(blocks[0], right_all, 0)
     parts = project(blocks[1], right_all, 1, partial)
     terms = [parts[0]] + [ring(parts[turn], "col", -turn) for turn in (2, 1, 3)]
@@ -528,19 +556,20 @@
         first[turn] = ring(after(first[turn], second[0]), "x", turn)
         second[turn] = ring(second[turn], "y", turn)
 
-    gram_part = gram_of([after(factors[0], first[2])] + factors[1:])
+    gram_part = gram_of([after(factors[0], first[1])] + factors[1:])
     rows = ranks // ranks_dev
     gram_pieces = lax.all_to_all(gram_part, row, split_axis=0, concat_axis=0, tiled=True)
-    copies = spread(gram_pieces.reshape(rows, ranks_dev, ranks))
 
     first = list(fold(first, at_y))
     for turn in (2, 1, 3):
         first[turn] = ring(first[turn], "y", turn)
     second = list(fold(second, at_x))
-    gram = lax.all_to_all(copies.reshape(ranks, ranks), row, split_axis=0, concat_axis=0, tiled=True)
     for turn in (2, 1, 3):
         second[turn] = ring(second[turn], "x", turn)
-    done = finish([after(first[0], copies)] + first[1:], second)
+    first[0], gram_pieces = lax.optimization_barrier((first[0], gram_pieces))
+    done = finish(first, second)
+    copies = spread(gram_pieces.reshape(rows, ranks_dev, ranks))
+    gram = lax.all_to_all(copies.reshape(ranks, ranks), row, split_axis=0, concat_axis=0, tiled=True)
     total = lax.all_gather(done, row, axis=0, tiled=True)
     total = total.reshape(16, 2, 2, EIGHTH, TILE)
 

time: 250 us -> 251 us (level)
  Pallas kernels: 65.3 us -> 85.1 us
  other arithmetic: 19.9 us -> 1.29 us
  waiting for transfers between devices: 80.9 us -> 84.8 us
  local copies, waits for them, and re-layouts: 8.54 us -> 5.31 us
    pallas_call x14 -> x22, Pallas kernels: 40.7 us -> 60.5 us  [call(): pl.pallas_call(kernel, in_specs=in_specs or [VMEM] * len(operands), out_s...]
    convert_element_type x8 -> x0, other arithmetic: 18.6 us -> none  [per_device(): last = (pair[0] + pair[1]).astype(HALF)]
    unnamed x22 -> x10, local copies, waits for them, and re-layouts: 8.54 us -> 5.31 us
    all_gather x1, waiting for transfers between devices: 7.65 us -> 10.2 us  [per_device(): right_all = lax.all_gather(right_factor, row, axis=0, tiled=True)]
  transfers between devices with their start and end apart: 33 -> 33, of which waited for: 16 -> 18; matrix products, arithmetic and copies ran while one was open for 8% -> 0% of each run, Pallas kernels for 19% -> 27%
where the time goes in v3:
time: 251 us; the launch traced here: 250 us
  Pallas kernels  85.1 us (34%)
  waiting for transfers between devices  84.8 us (34%)
  starting transfers between devices  59.2 us (24%)
  between operations  14.3 us (6%)
  local copies, waits for them, and re-layouts  5.31 us (2%)
    pallas_call x22, Pallas kernels, call(): pl.pallas_call(kernel, in_specs=in_specs or [VMEM] * len(operands), out_s...  60.5 us
    ppermute x27, waiting for transfers between devices, ring(): lax.ppermute(value, axis, [(i, (i + shift) % size) for i in range(size)])  54.5 us
    ppermute x27, starting transfers between devices, ring(): lax.ppermute(value, axis, [(i, (i + shift) % size) for i in range(size)])  44 us
    pallas_call x1, Pallas kernels, factorize(): pl.pallas_call(factor_kernel, out_shape=[pltpu.HBM(*out) for out in outs]...  24.6 us
    all_to_all x1, waiting for transfers between devices, per_device(): lax.all_to_all(copies.reshape(ranks, ranks), row, split_axis=0, concat_ax...  13.9 us
    all_gather x1, waiting for transfers between devices, per_device(): right_all = lax.all_gather(right_factor, row, axis=0, tiled=True)  10.2 us
    all_to_all x1, starting transfers between devices, per_device(): lax.all_to_all(copies.reshape(ranks, ranks), row, split_axis=0, concat_ax...  6.22 us
    all_to_all x1, starting transfers between devices, per_device(): lax.all_to_all(gram_part, row, split_axis=0, concat_axis=0, tiled=True)  5.75 us
  transfers between devices with their start and end apart: 33, of which 18 were waited for; matrix products, arithmetic and copies ran while one was open for 0% of the time, Pallas kernels for 27%

profile of v3, /device:TPU:1, one launch (start us, length us, event | category | flops | bytes accessed | tf_op | source)
XLA Modules:
  0.0 250.0 jit_solution(17729742732161301765)
XLA Ops:
  7.9 2.5 blend.14
  10.4 4.5 %collective-permute-start.4 = (bf16[128,3328]{1,0:T(8,128)(2,1)}, bf16[128,3328]{1,0:T(8,128)(2,1)S(1)}, u32[]{:S(2)}, u32[]{:S(2)}) collective-permute-start(bf16[128,3328]{1,0:T(8,128)(2,1)} %blend.14), channel_id=1, source_target_pairs={{0,2},{1,3},{2,0},{3,1},{4,6},{5,7},{6,4},{7,5},{8,10},{9,11},{10,... | collective-permute-start | bytes 2555912 | tf_op jit(solution)/shard_map/ppermute | solution.py:166
  14.9 2.5 blend.15
  17.9 2.4 blend.13
  21.4 1.5 blend.8.refs_0_.refs_4_
  22.9 2.6 %blend.12 = bf16[128,3328]{1,0:T(8,128)(2,1)} custom-call(s32[1]{0:T(128)} %bitcast.8.at_ref, bf16[128,26624]{1,0:T(8,128)(2,1)} %momentum.15, bf16[128,26624]{1,0:T(8,128)(2,1)} %gradient.15), custom_call_target="tpu_custom_call" | custom-call | flops 425984 | bytes 425984 | tf_op jit(solution)/shard_map/blend/pallas_call | solution.py:181
  25.5 1.7 collective-permute-start.2
  27.2 2.4 blend.11
  30.6 2.4 blend.10
  34.6 1.5 blend.9.refs_0_.refs_4_
  36.1 16.4 %collective-permute-done.5.refs_3_.refs_7_ = bf16[128,3328]{1,0:T(8,128)(2,1)S(1)} collective-permute-done((bf16[128,3328]{1,0:T(8,128)(2,1)}, bf16[128,3328]{1,0:T(8,128)(2,1)S(1)}, u32[]{:S(2)}, u32[]{:S(2)}) %collective-permute-start.5) | collective-permute-done | bytes 852000 | tf_op jit(solution)/shard_map/ppermute | solution.py:166
  53.5 10.2 %all-gather.3.cloned.1.call-done.refs_4_ = bf16[512,6656]{1,0:T(8,128)(2,1)} async-done(((bf16[16,6656]{1,0:T(8,128)(2,1)}), bf16[512,6656]{1,0:T(8,128)(2,1)}) %all-gather.3.cloned.1.call-update) | async-done | bytes 6815760 | tf_op jit(solution)/shard_map/all_gather | solution.py:536
  63.8 2.9 %copy-done = bf16[512,6656]{1,0:T(8,128)(2,1)S(1)} copy-done((bf16[512,6656]{1,0:T(8,128)(2,1)S(1)}, bf16[512,6656]{1,0:T(8,128)(2,1)}, u32[]{:S(2)}) %copy-start) | copy-done | bytes 6815768
  66.7 3.4 %project.2.refs_5_ = f32[512,512]{1,0:T(8,128)S(1)} custom-call(bf16[128,3328]{1,0:T(8,128)(2,1)S(1)} %blend.8.refs_0_.refs_4_, bf16[128,3328]{1,0:T(8,128)(2,1)} %collective-permute-done.3.refs_1_.refs_5_, bf16[128,3328]{1,0:T(8,128)(2,1)S(1)} %collective-permute-done.4.refs_2_.refs_6_, bf16[128,3328]{1,0:T(8,128)(2,1)S(1)} %collective-permute-done.5.refs_3_.refs_7_, ...), custom_call_target="tpu_custom_call" | custom-call | flops 1744830464 | bytes 11272192 | tf_op jit(solution)/shard_map/project/pallas_call | solution.py:181
  71.3 18.0 %collective-permute-done.refs_1_.refs_5_ = bf16[128,3328]{1,0:T(8,128)(2,1)} collective-permute-done((bf16[128,3328]{1,0:T(8,128)(2,1)}, bf16[128,3328]{1,0:T(8,128)(2,1)}, u32[]{:S(2)}, u32[]{:S(2)}) %collective-permute-start) | collective-permute-done | bytes 852000 | tf_op jit(solution)/shard_map/ppermute | solution.py:166
  89.4 3.8 %project.3 = (bf16[128,512]{1,0:T(8,128)(2,1)S(1)}, bf16[128,512]{1,0:T(8,128)(2,1)S(1)}, bf16[128,512]{1,0:T(8,128)(2,1)S(1)}, bf16[128,512]{1,0:T(8,128)(2,1)S(1)}) custom-call(bf16[128,3328]{1,0:T(8,128)(2,1)S(1)} %blend.9.refs_0_.refs_4_, bf16[128,3328]{1,0:T(8,128)(2,1)} %collective-permute-done.refs_1_.refs_5_, ...), custom_call_target="tpu_custom_call" | custom-call | flops 1744830464 | bytes 11796480 | tf_op jit(solution)/shard_map/project/pallas_call | solution.py:181
  93.1 3.0 %collective-permute-start.6 = (bf16[128,512]{1,0:T(8,128)(2,1)S(1)}, bf16[128,512]{1,0:T(8,128)(2,1)S(1)}, u32[]{:S(2)}, u32[]{:S(2)}) collective-permute-start(bf16[128,512]{1,0:T(8,128)(2,1)S(1)} %get-tuple-element.49), channel_id=1, source_target_pairs={{0,2},{1,3},{2,0},{3,1},{4,6},{5,7},{6,4},{7,5},{8,10},{9,11},{10,... | collective-permute-start | bytes 393224 | tf_op jit(solution)/shard_map/ppermute | solution.py:166
  96.2 1.5 collective-permute-start.8
  97.6 1.6 collective-permute-done.6.refs_1_
  99.3 1.9 collective-permute-done.7.refs_2_
  102.5 2.3 collective-permute-start.11
  104.8 1.5 collective-permute-start.10
  107.2 3.0 %collective-permute-done.10.refs_2_ = bf16[512,128]{1,0:T(8,128)(2,1)} collective-permute-done((bf16[512,128]{1,0:T(8,128)(2,1)S(1)}, bf16[512,128]{1,0:T(8,128)(2,1)}, u32[]{:S(2)}, u32[]{:S(2)}) %collective-permute-start.10) | collective-permute-done | bytes 131104 | tf_op jit(solution)/shard_map/ppermute | solution.py:166
  110.2 2.2 collective-permute-done.9.refs_1_
  112.4 3.4 %cross.3 = bf16[4,128,1664]{2,1,0:T(8,128)(2,1)} custom-call(s32[2]{0:T(128)S(1)} %pad_add_fusion.3.at_ref, bf16[512,128]{1,0:T(8,128)(2,1)S(1)} %get-tuple-element.64.refs_0_, bf16[512,128]{1,0:T(8,128)(2,1)} %collective-permute-done.9.refs_1_, bf16[512,128]{1,0:T(8,128)(2,1)} %collective-permute-done.10.refs_2_, ...), custom_call_target="tpu_custom_call" | custom-call | flops 872415232 | bytes 5636104 | tf_op jit(solution)/shard_map/cross/pallas_call | solution.py:181
  115.8 2.8 %collective-permute-start.12 = (bf16[4,128,1664]{2,1,0:T(8,128)(2,1)}, bf16[4,128,1664]{2,1,0:T(8,128)(2,1)}, u32[]{:S(2)}, u32[]{:S(2)}) collective-permute-start(bf16[4,128,1664]{2,1,0:T(8,128)(2,1)} %cross.3), channel_id=1, source_target_pairs={{0,4},{4,0},{1,5},{5,1},{2,6},{6,2},{3,7},{7,3},{8,12},{12,8},{9,1... | collective-permute-start | bytes 5111816 | tf_op jit(solution)/shard_map/ppermute | solution.py:170
  118.7 3.9 %cross.2 = bf16[4,128,1664]{2,1,0:T(8,128)(2,1)} custom-call(s32[2]{0:T(128)S(1)} %pad_add_fusion.2.at_ref, bf16[512,128]{1,0:T(8,128)(2,1)S(1)} %get-tuple-element.64.refs_0_, bf16[512,128]{1,0:T(8,128)(2,1)} %collective-permute-done.9.refs_1_, bf16[512,128]{1,0:T(8,128)(2,1)} %collective-permute-done.10.refs_2_, ...), custom_call_target="tpu_custom_call" | custom-call | flops 872415232 | bytes 5636104 | tf_op jit(solution)/shard_map/cross/pallas_call | solution.py:181
  123.0 3.8 %cross_add.2 = (bf16[128,1664]{1,0:T(8,128)(2,1)}, bf16[128,1664]{1,0:T(8,128)(2,1)}, bf16[128,1664]{1,0:T(8,128)(2,1)}, bf16[128,1664]{1,0:T(8,128)(2,1)}) custom-call(s32[2]{0:T(128)S(1)} %pad_add_fusion.at_ref, bf16[512,128]{1,0:T(8,128)(2,1)S(1)} %get-tuple-element.64.refs_0_, bf16[512,128]{1,0:T(8,128)(2,1)} %collective-permute-done.9.refs_1_, ...), custom_call_target="tpu_custom_call" | custom-call | flops 872415232 | bytes 7340040 | tf_op jit(solution)/shard_map/cross_add/pallas_call | solution.py:181
  126.9 3.8 %cross_add.3 = (bf16[128,1664]{1,0:T(8,128)(2,1)}, bf16[128,1664]{1,0:T(8,128)(2,1)}, bf16[128,1664]{1,0:T(8,128)(2,1)}, bf16[128,1664]{1,0:T(8,128)(2,1)}) custom-call(s32[2]{0:T(128)S(1)} %pad_add_fusion.1.at_ref, bf16[512,128]{1,0:T(8,128)(2,1)S(1)} %get-tuple-element.64.refs_0_, bf16[512,128]{1,0:T(8,128)(2,1)} %collective-permute-done.9.refs_1_, ...), custom_call_target="tpu_custom_call" | custom-call | flops 872415232 | bytes 7340040 | tf_op jit(solution)/shard_map/cross_add/pallas_call | solution.py:181
  132.0 2.5 collective-permute-start.15
  136.8 2.6 %collective-permute-start.21 = (bf16[128,1664]{1,0:T(8,128)(2,1)}, bf16[128,1664]{1,0:T(8,128)(2,1)}, u32[]{:S(2)}, u32[]{:S(2)}) collective-permute-start(bf16[128,1664]{1,0:T(8,128)(2,1)} %get-tuple-element.71), channel_id=1, source_target_pairs={{0,64},{32,96},{64,0},{96,32},{1,65},{33,97},{65,1},{97,33},{2,66}... | collective-permute-start | bytes 1277960 | tf_op jit(solution)/shard_map/ppermute | solution.py:166
  139.5 3.8 %collective-permute-done.14.refs_1_ = bf16[128,1664]{1,0:T(8,128)(2,1)S(1)} collective-permute-done((bf16[128,1664]{1,0:T(8,128)(2,1)}, bf16[128,1664]{1,0:T(8,128)(2,1)S(1)}, u32[]{:S(2)}, u32[]{:S(2)}) %collective-permute-start.14) | collective-permute-done | bytes 426016 | tf_op jit(solution)/shard_map/ppermute | solution.py:166
  144.0 2.8 %collective-permute-start.22 = (bf16[128,1664]{1,0:T(8,128)(2,1)}, bf16[128,1664]{1,0:T(8,128)(2,1)}, u32[]{:S(2)}, u32[]{:S(2)}) collective-permute-start(bf16[128,1664]{1,0:T(8,128)(2,1)} %get-tuple-element.72), channel_id=1, source_target_pairs={{0,96},{32,0},{64,32},{96,64},{1,97},{33,1},{65,33},{97,65},{2,98}... | collective-permute-start | bytes 1277960 | tf_op jit(solution)/shard_map/ppermute | solution.py:166
  146.8 1.7 gram.1
  149.3 5.7 %all-to-all-start = ((bf16[32,16,512]{2,1,0:T(8,128)(2,1)}), bf16[32,16,512]{2,1,0:T(8,128)(2,1)}, u32[]{:S(2)}, u32[]{:S(2)}) async-start(bf16[32,16,512]{2,1,0:T(8,128)(2,1)} %bitcast.20), calls=%async_computation | async-start | bytes 1048576 | tf_op jit(solution)/shard_map/all_to_all | solution.py:561
  155.2 2.3 fold.2
  158.9 2.4 collective-permute-start.18
  162.5 2.3 fold.3
  166.1 2.4 collective-permute-start.24
  170.3 2.3 collective-permute-done.24.refs_6_
  173.7 2.0 finish.1
  177.7 6.2 %all-to-all-start.1 = ((bf16[32,16,512]{2,1,0:T(8,128)(2,1)}), bf16[32,16,512]{2,1,0:T(8,128)(2,1)}, u32[]{:S(2)}, u32[]{:S(2)}) async-start(bf16[32,16,512]{2,1,0:T(8,128)(2,1)} %copy-done.3), calls=%async_computation.1 | async-start | bytes 1048576 | tf_op jit(solution)/shard_map/all_to_all | solution.py:572
  184.0 13.9 %all-to-all-done.1 = bf16[32,16,512]{2,1,0:T(8,128)(2,1)} async-done(((bf16[32,16,512]{2,1,0:T(8,128)(2,1)}), bf16[32,16,512]{2,1,0:T(8,128)(2,1)}, u32[]{:S(2)}, u32[]{:S(2)}) %all-to-all-start.1) | async-done | bytes 524320 | tf_op jit(solution)/shard_map/all_to_all | solution.py:572
  197.9 24.6 %factorize.1 = (bf16[32,512]{1,0:T(8,128)(2,1)}, bf16[512,512]{1,0:T(8,128)(2,1)}, f32[128,512]{1,0:T(8,128)}) custom-call(s32[1]{0:T(128)} %bitcast.1.at_ref, bf16[512,512]{1,0:T(8,128)(2,1)} %bitcast.18.g_ref, bf16[512,128]{1,0:T(8,128)(2,1)S(1)} %get-tuple-element.64.refs_0_, bf16[512,128]{1,0:T(8,128)(2,1)} %collective-permute-done.9.refs_1_, ...), custom_call_target="tpu_custom_call" | custom-call | flops 20000000000 | bytes 4194304 | tf_op jit(solution)/shard_map/factorize/pallas_call | solution.py:138
  222.4 5.5 %all-gather.5.cloned.1.call-done = bf16[2048,1664]{1,0:T(8,128)(2,1)} async-done(((bf16[64,1664]{1,0:T(8,128)(2,1)}), bf16[2048,1664]{1,0:T(8,128)(2,1)}) %all-gather.5.cloned.1.call-update) | async-done | bytes 6815760 | tf_op jit(solution)/shard_map/all_gather | solution.py:573
  228.0 3.5 %right_rows.1 = (f32[16,6656]{1,0:T(8,128)S(1)}, f32[16,128]{1,0:T(8,128)S(1)}, bf16[512,512]{1,0:T(8,128)(2,1)S(1)}, bf16[16,2,2,32,1664]{4,3,2,1,0:T(8,128)(2,1)S(1)}) custom-call(bf16[32,512]{1,0:T(8,128)(2,1)} %get-tuple-element.78.rows_hbm, bf16[512,512]{1,0:T(8,128)(2,1)} %get-tuple-element.79.weights_hbm, bf16[16,2,2,32,1664]{4,3,2,1,0:T(8,128)(2,1)} %bitcast.21), custom_call_target="tpu_custom_call" | custom-call | flops 218103808 | bytes 15147008 | tf_op jit(solution)/shard_map/right_rows/pallas_call | solution.py:181
  231.5 2.7 %collective-permute-start.28 = (f32[16,128]{1,0:T(8,128)S(1)}, f32[16,128]{1,0:T(8,128)S(1)}, u32[]{:S(2)}, u32[]{:S(2)}) collective-permute-start(f32[16,128]{1,0:T(8,128)S(1)} %get-tuple-element.84), channel_id=1, source_target_pairs={{0,3},{1,0},{2,1},{3,2},{4,7},{5,4},{6,5},{7,6},{8,11},{9,8},{10,9... | collective-permute-start | bytes 24584 | tf_op jit(solution)/shard_map/ppermute | solution.py:166
  235.3 6.8 %feedback.1 = bf16[512,6656]{1,0:T(8,128)(2,1)} custom-call(s32[1]{0:T(128)} %bitcast.at_ref, bf16[512,512]{1,0:T(8,128)(2,1)S(1)} %get-tuple-element.80.weights_ref, bf16[16,2,2,32,1664]{4,3,2,1,0:T(8,128)(2,1)S(1)} %get-tuple-element.81.total_ref, bf16[128,3328]{1,0:T(8,128)(2,1)S(1)} %blend.8.refs_0_.refs_4_, ...), custom_call_target="tpu_custom_call" | custom-call | flops 3489660928 | bytes 20971524 | tf_op jit(solution)/shard_map/feedback/pallas_call | solution.py:181
  (59 shorter events, 25.9 us)
Async XLA Ops:
  7.2 56.6 %all-gather.3.cloned.1.call-start = ((), (), s32[]{:S(2)}) async-start(), calls=%async_computation.2 | async-start | bytes 7028736 | tf_op jit(solution)/shard_map/all_gather | solution.py:536
  10.4 23.4 %collective-permute-start.4 = (bf16[128,3328]{1,0:T(8,128)(2,1)}, bf16[128,3328]{1,0:T(8,128)(2,1)S(1)}, u32[]{:S(2)}, u32[]{:S(2)}) collective-permute-start(bf16[128,3328]{1,0:T(8,128)(2,1)} %blend.14), channel_id=1, source_target_pairs={{0,2},{1,3},{2,0},{3,1},{4,6},{5,7},{6,4},{7,5},{8,10},{9,11},{10,... | collective-permute-start | bytes 2555912 | tf_op jit(solution)/shard_map/ppermute | solution.py:166
  17.4 35.2 %collective-permute-start.5 = (bf16[128,3328]{1,0:T(8,128)(2,1)}, bf16[128,3328]{1,0:T(8,128)(2,1)S(1)}, u32[]{:S(2)}, u32[]{:S(2)}) collective-permute-start(bf16[128,3328]{1,0:T(8,128)(2,1)} %blend.15), channel_id=1, source_target_pairs={{0,3},{1,0},{2,1},{3,2},{4,7},{5,4},{6,5},{7,6},{8,11},{9,8},{10,9... | collective-permute-start | bytes 2555912 | tf_op jit(solution)/shard_map/ppermute | solution.py:166
  20.3 33.2 %collective-permute-start.3 = (bf16[128,3328]{1,0:T(8,128)(2,1)}, bf16[128,3328]{1,0:T(8,128)(2,1)}, u32[]{:S(2)}, u32[]{:S(2)}) collective-permute-start(bf16[128,3328]{1,0:T(8,128)(2,1)} %blend.13), channel_id=1, source_target_pairs={{0,1},{1,2},{2,3},{3,0},{4,5},{5,6},{6,7},{7,4},{8,9},{9,10},{10,1... | collective-permute-start | bytes 2555912 | tf_op jit(solution)/shard_map/ppermute | solution.py:166
  25.5 45.8 %collective-permute-start.2 = (bf16[128,3328]{1,0:T(8,128)(2,1)}, bf16[128,3328]{1,0:T(8,128)(2,1)}, u32[]{:S(2)}, u32[]{:S(2)}) collective-permute-start(bf16[128,3328]{1,0:T(8,128)(2,1)} %blend.12), channel_id=1, source_target_pairs={{0,3},{1,0},{2,1},{3,2},{4,7},{5,4},{6,5},{7,6},{8,11},{9,8},{10,9... | collective-permute-start | bytes 2555912 | tf_op jit(solution)/shard_map/ppermute | solution.py:166
  29.6 41.7 %collective-permute-start.1 = (bf16[128,3328]{1,0:T(8,128)(2,1)}, bf16[128,3328]{1,0:T(8,128)(2,1)}, u32[]{:S(2)}, u32[]{:S(2)}) collective-permute-start(bf16[128,3328]{1,0:T(8,128)(2,1)} %blend.11), channel_id=1, source_target_pairs={{0,2},{1,3},{2,0},{3,1},{4,6},{5,7},{6,4},{7,5},{8,10},{9,11},{10,... | collective-permute-start | bytes 2555912 | tf_op jit(solution)/shard_map/ppermute | solution.py:166
  33.8 55.6 %collective-permute-start = (bf16[128,3328]{1,0:T(8,128)(2,1)}, bf16[128,3328]{1,0:T(8,128)(2,1)}, u32[]{:S(2)}, u32[]{:S(2)}) collective-permute-start(bf16[128,3328]{1,0:T(8,128)(2,1)} %blend.10), channel_id=1, source_target_pairs={{0,1},{1,2},{2,3},{3,0},{4,5},{5,6},{6,7},{7,4},{8,9},{9,10},{10,1... | collective-permute-start | bytes 2555912 | tf_op jit(solution)/shard_map/ppermute | solution.py:166
  63.8 2.9 %copy-start = (bf16[512,6656]{1,0:T(8,128)(2,1)S(1)}, bf16[512,6656]{1,0:T(8,128)(2,1)}, u32[]{:S(2)}) copy-start(bf16[512,6656]{1,0:T(8,128)(2,1)} %all-gather.3.cloned.1.call-done.refs_4_) | copy-start | bytes 20447236
  66.7 22.7 %copy-start.1 = (bf16[512,6656]{1,0:T(8,128)(2,1)S(1)}, bf16[512,6656]{1,0:T(8,128)(2,1)}, u32[]{:S(2)}) copy-start(bf16[512,6656]{1,0:T(8,128)(2,1)} %all-gather.3.cloned.1.call-done.refs_4_) | copy-start | bytes 20447236
  93.1 6.2 %collective-permute-start.6 = (bf16[128,512]{1,0:T(8,128)(2,1)S(1)}, bf16[128,512]{1,0:T(8,128)(2,1)S(1)}, u32[]{:S(2)}, u32[]{:S(2)}) collective-permute-start(bf16[128,512]{1,0:T(8,128)(2,1)S(1)} %get-tuple-element.49), channel_id=1, source_target_pairs={{0,2},{1,3},{2,0},{3,1},{4,6},{5,7},{6,4},{7,5},{8,10},{9,11},{10,... | collective-permute-start | bytes 393224 | tf_op jit(solution)/shard_map/ppermute | solution.py:166
  96.2 5.0 %collective-permute-start.7 = (bf16[128,512]{1,0:T(8,128)(2,1)S(1)}, bf16[128,512]{1,0:T(8,128)(2,1)S(1)}, u32[]{:S(2)}, u32[]{:S(2)}) collective-permute-start(bf16[128,512]{1,0:T(8,128)(2,1)S(1)} %get-tuple-element.50), channel_id=1, source_target_pairs={{0,3},{1,0},{2,1},{3,2},{4,7},{5,4},{6,5},{7,6},{8,11},{9,8},{10,9... | collective-permute-start | bytes 393224 | tf_op jit(solution)/shard_map/ppermute | solution.py:166
  96.2 5.6 %collective-permute-start.8 = (bf16[128,512]{1,0:T(8,128)(2,1)S(1)}, bf16[128,512]{1,0:T(8,128)(2,1)S(1)}, u32[]{:S(2)}, u32[]{:S(2)}) collective-permute-start(bf16[128,512]{1,0:T(8,128)(2,1)S(1)} %get-tuple-element.51), channel_id=1, source_target_pairs={{0,1},{1,2},{2,3},{3,0},{4,5},{5,6},{6,7},{7,4},{8,9},{9,10},{10,1... | collective-permute-start | bytes 393224 | tf_op jit(solution)/shard_map/ppermute | solution.py:166
  102.5 4.8 %collective-permute-start.11 = (bf16[512,128]{1,0:T(8,128)(2,1)S(1)}, bf16[512,128]{1,0:T(8,128)(2,1)}, u32[]{:S(2)}, u32[]{:S(2)}) collective-permute-start(bf16[512,128]{1,0:T(8,128)(2,1)S(1)} %get-tuple-element.64.refs_0_), channel_id=1, source_target_pairs={{0,3},{1,0},{2,1},{3,2},{4,7},{5,4},{6,5},{7,6},{8,11},{9,8},{10,9... | collective-permute-start | bytes 393224 | tf_op jit(solution)/shard_map/ppermute | solution.py:166
  104.8 5.4 %collective-permute-start.10 = (bf16[512,128]{1,0:T(8,128)(2,1)S(1)}, bf16[512,128]{1,0:T(8,128)(2,1)}, u32[]{:S(2)}, u32[]{:S(2)}) collective-permute-start(bf16[512,128]{1,0:T(8,128)(2,1)S(1)} %get-tuple-element.64.refs_0_), channel_id=1, source_target_pairs={{0,2},{1,3},{2,0},{3,1},{4,6},{5,7},{6,4},{7,5},{8,10},{9,11},{10,... | collective-permute-start | bytes 393224 | tf_op jit(solution)/shard_map/ppermute | solution.py:166
  106.3 6.1 %collective-permute-start.9 = (bf16[512,128]{1,0:T(8,128)(2,1)S(1)}, bf16[512,128]{1,0:T(8,128)(2,1)}, u32[]{:S(2)}, u32[]{:S(2)}) collective-permute-start(bf16[512,128]{1,0:T(8,128)(2,1)S(1)} %get-tuple-element.64.refs_0_), channel_id=1, source_target_pairs={{0,1},{1,2},{2,3},{3,0},{4,5},{5,6},{6,7},{7,4},{8,9},{9,10},{10,1... | collective-permute-start | bytes 393224 | tf_op jit(solution)/shard_map/ppermute | solution.py:166
  115.8 7.2 %collective-permute-start.12 = (bf16[4,128,1664]{2,1,0:T(8,128)(2,1)}, bf16[4,128,1664]{2,1,0:T(8,128)(2,1)}, u32[]{:S(2)}, u32[]{:S(2)}) collective-permute-start(bf16[4,128,1664]{2,1,0:T(8,128)(2,1)} %cross.3), channel_id=1, source_target_pairs={{0,4},{4,0},{1,5},{5,1},{2,6},{6,2},{3,7},{7,3},{8,12},{12,8},{9,1... | collective-permute-start | bytes 5111816 | tf_op jit(solution)/shard_map/ppermute | solution.py:170
  122.6 4.3 %collective-permute-start.13 = (bf16[4,128,1664]{2,1,0:T(8,128)(2,1)}, bf16[4,128,1664]{2,1,0:T(8,128)(2,1)S(1)}, u32[]{:S(2)}, u32[]{:S(2)}) collective-permute-start(bf16[4,128,1664]{2,1,0:T(8,128)(2,1)} %cross.2), channel_id=1, source_target_pairs={{0,4},{4,0},{1,5},{5,1},{2,6},{6,2},{3,7},{7,3},{8,12},{12,8},{9,1... | collective-permute-start | bytes 5111816 | tf_op jit(solution)/shard_map/ppermute | solution.py:170
  130.7 12.6 %collective-permute-start.14 = (bf16[128,1664]{1,0:T(8,128)(2,1)}, bf16[128,1664]{1,0:T(8,128)(2,1)S(1)}, u32[]{:S(2)}, u32[]{:S(2)}) collective-permute-start(bf16[128,1664]{1,0:T(8,128)(2,1)} %get-tuple-element.58), channel_id=1, source_target_pairs={{0,8},{8,16},{16,24},{24,0},{1,9},{9,17},{17,25},{25,1},{2,10},{10... | collective-permute-start | bytes 1277960 | tf_op jit(solution)/shard_map/ppermute | solution.py:166
  132.0 23.2 %collective-permute-start.15 = (bf16[128,1664]{1,0:T(8,128)(2,1)}, bf16[128,1664]{1,0:T(8,128)(2,1)}, u32[]{:S(2)}, u32[]{:S(2)}) collective-permute-start(bf16[128,1664]{1,0:T(8,128)(2,1)} %get-tuple-element.60), channel_id=1, source_target_pairs={{0,16},{8,24},{16,0},{24,8},{1,17},{9,25},{17,1},{25,9},{2,18},{10... | collective-permute-start | bytes 1277960 | tf_op jit(solution)/shard_map/ppermute | solution.py:166
  134.4 20.7 %collective-permute-start.16 = (bf16[128,1664]{1,0:T(8,128)(2,1)}, bf16[128,1664]{1,0:T(8,128)(2,1)}, u32[]{:S(2)}, u32[]{:S(2)}) collective-permute-start(bf16[128,1664]{1,0:T(8,128)(2,1)} %get-tuple-element.62), channel_id=1, source_target_pairs={{0,24},{8,0},{16,8},{24,16},{1,25},{9,1},{17,9},{25,17},{2,26},{10... | collective-permute-start | bytes 1277960 | tf_op jit(solution)/shard_map/ppermute | solution.py:166
  135.5 25.9 %collective-permute-start.20 = (bf16[128,1664]{1,0:T(8,128)(2,1)}, bf16[128,1664]{1,0:T(8,128)(2,1)}, u32[]{:S(2)}, u32[]{:S(2)}) collective-permute-start(bf16[128,1664]{1,0:T(8,128)(2,1)} %get-tuple-element.70), channel_id=1, source_target_pairs={{0,32},{32,64},{64,96},{96,0},{1,33},{33,65},{65,97},{97,1},{2,34}... | collective-permute-start | bytes 1277960 | tf_op jit(solution)/shard_map/ppermute | solution.py:166
  136.8 25.7 %collective-permute-start.21 = (bf16[128,1664]{1,0:T(8,128)(2,1)}, bf16[128,1664]{1,0:T(8,128)(2,1)}, u32[]{:S(2)}, u32[]{:S(2)}) collective-permute-start(bf16[128,1664]{1,0:T(8,128)(2,1)} %get-tuple-element.71), channel_id=1, source_target_pairs={{0,64},{32,96},{64,0},{96,32},{1,65},{33,97},{65,1},{97,33},{2,66}... | collective-permute-start | bytes 1277960 | tf_op jit(solution)/shard_map/ppermute | solution.py:166
  143.2 0.8 copy-start.4
  144.0 18.5 %collective-permute-start.22 = (bf16[128,1664]{1,0:T(8,128)(2,1)}, bf16[128,1664]{1,0:T(8,128)(2,1)}, u32[]{:S(2)}, u32[]{:S(2)}) collective-permute-start(bf16[128,1664]{1,0:T(8,128)(2,1)} %get-tuple-element.72), channel_id=1, source_target_pairs={{0,96},{32,0},{64,32},{96,64},{1,97},{33,1},{65,33},{97,65},{2,98}... | collective-permute-start | bytes 1277960 | tf_op jit(solution)/shard_map/ppermute | solution.py:166
  148.5 0.8 copy-start.2
  149.3 20.4 %all-to-all-start = ((bf16[32,16,512]{2,1,0:T(8,128)(2,1)}), bf16[32,16,512]{2,1,0:T(8,128)(2,1)}, u32[]{:S(2)}, u32[]{:S(2)}) async-start(bf16[32,16,512]{2,1,0:T(8,128)(2,1)} %bitcast.20), calls=%async_computation | async-start | bytes 1048576 | tf_op jit(solution)/shard_map/all_to_all | solution.py:561
  155.1 72.9 %all-gather.5.cloned.1.call-start = ((), (), s32[]{:S(2)}) async-start(), calls=%async_computation.3 | async-start | bytes 7028736 | tf_op jit(solution)/shard_map/all_gather | solution.py:573
  157.5 11.1 %collective-permute-start.17 = (bf16[32,1664]{1,0:T(8,128)(2,1)}, bf16[32,1664]{1,0:T(8,128)(2,1)}, u32[]{:S(2)}, u32[]{:S(2)}) collective-permute-start(bf16[32,1664]{1,0:T(8,128)(2,1)} %get-tuple-element.67), channel_id=1, source_target_pairs={{0,32},{32,64},{64,96},{96,0},{1,33},{33,65},{65,97},{97,1},{2,34}... | collective-permute-start | bytes 319496 | tf_op jit(solution)/shard_map/ppermute | solution.py:166
  158.9 11.1 %collective-permute-start.18 = (bf16[32,1664]{1,0:T(8,128)(2,1)}, bf16[32,1664]{1,0:T(8,128)(2,1)}, u32[]{:S(2)}, u32[]{:S(2)}) collective-permute-start(bf16[32,1664]{1,0:T(8,128)(2,1)} %get-tuple-element.68), channel_id=1, source_target_pairs={{0,64},{32,96},{64,0},{96,32},{1,65},{33,97},{65,1},{97,33},{2,66}... | collective-permute-start | bytes 319496 | tf_op jit(solution)/shard_map/ppermute | solution.py:166
  161.4 8.6 %collective-permute-start.19 = (bf16[32,1664]{1,0:T(8,128)(2,1)}, bf16[32,1664]{1,0:T(8,128)(2,1)}, u32[]{:S(2)}, u32[]{:S(2)}) collective-permute-start(bf16[32,1664]{1,0:T(8,128)(2,1)} %get-tuple-element.69), channel_id=1, source_target_pairs={{0,96},{32,0},{64,32},{96,64},{1,97},{33,1},{65,33},{97,65},{2,98}... | collective-permute-start | bytes 319496 | tf_op jit(solution)/shard_map/ppermute | solution.py:166
  164.8 5.4 %collective-permute-start.23 = (bf16[32,1664]{1,0:T(8,128)(2,1)}, bf16[32,1664]{1,0:T(8,128)(2,1)}, u32[]{:S(2)}, u32[]{:S(2)}) collective-permute-start(bf16[32,1664]{1,0:T(8,128)(2,1)} %get-tuple-element.74), channel_id=1, source_target_pairs={{0,8},{8,16},{16,24},{24,0},{1,9},{9,17},{17,25},{25,1},{2,10},{10... | collective-permute-start | bytes 319496 | tf_op jit(solution)/shard_map/ppermute | solution.py:166
  166.1 6.5 %collective-permute-start.24 = (bf16[32,1664]{1,0:T(8,128)(2,1)}, bf16[32,1664]{1,0:T(8,128)(2,1)}, u32[]{:S(2)}, u32[]{:S(2)}) collective-permute-start(bf16[32,1664]{1,0:T(8,128)(2,1)} %get-tuple-element.75), channel_id=1, source_target_pairs={{0,16},{8,24},{16,0},{24,8},{1,17},{9,25},{17,1},{25,9},{2,18},{10... | collective-permute-start | bytes 319496 | tf_op jit(solution)/shard_map/ppermute | solution.py:166
  168.5 5.2 %collective-permute-start.25 = (bf16[32,1664]{1,0:T(8,128)(2,1)}, bf16[32,1664]{1,0:T(8,128)(2,1)}, u32[]{:S(2)}, u32[]{:S(2)}) collective-permute-start(bf16[32,1664]{1,0:T(8,128)(2,1)} %get-tuple-element.76), channel_id=1, source_target_pairs={{0,24},{8,0},{16,8},{24,16},{1,25},{9,1},{17,9},{25,17},{2,26},{10... | collective-permute-start | bytes 319496 | tf_op jit(solution)/shard_map/ppermute | solution.py:166
  176.9 0.8 copy-start.3
  177.7 20.1 %all-to-all-start.1 = ((bf16[32,16,512]{2,1,0:T(8,128)(2,1)}), bf16[32,16,512]{2,1,0:T(8,128)(2,1)}, u32[]{:S(2)}, u32[]{:S(2)}) async-start(bf16[32,16,512]{2,1,0:T(8,128)(2,1)} %copy-done.3), calls=%async_computation.1 | async-start | bytes 1048576 | tf_op jit(solution)/shard_map/all_to_all | solution.py:572
  231.5 10.6 %collective-permute-start.28 = (f32[16,128]{1,0:T(8,128)S(1)}, f32[16,128]{1,0:T(8,128)S(1)}, u32[]{:S(2)}, u32[]{:S(2)}) collective-permute-start(f32[16,128]{1,0:T(8,128)S(1)} %get-tuple-element.84), channel_id=1, source_target_pairs={{0,3},{1,0},{2,1},{3,2},{4,7},{5,4},{6,5},{7,6},{8,11},{9,8},{10,9... | collective-permute-start | bytes 24584 | tf_op jit(solution)/shard_map/ppermute | solution.py:166
  234.2 7.9 %collective-permute-start.27 = (f32[16,128]{1,0:T(8,128)S(1)}, f32[16,128]{1,0:T(8,128)S(1)}, u32[]{:S(2)}, u32[]{:S(2)}) collective-permute-start(f32[16,128]{1,0:T(8,128)S(1)} %get-tuple-element.84), channel_id=1, source_target_pairs={{0,2},{1,3},{2,0},{3,1},{4,6},{5,7},{6,4},{7,5},{8,10},{9,11},{10,... | collective-permute-start | bytes 24584 | tf_op jit(solution)/shard_map/ppermute | solution.py:166
  234.6 7.5 %collective-permute-start.26 = (f32[16,128]{1,0:T(8,128)S(1)}, f32[16,128]{1,0:T(8,128)S(1)}, u32[]{:S(2)}, u32[]{:S(2)}) collective-permute-start(f32[16,128]{1,0:T(8,128)S(1)} %get-tuple-element.84), channel_id=1, source_target_pairs={{0,1},{1,2},{2,3},{3,0},{4,5},{5,6},{6,7},{7,4},{8,9},{9,10},{10,1... | collective-permute-start | bytes 24584 | tf_op jit(solution)/shard_map/ppermute | solution.py:166
Sparse Core Ops, SparseCore 0:
  10.2 53.4 all-gather.2
  175.9 52.0 all-gather.4

commit v4 on v2

--- a/solution.py
+++ b/solution.py
@@ -250,7 +250,11 @@
         total += lax.dot_general(
             factor[...], factor[...], (((1,), (1,)), ((), ())), preferred_element_type=F32
         )
-    refs[4][...] = total.astype(HALF)
+    out, held, sem = refs[4:]
+    held[...] = total.astype(HALF)
+    store = pltpu.make_async_copy(held, out, sem)
+    store.start()
+    store.wait()
 
 
 def gram_of(factors):
@@ -259,7 +263,9 @@
         gram_kernel,
         "gram",
         factors,
-        jax.ShapeDtypeStruct((ranks, ranks), HALF),
+        pltpu.HBM((ranks, ranks), HALF),
+        out_specs=HBM,
+        scratch=[pltpu.VMEM((ranks, ranks), HALF), pltpu.SemaphoreType.DMA],
         flops=8 * rows * ranks * ranks,
     )
 
@@ -336,40 +342,41 @@
 
 
 def fold_kernel(at_ref, *refs):
-    terms, outs, (taken, held, in_sems, out_sems) = refs[:4], refs[4:8], refs[8:]
-    loads = [pltpu.make_async_copy(terms[i], taken.at[i], in_sems.at[i]) for i in range(4)]
-    stores = [pltpu.make_async_copy(held.at[i], outs[i], out_sems.at[i]) for i in range(4)]
+    terms, outs, (taken, held, in_sems, out_sems) = refs[:8], refs[8:16], refs[16:]
+    loads = [pltpu.make_async_copy(terms[i], taken.at[i], in_sems.at[i]) for i in range(8)]
+    stores = [pltpu.make_async_copy(held.at[i], outs[i], out_sems.at[i]) for i in range(8)]
     for load in loads:
         load.start()
-    for load in loads:
-        load.wait()
-    for turn in range(4):
-        at = lax.rem(at_ref[0] + turn, 4) * EIGHTH
-        here = pl.ds(pl.multiple_of(at, EIGHTH), EIGHTH)
-        total = taken[0, here, :].astype(F32)
-        for i in range(1, 4):
-            total += taken[i, here, :].astype(F32)
-        held[turn] = total.astype(HALF)
-        stores[turn].start()
+    for side in range(2):
+        for load in loads[4 * side:4 * side + 4]:
+            load.wait()
+        for turn in range(4):
+            at = lax.rem(at_ref[side] + turn, 4) * EIGHTH
+            here = pl.ds(pl.multiple_of(at, EIGHTH), EIGHTH)
+            total = taken[4 * side, here, :].astype(F32)
+            for i in range(1, 4):
+                total += taken[4 * side + i, here, :].astype(F32)
+            held[4 * side + turn] = total.astype(HALF)
+            stores[4 * side + turn].start()
     for store in stores:
         store.wait()
 
 
-def fold(terms, at):
+def fold(first, second, at_first, at_second):
     return call(
         fold_kernel,
         "fold",
-        [jnp.full((1,), at, jnp.int32), *in_hbm(terms)],
-        [pltpu.HBM((EIGHTH, TILE), HALF)] * 4,
-        in_specs=[SMEM] + [HBM] * 4,
-        out_specs=[HBM] * 4,
+        [jnp.stack([at_first, at_second]).astype(jnp.int32), *in_hbm([*first, *second])],
+        [pltpu.HBM((EIGHTH, TILE), HALF)] * 8,
+        in_specs=[SMEM] + [HBM] * 8,
+        out_specs=[HBM] * 8,
         scratch=[
-            pltpu.VMEM((4, QUARTER, TILE), HALF),
-            pltpu.VMEM((4, EIGHTH, TILE), HALF),
-            pltpu.SemaphoreType.DMA((4,)),
-            pltpu.SemaphoreType.DMA((4,)),
+            pltpu.VMEM((8, QUARTER, TILE), HALF),
+            pltpu.VMEM((8, EIGHTH, TILE), HALF),
+            pltpu.SemaphoreType.DMA((8,)),
+            pltpu.SemaphoreType.DMA((8,)),
         ],
-        flops=4 * QUARTER * TILE,
+        flops=8 * QUARTER * TILE,
     )
 
 
@@ -533,10 +540,10 @@
     gram_pieces = lax.all_to_all(gram_part, row, split_axis=0, concat_axis=0, tiled=True)
     copies = spread(gram_pieces.reshape(rows, ranks_dev, ranks))
 
-    first = list(fold(first, at_y))
+    pieces = fold(first, second, at_y, at_x)
+    first, second = list(pieces[:4]), list(pieces[4:])
     for turn in (2, 1, 3):
         first[turn] = ring(first[turn], "y", turn)
-    second = list(fold(second, at_x))
     gram = lax.all_to_all(copies.reshape(ranks, ranks), row, split_axis=0, concat_axis=0, tiled=True)
     for turn in (2, 1, 3):
         second[turn] = ring(second[turn], "x", turn)

time: 250 us -> 251 us (level)
  waiting for transfers between devices: 80.9 us -> 83.9 us
    ppermute x27, waiting for transfers between devices: 54 us -> 56.7 us  [ring(): lax.ppermute(value, axis, [(i, (i + shift) % size) for i in range(size)])]
    unnamed x22 -> x18, local copies, waits for them, and re-layouts: 8.54 us -> 6.96 us
    pallas_call x14 -> x13, Pallas kernels: 40.7 us -> 40.3 us  [call(): pl.pallas_call(kernel, in_specs=in_specs or [VMEM] * len(operands), out_s...]
  transfers between devices with their start and end apart: 33 -> 33, of which waited for: 16 -> 18; matrix products, arithmetic and copies ran while one was open for 8% -> 8% of each run, Pallas kernels for 19% -> 19%
where the time goes in v4:
time: 251 us; the launch traced here: 250 us
  waiting for transfers between devices  83.9 us (33%)
  Pallas kernels  64.9 us (26%)
  starting transfers between devices  60.3 us (24%)
  other arithmetic  19.9 us (8%)
  between operations  14.3 us (6%)
  local copies, waits for them, and re-layouts  6.96 us (3%)
    ppermute x27, waiting for transfers between devices, ring(): lax.ppermute(value, axis, [(i, (i + shift) % size) for i in range(size)])  56.7 us
    ppermute x27, starting transfers between devices, ring(): lax.ppermute(value, axis, [(i, (i + shift) % size) for i in range(size)])  43.3 us
    pallas_call x13, Pallas kernels, call(): pl.pallas_call(kernel, in_specs=in_specs or [VMEM] * len(operands), out_s...  40.3 us
    pallas_call x1, Pallas kernels, factorize(): pl.pallas_call(factor_kernel, out_shape=[pltpu.HBM(*out) for out in outs]...  24.6 us
    convert_element_type x8, other arithmetic, per_device(): last = (pair[0] + pair[1]).astype(HALF)  18.6 us
    all_to_all x1, waiting for transfers between devices, per_device(): lax.all_to_all(copies.reshape(ranks, ranks), row, split_axis=0, concat_ax...  13.8 us
    all_gather x1, waiting for transfers between devices, per_device(): right_all = lax.all_gather(right_factor, row, axis=0, tiled=True)  7.69 us
    all_to_all x1, starting transfers between devices, per_device(): lax.all_to_all(copies.reshape(ranks, ranks), row, split_axis=0, concat_ax...  7.39 us
  transfers between devices with their start and end apart: 33, of which 18 were waited for; matrix products, arithmetic and copies ran while one was open for 8% of the time, Pallas kernels for 19%

profile of v4, /device:TPU:1, one launch (start us, length us, event | category | flops | bytes accessed | tf_op | source)
XLA Modules:
  0.0 250.3 jit_solution(12427167048232751546)
XLA Ops:
  7.9 2.5 %add_convert_fusion.7 = bf16[128,3328]{1,0:T(8,128)(2,1)} fusion(bf16[128,26624]{1,0:T(8,128)(2,1)} %param.4, s32[]{:T(128)S(6)} %select_n.32, bf16[128,26624]{1,0:T(8,128)(2,1)} %param.3), kind=kLoop, calls=%fused_computation.7 | loop fusion | flops 1703936 | bytes 2555908 | tf_op jit(solution)/shard_map/convert_element_type | solution.py:521
  10.4 4.4 %collective-permute-start.4 = (bf16[128,3328]{1,0:T(8,128)(2,1)}, bf16[128,3328]{1,0:T(8,128)(2,1)S(1)}, u32[]{:S(2)}, u32[]{:S(2)}) collective-permute-start(bf16[128,3328]{1,0:T(8,128)(2,1)} %add_convert_fusion.7), channel_id=1, source_target_pairs={{0,2},{1,3},{2,0},{3,1},{4,6},{5,7},{6,4},{7,5},{8,10},{9,11},{10,... | collective-permute-start | bytes 2555912 | tf_op jit(solution)/shard_map/ppermute | solution.py:166
  14.9 2.6 %add_convert_fusion.6 = bf16[128,3328]{1,0:T(8,128)(2,1)} fusion(bf16[128,26624]{1,0:T(8,128)(2,1)} %param.4, s32[]{:T(128)S(6)} %select_n.33, bf16[128,26624]{1,0:T(8,128)(2,1)} %param.3), kind=kLoop, calls=%fused_computation.6 | loop fusion | flops 1703936 | bytes 2555908 | tf_op jit(solution)/shard_map/convert_element_type | solution.py:521
  18.2 2.5 %add_convert_fusion.5 = bf16[128,3328]{1,0:T(8,128)(2,1)} fusion(bf16[128,26624]{1,0:T(8,128)(2,1)} %param.4, s32[]{:T(128)S(6)} %select_n.34, bf16[128,26624]{1,0:T(8,128)(2,1)} %param.3), kind=kLoop, calls=%fused_computation.5 | loop fusion | flops 1703936 | bytes 2555908 | tf_op jit(solution)/shard_map/convert_element_type | solution.py:521
  20.7 1.9 collective-permute-start.5
  22.6 1.7 add_convert_fusion.4.refs_0_.refs_4_
  24.3 2.5 %add_convert_fusion.3 = bf16[128,3328]{1,0:T(8,128)(2,1)} fusion(bf16[128,26624]{1,0:T(8,128)(2,1)} %param.4, s32[]{:T(128)S(6)} %select_n.36, bf16[128,26624]{1,0:T(8,128)(2,1)} %param.3), kind=kLoop, calls=%fused_computation.3 | loop fusion | flops 1703936 | bytes 2555908 | tf_op jit(solution)/shard_map/convert_element_type | solution.py:521
  26.9 2.5 %add_convert_fusion.2 = bf16[128,3328]{1,0:T(8,128)(2,1)} fusion(bf16[128,26624]{1,0:T(8,128)(2,1)} %param.4, s32[]{:T(128)S(6)} %select_n.37, bf16[128,26624]{1,0:T(8,128)(2,1)} %param.3), kind=kLoop, calls=%fused_computation.2 | loop fusion | flops 1703936 | bytes 2555908 | tf_op jit(solution)/shard_map/convert_element_type | solution.py:521
  29.4 2.5 %add_convert_fusion.1 = bf16[128,3328]{1,0:T(8,128)(2,1)} fusion(bf16[128,26624]{1,0:T(8,128)(2,1)} %param.4, s32[]{:T(128)S(6)} %select_n.38, bf16[128,26624]{1,0:T(8,128)(2,1)} %param.3), kind=kLoop, calls=%fused_computation.1 | loop fusion | flops 1703936 | bytes 2555908 | tf_op jit(solution)/shard_map/convert_element_type | solution.py:521
  31.9 2.7 %collective-permute-start.2 = (bf16[128,3328]{1,0:T(8,128)(2,1)}, bf16[128,3328]{1,0:T(8,128)(2,1)}, u32[]{:S(2)}, u32[]{:S(2)}) collective-permute-start(bf16[128,3328]{1,0:T(8,128)(2,1)} %add_convert_fusion.1), channel_id=1, source_target_pairs={{0,3},{1,0},{2,1},{3,2},{4,7},{5,4},{6,5},{7,6},{8,11},{9,8},{10,9... | collective-permute-start | bytes 2555912 | tf_op jit(solution)/shard_map/ppermute | solution.py:166
  34.6 18.0 %collective-permute-done.5.refs_3_.refs_7_ = bf16[128,3328]{1,0:T(8,128)(2,1)S(1)} collective-permute-done((bf16[128,3328]{1,0:T(8,128)(2,1)}, bf16[128,3328]{1,0:T(8,128)(2,1)S(1)}, u32[]{:S(2)}, u32[]{:S(2)}) %collective-permute-start.5) | collective-permute-done | bytes 852000 | tf_op jit(solution)/shard_map/ppermute | solution.py:166
  54.4 1.7 add_convert_fusion.refs_0_.refs_4_
  56.1 7.7 %all-gather.3.cloned.1.call-done.refs_4_ = bf16[512,6656]{1,0:T(8,128)(2,1)} async-done(((bf16[16,6656]{1,0:T(8,128)(2,1)}), bf16[512,6656]{1,0:T(8,128)(2,1)}) %all-gather.3.cloned.1.call-update) | async-done | bytes 6815760 | tf_op jit(solution)/shard_map/all_gather | solution.py:512
  63.8 2.9 %copy-done = bf16[512,6656]{1,0:T(8,128)(2,1)S(1)} copy-done((bf16[512,6656]{1,0:T(8,128)(2,1)S(1)}, bf16[512,6656]{1,0:T(8,128)(2,1)}, u32[]{:S(2)}) %copy-start) | copy-done | bytes 6815768
  67.9 2.1 project.2.refs_5_
  70.0 1.4 collective-permute-done.2.refs_3_.refs_7_
  71.8 16.9 %collective-permute-done.1.refs_2_.refs_6_ = bf16[128,3328]{1,0:T(8,128)(2,1)} collective-permute-done((bf16[128,3328]{1,0:T(8,128)(2,1)}, bf16[128,3328]{1,0:T(8,128)(2,1)}, u32[]{:S(2)}, u32[]{:S(2)}) %collective-permute-start.1) | collective-permute-done | bytes 852000 | tf_op jit(solution)/shard_map/ppermute | solution.py:166
  88.7 3.7 %project.3 = (bf16[128,512]{1,0:T(8,128)(2,1)S(1)}, bf16[128,512]{1,0:T(8,128)(2,1)S(1)}, bf16[128,512]{1,0:T(8,128)(2,1)S(1)}, bf16[128,512]{1,0:T(8,128)(2,1)S(1)}) custom-call(bf16[128,3328]{1,0:T(8,128)(2,1)S(1)} %add_convert_fusion.refs_0_.refs_4_, bf16[128,3328]{1,0:T(8,128)(2,1)} %collective-permute-done.refs_1_.refs_5_, ...), custom_call_target="tpu_custom_call" | custom-call | flops 1744830464 | bytes 11796480 | tf_op jit(solution)/shard_map/project/pallas_call | solution.py:180
  92.4 2.7 %collective-permute-start.6 = (bf16[128,512]{1,0:T(8,128)(2,1)S(1)}, bf16[128,512]{1,0:T(8,128)(2,1)S(1)}, u32[]{:S(2)}, u32[]{:S(2)}) collective-permute-start(bf16[128,512]{1,0:T(8,128)(2,1)S(1)} %get-tuple-element.56), channel_id=1, source_target_pairs={{0,2},{1,3},{2,0},{3,1},{4,6},{5,7},{6,4},{7,5},{8,10},{9,11},{10,... | collective-permute-start | bytes 393224 | tf_op jit(solution)/shard_map/ppermute | solution.py:166
  97.8 2.9 %collective-permute-done.7.refs_2_ = bf16[128,512]{1,0:T(8,128)(2,1)S(1)} collective-permute-done((bf16[128,512]{1,0:T(8,128)(2,1)S(1)}, bf16[128,512]{1,0:T(8,128)(2,1)S(1)}, u32[]{:S(2)}, u32[]{:S(2)}) %collective-permute-start.7) | collective-permute-done | bytes 131104 | tf_op jit(solution)/shard_map/ppermute | solution.py:166
  102.0 3.0 %collective-permute-start.11 = (bf16[512,128]{1,0:T(8,128)(2,1)S(1)}, bf16[512,128]{1,0:T(8,128)(2,1)}, u32[]{:S(2)}, u32[]{:S(2)}) collective-permute-start(bf16[512,128]{1,0:T(8,128)(2,1)S(1)} %get-tuple-element.66.refs_0_), channel_id=1, source_target_pairs={{0,3},{1,0},{2,1},{3,2},{4,7},{5,4},{6,5},{7,6},{8,11},{9,8},{10,9... | collective-permute-start | bytes 393224 | tf_op jit(solution)/shard_map/ppermute | solution.py:166
  105.7 4.7 %collective-permute-done.11.refs_3_ = bf16[512,128]{1,0:T(8,128)(2,1)} collective-permute-done((bf16[512,128]{1,0:T(8,128)(2,1)S(1)}, bf16[512,128]{1,0:T(8,128)(2,1)}, u32[]{:S(2)}, u32[]{:S(2)}) %collective-permute-start.11) | collective-permute-done | bytes 131104 | tf_op jit(solution)/shard_map/ppermute | solution.py:166
  110.5 2.5 collective-permute-done.9.refs_1_
  114.2 3.0 %cross.3 = bf16[4,128,1664]{2,1,0:T(8,128)(2,1)} custom-call(s32[2]{0:T(128)S(1)} %pad_add_fusion.4.at_ref, bf16[512,128]{1,0:T(8,128)(2,1)S(1)} %get-tuple-element.66.refs_0_, bf16[512,128]{1,0:T(8,128)(2,1)} %collective-permute-done.9.refs_1_, bf16[512,128]{1,0:T(8,128)(2,1)} %collective-permute-done.10.refs_2_, ...), custom_call_target="tpu_custom_call" | custom-call | flops 872415232 | bytes 5636104 | tf_op jit(solution)/shard_map/cross/pallas_call | solution.py:180
  117.2 2.1 collective-permute-start.12
  119.4 4.0 %cross.2 = bf16[4,128,1664]{2,1,0:T(8,128)(2,1)} custom-call(s32[2]{0:T(128)S(1)} %pad_add_fusion.3.at_ref, bf16[512,128]{1,0:T(8,128)(2,1)S(1)} %get-tuple-element.66.refs_0_, bf16[512,128]{1,0:T(8,128)(2,1)} %collective-permute-done.9.refs_1_, bf16[512,128]{1,0:T(8,128)(2,1)} %collective-permute-done.10.refs_2_, ...), custom_call_target="tpu_custom_call" | custom-call | flops 872415232 | bytes 5636104 | tf_op jit(solution)/shard_map/cross/pallas_call | solution.py:180
  123.8 3.6 %cross_add.2 = (bf16[128,1664]{1,0:T(8,128)(2,1)}, bf16[128,1664]{1,0:T(8,128)(2,1)}, bf16[128,1664]{1,0:T(8,128)(2,1)}, bf16[128,1664]{1,0:T(8,128)(2,1)}) custom-call(s32[2]{0:T(128)S(1)} %pad_add_fusion.at_ref, bf16[512,128]{1,0:T(8,128)(2,1)S(1)} %get-tuple-element.66.refs_0_, bf16[512,128]{1,0:T(8,128)(2,1)} %collective-permute-done.9.refs_1_, ...), custom_call_target="tpu_custom_call" | custom-call | flops 872415232 | bytes 7340040 | tf_op jit(solution)/shard_map/cross_add/pallas_call | solution.py:180
  127.5 3.8 %cross_add.3 = (bf16[128,1664]{1,0:T(8,128)(2,1)}, bf16[128,1664]{1,0:T(8,128)(2,1)}, bf16[128,1664]{1,0:T(8,128)(2,1)}, bf16[128,1664]{1,0:T(8,128)(2,1)}) custom-call(s32[2]{0:T(128)S(1)} %pad_add_fusion.1.at_ref, bf16[512,128]{1,0:T(8,128)(2,1)S(1)} %get-tuple-element.66.refs_0_, bf16[512,128]{1,0:T(8,128)(2,1)} %collective-permute-done.9.refs_1_, ...), custom_call_target="tpu_custom_call" | custom-call | flops 872415232 | bytes 7340040 | tf_op jit(solution)/shard_map/cross_add/pallas_call | solution.py:180
  131.4 2.8 %collective-permute-start.14 = (bf16[128,1664]{1,0:T(8,128)(2,1)S(1)}, bf16[128,1664]{1,0:T(8,128)(2,1)}, u32[]{:S(2)}, u32[]{:S(2)}) collective-permute-start(bf16[128,1664]{1,0:T(8,128)(2,1)S(1)} %copy-done.8), channel_id=1, source_target_pairs={{0,16},{8,24},{16,0},{24,8},{1,17},{9,25},{17,1},{25,9},{2,18},{10... | collective-permute-start | bytes 1277960 | tf_op jit(solution)/shard_map/ppermute | solution.py:166
  134.5 2.3 collective-permute-start.16
  138.2 2.6 %collective-permute-start.18 = (bf16[128,1664]{1,0:T(8,128)(2,1)}, bf16[128,1664]{1,0:T(8,128)(2,1)}, u32[]{:S(2)}, u32[]{:S(2)}) collective-permute-start(bf16[128,1664]{1,0:T(8,128)(2,1)} %get-tuple-element.72), channel_id=1, source_target_pairs={{0,64},{32,96},{64,0},{96,32},{1,65},{33,97},{65,1},{97,33},{2,66}... | collective-permute-start | bytes 1277960 | tf_op jit(solution)/shard_map/ppermute | solution.py:166
  140.8 3.3 %collective-permute-done.14.refs_2_ = bf16[128,1664]{1,0:T(8,128)(2,1)} collective-permute-done((bf16[128,1664]{1,0:T(8,128)(2,1)S(1)}, bf16[128,1664]{1,0:T(8,128)(2,1)}, u32[]{:S(2)}, u32[]{:S(2)}) %collective-permute-start.14) | collective-permute-done | bytes 426016 | tf_op jit(solution)/shard_map/ppermute | solution.py:166
  144.1 2.7 %collective-permute-start.19 = (bf16[128,1664]{1,0:T(8,128)(2,1)}, bf16[128,1664]{1,0:T(8,128)(2,1)}, u32[]{:S(2)}, u32[]{:S(2)}) collective-permute-start(bf16[128,1664]{1,0:T(8,128)(2,1)} %get-tuple-element.73), channel_id=1, source_target_pairs={{0,96},{32,0},{64,32},{96,64},{1,97},{33,1},{65,33},{97,65},{2,98}... | collective-permute-start | bytes 1277960 | tf_op jit(solution)/shard_map/ppermute | solution.py:166
  146.8 2.5 %gram.1 = bf16[512,512]{1,0:T(8,128)(2,1)} custom-call(bf16[512,128]{1,0:T(8,128)(2,1)S(1)} %get-tuple-element.66.refs_0_, bf16[512,128]{1,0:T(8,128)(2,1)} %collective-permute-done.9.refs_1_, bf16[512,128]{1,0:T(8,128)(2,1)} %collective-permute-done.10.refs_2_, bf16[512,128]{1,0:T(8,128)(2,1)} %collective-permute-done.11.refs_3_), custom_call_target="tpu_custom_call" | custom-call | flops 268435456 | bytes 1048576 | tf_op jit(solution)/shard_map/gram/pallas_call | solution.py:180
  149.4 7.1 %all-to-all-start = ((bf16[32,16,512]{2,1,0:T(8,128)(2,1)}), bf16[32,16,512]{2,1,0:T(8,128)(2,1)}, u32[]{:S(2)}, u32[]{:S(2)}) async-start(bf16[32,16,512]{2,1,0:T(8,128)(2,1)} %bitcast.11), calls=%async_computation | async-start | bytes 1048576 | tf_op jit(solution)/shard_map/all_to_all | solution.py:540
  156.6 2.2 collective-permute-done.18.refs_6_
  158.8 3.4 %fold.1 = (bf16[32,1664]{1,0:T(8,128)(2,1)}, bf16[32,1664]{1,0:T(8,128)(2,1)}, bf16[32,1664]{1,0:T(8,128)(2,1)}, bf16[32,1664]{1,0:T(8,128)(2,1)}, bf16[32,1664]...) custom-call(s32[2]{0:T(128)S(1)} %pad_add_fusion.2.at_ref, ...), custom_call_target="tpu_custom_call" | custom-call | flops 1703936 | bytes 4259848 | tf_op jit(solution)/shard_map/fold/pallas_call | solution.py:180
  162.3 3.7 %collective-permute-start.20 = (bf16[32,1664]{1,0:T(8,128)(2,1)}, bf16[32,1664]{1,0:T(8,128)(2,1)}, u32[]{:S(2)}, u32[]{:S(2)}) collective-permute-start(bf16[32,1664]{1,0:T(8,128)(2,1)} %get-tuple-element.76), channel_id=1, source_target_pairs={{0,32},{32,64},{64,96},{96,0},{1,33},{33,65},{65,97},{97,1},{2,34}... | collective-permute-start | bytes 319496 | tf_op jit(solution)/shard_map/ppermute | solution.py:166
  166.0 2.5 collective-permute-start.22
  168.7 2.4 collective-permute-start.25
  175.6 2.0 finish.1
  177.7 7.4 %all-to-all-start.1 = ((bf16[32,16,512]{2,1,0:T(8,128)(2,1)}), bf16[32,16,512]{2,1,0:T(8,128)(2,1)}, u32[]{:S(2)}, u32[]{:S(2)}) async-start(bf16[32,16,512]{2,1,0:T(8,128)(2,1)} %copy-done.7), calls=%async_computation.1 | async-start | bytes 1048576 | tf_op jit(solution)/shard_map/all_to_all | solution.py:547
  185.1 13.8 %all-to-all-done.1 = bf16[32,16,512]{2,1,0:T(8,128)(2,1)} async-done(((bf16[32,16,512]{2,1,0:T(8,128)(2,1)}), bf16[32,16,512]{2,1,0:T(8,128)(2,1)}, u32[]{:S(2)}, u32[]{:S(2)}) %all-to-all-start.1) | async-done | bytes 524320 | tf_op jit(solution)/shard_map/all_to_all | solution.py:547
  198.8 24.6 %factorize.1 = (bf16[32,512]{1,0:T(8,128)(2,1)}, bf16[512,512]{1,0:T(8,128)(2,1)}, f32[128,512]{1,0:T(8,128)}) custom-call(s32[1]{0:T(128)} %bitcast.1.at_ref, bf16[512,512]{1,0:T(8,128)(2,1)} %bitcast.8.g_ref, bf16[512,128]{1,0:T(8,128)(2,1)S(1)} %get-tuple-element.66.refs_0_, bf16[512,128]{1,0:T(8,128)(2,1)} %collective-permute-done.9.refs_1_, ...), custom_call_target="tpu_custom_call" | custom-call | flops 20000000000 | bytes 4194304 | tf_op jit(solution)/shard_map/factorize/pallas_call | solution.py:138
  223.4 5.0 %all-gather.5.cloned.1.call-done = bf16[2048,1664]{1,0:T(8,128)(2,1)} async-done(((bf16[64,1664]{1,0:T(8,128)(2,1)}), bf16[2048,1664]{1,0:T(8,128)(2,1)}) %all-gather.5.cloned.1.call-update) | async-done | bytes 6815760 | tf_op jit(solution)/shard_map/all_gather | solution.py:551
  228.4 3.6 %right_rows.1 = (f32[16,6656]{1,0:T(8,128)S(1)}, f32[16,128]{1,0:T(8,128)S(1)}, bf16[512,512]{1,0:T(8,128)(2,1)S(1)}, bf16[16,2,2,32,1664]{4,3,2,1,0:T(8,128)(2,1)S(1)}) custom-call(bf16[32,512]{1,0:T(8,128)(2,1)} %get-tuple-element.84.rows_hbm, bf16[512,512]{1,0:T(8,128)(2,1)} %get-tuple-element.85.weights_hbm, bf16[16,2,2,32,1664]{4,3,2,1,0:T(8,128)(2,1)} %bitcast.10), custom_call_target="tpu_custom_call" | custom-call | flops 218103808 | bytes 15147008 | tf_op jit(solution)/shard_map/right_rows/pallas_call | solution.py:180
  232.1 2.7 %collective-permute-start.28 = (f32[16,128]{1,0:T(8,128)S(1)}, f32[16,128]{1,0:T(8,128)S(1)}, u32[]{:S(2)}, u32[]{:S(2)}) collective-permute-start(f32[16,128]{1,0:T(8,128)S(1)} %get-tuple-element.90), channel_id=1, source_target_pairs={{0,3},{1,0},{2,1},{3,2},{4,7},{5,4},{6,5},{7,6},{8,11},{9,8},{10,9... | collective-permute-start | bytes 24584 | tf_op jit(solution)/shard_map/ppermute | solution.py:166
  235.9 6.6 %feedback.1 = bf16[512,6656]{1,0:T(8,128)(2,1)} custom-call(s32[1]{0:T(128)} %bitcast.at_ref, bf16[512,512]{1,0:T(8,128)(2,1)S(1)} %get-tuple-element.86.weights_ref, bf16[16,2,2,32,1664]{4,3,2,1,0:T(8,128)(2,1)S(1)} %get-tuple-element.87.total_ref, bf16[128,3328]{1,0:T(8,128)(2,1)S(1)} %add_convert_fusion.4.refs_0_.refs_4_, ...), custom_call_target="tpu_custom_call" | custom-call | flops 3489660928 | bytes 20971524 | tf_op jit(solution)/shard_map/feedback/pallas_call | solution.py:180
  (67 shorter events, 19.8 us)
Async XLA Ops:
  7.2 56.6 %all-gather.3.cloned.1.call-start = ((), (), s32[]{:S(2)}) async-start(), calls=%async_computation.2 | async-start | bytes 7028736 | tf_op jit(solution)/shard_map/all_gather | solution.py:512
  10.4 45.6 %collective-permute-start.4 = (bf16[128,3328]{1,0:T(8,128)(2,1)}, bf16[128,3328]{1,0:T(8,128)(2,1)S(1)}, u32[]{:S(2)}, u32[]{:S(2)}) collective-permute-start(bf16[128,3328]{1,0:T(8,128)(2,1)} %add_convert_fusion.7), channel_id=1, source_target_pairs={{0,2},{1,3},{2,0},{3,1},{4,6},{5,7},{6,4},{7,5},{8,10},{9,11},{10,... | collective-permute-start | bytes 2555912 | tf_op jit(solution)/shard_map/ppermute | solution.py:166
  17.4 38.6 %collective-permute-start.3 = (bf16[128,3328]{1,0:T(8,128)(2,1)}, bf16[128,3328]{1,0:T(8,128)(2,1)S(1)}, u32[]{:S(2)}, u32[]{:S(2)}) collective-permute-start(bf16[128,3328]{1,0:T(8,128)(2,1)} %add_convert_fusion.6), channel_id=1, source_target_pairs={{0,1},{1,2},{2,3},{3,0},{4,5},{5,6},{6,7},{7,4},{8,9},{9,10},{10,1... | collective-permute-start | bytes 2555912 | tf_op jit(solution)/shard_map/ppermute | solution.py:166
  20.7 31.9 %collective-permute-start.5 = (bf16[128,3328]{1,0:T(8,128)(2,1)}, bf16[128,3328]{1,0:T(8,128)(2,1)S(1)}, u32[]{:S(2)}, u32[]{:S(2)}) collective-permute-start(bf16[128,3328]{1,0:T(8,128)(2,1)} %add_convert_fusion.5), channel_id=1, source_target_pairs={{0,3},{1,0},{2,1},{3,2},{4,7},{5,4},{6,5},{7,6},{8,11},{9,8},{10,9... | collective-permute-start | bytes 2555912 | tf_op jit(solution)/shard_map/ppermute | solution.py:166
  29.4 42.4 %collective-permute-start = (bf16[128,3328]{1,0:T(8,128)(2,1)}, bf16[128,3328]{1,0:T(8,128)(2,1)}, u32[]{:S(2)}, u32[]{:S(2)}) collective-permute-start(bf16[128,3328]{1,0:T(8,128)(2,1)} %add_convert_fusion.2), channel_id=1, source_target_pairs={{0,1},{1,2},{2,3},{3,0},{4,5},{5,6},{6,7},{7,4},{8,9},{9,10},{10,1... | collective-permute-start | bytes 2555912 | tf_op jit(solution)/shard_map/ppermute | solution.py:166
  31.9 39.4 %collective-permute-start.2 = (bf16[128,3328]{1,0:T(8,128)(2,1)}, bf16[128,3328]{1,0:T(8,128)(2,1)}, u32[]{:S(2)}, u32[]{:S(2)}) collective-permute-start(bf16[128,3328]{1,0:T(8,128)(2,1)} %add_convert_fusion.1), channel_id=1, source_target_pairs={{0,3},{1,0},{2,1},{3,2},{4,7},{5,4},{6,5},{7,6},{8,11},{9,8},{10,9... | collective-permute-start | bytes 2555912 | tf_op jit(solution)/shard_map/ppermute | solution.py:166
  52.6 0.9 copy-start.2
  53.5 35.2 %collective-permute-start.1 = (bf16[128,3328]{1,0:T(8,128)(2,1)}, bf16[128,3328]{1,0:T(8,128)(2,1)}, u32[]{:S(2)}, u32[]{:S(2)}) collective-permute-start(bf16[128,3328]{1,0:T(8,128)(2,1)} %add_convert_fusion.3), channel_id=1, source_target_pairs={{0,2},{1,3},{2,0},{3,1},{4,6},{5,7},{6,4},{7,5},{8,10},{9,11},{10,... | collective-permute-start | bytes 2555912 | tf_op jit(solution)/shard_map/ppermute | solution.py:166
  63.8 2.9 %copy-start = (bf16[512,6656]{1,0:T(8,128)(2,1)S(1)}, bf16[512,6656]{1,0:T(8,128)(2,1)}, u32[]{:S(2)}) copy-start(bf16[512,6656]{1,0:T(8,128)(2,1)} %all-gather.3.cloned.1.call-done.refs_4_) | copy-start | bytes 20447236
  66.7 1.2 copy-start.3
  67.9 20.8 %copy-start.1 = (bf16[512,6656]{1,0:T(8,128)(2,1)S(1)}, bf16[512,6656]{1,0:T(8,128)(2,1)}, u32[]{:S(2)}) copy-start(bf16[512,6656]{1,0:T(8,128)(2,1)} %all-gather.3.cloned.1.call-done.refs_4_) | copy-start | bytes 20447236
  92.4 5.4 %collective-permute-start.6 = (bf16[128,512]{1,0:T(8,128)(2,1)S(1)}, bf16[128,512]{1,0:T(8,128)(2,1)S(1)}, u32[]{:S(2)}, u32[]{:S(2)}) collective-permute-start(bf16[128,512]{1,0:T(8,128)(2,1)S(1)} %get-tuple-element.56), channel_id=1, source_target_pairs={{0,2},{1,3},{2,0},{3,1},{4,6},{5,7},{6,4},{7,5},{8,10},{9,11},{10,... | collective-permute-start | bytes 393224 | tf_op jit(solution)/shard_map/ppermute | solution.py:166
  95.2 5.6 %collective-permute-start.7 = (bf16[128,512]{1,0:T(8,128)(2,1)S(1)}, bf16[128,512]{1,0:T(8,128)(2,1)S(1)}, u32[]{:S(2)}, u32[]{:S(2)}) collective-permute-start(bf16[128,512]{1,0:T(8,128)(2,1)S(1)} %get-tuple-element.57), channel_id=1, source_target_pairs={{0,3},{1,0},{2,1},{3,2},{4,7},{5,4},{6,5},{7,6},{8,11},{9,8},{10,9... | collective-permute-start | bytes 393224 | tf_op jit(solution)/shard_map/ppermute | solution.py:166
  95.6 5.7 %collective-permute-start.8 = (bf16[128,512]{1,0:T(8,128)(2,1)S(1)}, bf16[128,512]{1,0:T(8,128)(2,1)S(1)}, u32[]{:S(2)}, u32[]{:S(2)}) collective-permute-start(bf16[128,512]{1,0:T(8,128)(2,1)S(1)} %get-tuple-element.58), channel_id=1, source_target_pairs={{0,1},{1,2},{2,3},{3,0},{4,5},{5,6},{6,7},{7,4},{8,9},{9,10},{10,1... | collective-permute-start | bytes 393224 | tf_op jit(solution)/shard_map/ppermute | solution.py:166
  102.0 8.4 %collective-permute-start.11 = (bf16[512,128]{1,0:T(8,128)(2,1)S(1)}, bf16[512,128]{1,0:T(8,128)(2,1)}, u32[]{:S(2)}, u32[]{:S(2)}) collective-permute-start(bf16[512,128]{1,0:T(8,128)(2,1)S(1)} %get-tuple-element.66.refs_0_), channel_id=1, source_target_pairs={{0,3},{1,0},{2,1},{3,2},{4,7},{5,4},{6,5},{7,6},{8,11},{9,8},{10,9... | collective-permute-start | bytes 393224 | tf_op jit(solution)/shard_map/ppermute | solution.py:166
  105.0 5.5 %collective-permute-start.10 = (bf16[512,128]{1,0:T(8,128)(2,1)S(1)}, bf16[512,128]{1,0:T(8,128)(2,1)}, u32[]{:S(2)}, u32[]{:S(2)}) collective-permute-start(bf16[512,128]{1,0:T(8,128)(2,1)S(1)} %get-tuple-element.66.refs_0_), channel_id=1, source_target_pairs={{0,2},{1,3},{2,0},{3,1},{4,6},{5,7},{6,4},{7,5},{8,10},{9,11},{10,... | collective-permute-start | bytes 393224 | tf_op jit(solution)/shard_map/ppermute | solution.py:166
  105.0 8.0 %collective-permute-start.9 = (bf16[512,128]{1,0:T(8,128)(2,1)S(1)}, bf16[512,128]{1,0:T(8,128)(2,1)}, u32[]{:S(2)}, u32[]{:S(2)}) collective-permute-start(bf16[512,128]{1,0:T(8,128)(2,1)S(1)} %get-tuple-element.66.refs_0_), channel_id=1, source_target_pairs={{0,1},{1,2},{2,3},{3,0},{4,5},{5,6},{6,7},{7,4},{8,9},{9,10},{10,1... | collective-permute-start | bytes 393224 | tf_op jit(solution)/shard_map/ppermute | solution.py:166
  113.0 1.2 copy-start.4
  117.2 6.6 %collective-permute-start.12 = (bf16[4,128,1664]{2,1,0:T(8,128)(2,1)}, bf16[4,128,1664]{2,1,0:T(8,128)(2,1)}, u32[]{:S(2)}, u32[]{:S(2)}) collective-permute-start(bf16[4,128,1664]{2,1,0:T(8,128)(2,1)} %cross.3), channel_id=1, source_target_pairs={{0,4},{4,0},{1,5},{5,1},{2,6},{6,2},{3,7},{7,3},{8,12},{12,8},{9,1... | collective-permute-start | bytes 5111816 | tf_op jit(solution)/shard_map/ppermute | solution.py:170
  119.4 4.4 %copy-start.5 = (bf16[128,3328]{1,0:T(8,128)(2,1)S(1)}, bf16[128,3328]{1,0:T(8,128)(2,1)}, u32[]{:S(2)}) copy-start(bf16[128,3328]{1,0:T(8,128)(2,1)} %copy-done.2) | copy-start | bytes 2555908
  123.4 4.1 %collective-permute-start.13 = (bf16[4,128,1664]{2,1,0:T(8,128)(2,1)}, bf16[4,128,1664]{2,1,0:T(8,128)(2,1)S(1)}, u32[]{:S(2)}, u32[]{:S(2)}) collective-permute-start(bf16[4,128,1664]{2,1,0:T(8,128)(2,1)} %cross.2), channel_id=1, source_target_pairs={{0,4},{4,0},{1,5},{5,1},{2,6},{6,2},{3,7},{7,3},{8,12},{12,8},{9,1... | collective-permute-start | bytes 5111816 | tf_op jit(solution)/shard_map/ppermute | solution.py:170
  127.5 3.9 %copy-start.8 = (bf16[128,1664]{1,0:T(8,128)(2,1)S(1)}, bf16[128,1664]{1,0:T(8,128)(2,1)}, u32[]{:S(2)}) copy-start(bf16[128,1664]{1,0:T(8,128)(2,1)} %get-tuple-element.65) | copy-start | bytes 1277956
  131.4 12.7 %collective-permute-start.14 = (bf16[128,1664]{1,0:T(8,128)(2,1)S(1)}, bf16[128,1664]{1,0:T(8,128)(2,1)}, u32[]{:S(2)}, u32[]{:S(2)}) collective-permute-start(bf16[128,1664]{1,0:T(8,128)(2,1)S(1)} %copy-done.8), channel_id=1, source_target_pairs={{0,16},{8,24},{16,0},{24,8},{1,17},{9,25},{17,1},{25,9},{2,18},{10... | collective-permute-start | bytes 1277960 | tf_op jit(solution)/shard_map/ppermute | solution.py:166
  134.2 22.4 %collective-permute-start.15 = (bf16[128,1664]{1,0:T(8,128)(2,1)}, bf16[128,1664]{1,0:T(8,128)(2,1)}, u32[]{:S(2)}, u32[]{:S(2)}) collective-permute-start(bf16[128,1664]{1,0:T(8,128)(2,1)} %get-tuple-element.68), channel_id=1, source_target_pairs={{0,8},{8,16},{16,24},{24,0},{1,9},{9,17},{17,25},{25,1},{2,10},{10... | collective-permute-start | bytes 1277960 | tf_op jit(solution)/shard_map/ppermute | solution.py:166
  134.5 22.1 %collective-permute-start.16 = (bf16[128,1664]{1,0:T(8,128)(2,1)}, bf16[128,1664]{1,0:T(8,128)(2,1)}, u32[]{:S(2)}, u32[]{:S(2)}) collective-permute-start(bf16[128,1664]{1,0:T(8,128)(2,1)} %get-tuple-element.70), channel_id=1, source_target_pairs={{0,24},{8,0},{16,8},{24,16},{1,25},{9,1},{17,9},{25,17},{2,26},{10... | collective-permute-start | bytes 1277960 | tf_op jit(solution)/shard_map/ppermute | solution.py:166
  136.9 19.7 %collective-permute-start.17 = (bf16[128,1664]{1,0:T(8,128)(2,1)}, bf16[128,1664]{1,0:T(8,128)(2,1)}, u32[]{:S(2)}, u32[]{:S(2)}) collective-permute-start(bf16[128,1664]{1,0:T(8,128)(2,1)} %get-tuple-element.71), channel_id=1, source_target_pairs={{0,32},{32,64},{64,96},{96,0},{1,33},{33,65},{65,97},{97,1},{2,34}... | collective-permute-start | bytes 1277960 | tf_op jit(solution)/shard_map/ppermute | solution.py:166
  138.2 20.6 %collective-permute-start.18 = (bf16[128,1664]{1,0:T(8,128)(2,1)}, bf16[128,1664]{1,0:T(8,128)(2,1)}, u32[]{:S(2)}, u32[]{:S(2)}) collective-permute-start(bf16[128,1664]{1,0:T(8,128)(2,1)} %get-tuple-element.72), channel_id=1, source_target_pairs={{0,64},{32,96},{64,0},{96,32},{1,65},{33,97},{65,1},{97,33},{2,66}... | collective-permute-start | bytes 1277960 | tf_op jit(solution)/shard_map/ppermute | solution.py:166
  144.1 14.7 %collective-permute-start.19 = (bf16[128,1664]{1,0:T(8,128)(2,1)}, bf16[128,1664]{1,0:T(8,128)(2,1)}, u32[]{:S(2)}, u32[]{:S(2)}) collective-permute-start(bf16[128,1664]{1,0:T(8,128)(2,1)} %get-tuple-element.73), channel_id=1, source_target_pairs={{0,96},{32,0},{64,32},{96,64},{1,97},{33,1},{65,33},{97,65},{2,98}... | collective-permute-start | bytes 1277960 | tf_op jit(solution)/shard_map/ppermute | solution.py:166
  149.4 21.8 %all-to-all-start = ((bf16[32,16,512]{2,1,0:T(8,128)(2,1)}), bf16[32,16,512]{2,1,0:T(8,128)(2,1)}, u32[]{:S(2)}, u32[]{:S(2)}) async-start(bf16[32,16,512]{2,1,0:T(8,128)(2,1)} %bitcast.11), calls=%async_computation | async-start | bytes 1048576 | tf_op jit(solution)/shard_map/all_to_all | solution.py:540
  156.5 72.0 %all-gather.5.cloned.1.call-start = ((), (), s32[]{:S(2)}) async-start(), calls=%async_computation.3 | async-start | bytes 7028736 | tf_op jit(solution)/shard_map/all_gather | solution.py:551
  162.3 6.5 %collective-permute-start.20 = (bf16[32,1664]{1,0:T(8,128)(2,1)}, bf16[32,1664]{1,0:T(8,128)(2,1)}, u32[]{:S(2)}, u32[]{:S(2)}) collective-permute-start(bf16[32,1664]{1,0:T(8,128)(2,1)} %get-tuple-element.76), channel_id=1, source_target_pairs={{0,32},{32,64},{64,96},{96,0},{1,33},{33,65},{65,97},{97,1},{2,34}... | collective-permute-start | bytes 319496 | tf_op jit(solution)/shard_map/ppermute | solution.py:166
  166.0 7.1 %collective-permute-start.21 = (bf16[32,1664]{1,0:T(8,128)(2,1)}, bf16[32,1664]{1,0:T(8,128)(2,1)}, u32[]{:S(2)}, u32[]{:S(2)}) collective-permute-start(bf16[32,1664]{1,0:T(8,128)(2,1)} %get-tuple-element.77), channel_id=1, source_target_pairs={{0,64},{32,96},{64,0},{96,32},{1,65},{33,97},{65,1},{97,33},{2,66}... | collective-permute-start | bytes 319496 | tf_op jit(solution)/shard_map/ppermute | solution.py:166
  166.0 7.1 %collective-permute-start.22 = (bf16[32,1664]{1,0:T(8,128)(2,1)}, bf16[32,1664]{1,0:T(8,128)(2,1)}, u32[]{:S(2)}, u32[]{:S(2)}) collective-permute-start(bf16[32,1664]{1,0:T(8,128)(2,1)} %get-tuple-element.78), channel_id=1, source_target_pairs={{0,96},{32,0},{64,32},{96,64},{1,97},{33,1},{65,33},{97,65},{2,98}... | collective-permute-start | bytes 319496 | tf_op jit(solution)/shard_map/ppermute | solution.py:166
  168.5 5.9 %collective-permute-start.23 = (bf16[32,1664]{1,0:T(8,128)(2,1)}, bf16[32,1664]{1,0:T(8,128)(2,1)}, u32[]{:S(2)}, u32[]{:S(2)}) collective-permute-start(bf16[32,1664]{1,0:T(8,128)(2,1)} %get-tuple-element.80), channel_id=1, source_target_pairs={{0,8},{8,16},{16,24},{24,0},{1,9},{9,17},{17,25},{25,1},{2,10},{10... | collective-permute-start | bytes 319496 | tf_op jit(solution)/shard_map/ppermute | solution.py:166
  168.5 6.4 %collective-permute-start.24 = (bf16[32,1664]{1,0:T(8,128)(2,1)}, bf16[32,1664]{1,0:T(8,128)(2,1)}, u32[]{:S(2)}, u32[]{:S(2)}) collective-permute-start(bf16[32,1664]{1,0:T(8,128)(2,1)} %get-tuple-element.81), channel_id=1, source_target_pairs={{0,16},{8,24},{16,0},{24,8},{1,17},{9,25},{17,1},{25,9},{2,18},{10... | collective-permute-start | bytes 319496 | tf_op jit(solution)/shard_map/ppermute | solution.py:166
  168.7 6.9 %collective-permute-start.25 = (bf16[32,1664]{1,0:T(8,128)(2,1)}, bf16[32,1664]{1,0:T(8,128)(2,1)}, u32[]{:S(2)}, u32[]{:S(2)}) collective-permute-start(bf16[32,1664]{1,0:T(8,128)(2,1)} %get-tuple-element.82), channel_id=1, source_target_pairs={{0,24},{8,0},{16,8},{24,16},{1,25},{9,1},{17,9},{25,17},{2,26},{10... | collective-permute-start | bytes 319496 | tf_op jit(solution)/shard_map/ppermute | solution.py:166
  172.3 0.8 copy-start.7
  177.7 21.2 %all-to-all-start.1 = ((bf16[32,16,512]{2,1,0:T(8,128)(2,1)}), bf16[32,16,512]{2,1,0:T(8,128)(2,1)}, u32[]{:S(2)}, u32[]{:S(2)}) async-start(bf16[32,16,512]{2,1,0:T(8,128)(2,1)} %copy-done.7), calls=%async_computation.1 | async-start | bytes 1048576 | tf_op jit(solution)/shard_map/all_to_all | solution.py:547
  228.4 7.4 %copy-start.6 = (bf16[128,3328]{1,0:T(8,128)(2,1)S(1)}, bf16[128,3328]{1,0:T(8,128)(2,1)}, u32[]{:S(2)}) copy-start(bf16[128,3328]{1,0:T(8,128)(2,1)} %copy-done.2) | copy-start | bytes 2555908
  232.1 10.4 %collective-permute-start.28 = (f32[16,128]{1,0:T(8,128)S(1)}, f32[16,128]{1,0:T(8,128)S(1)}, u32[]{:S(2)}, u32[]{:S(2)}) collective-permute-start(f32[16,128]{1,0:T(8,128)S(1)} %get-tuple-element.90), channel_id=1, source_target_pairs={{0,3},{1,0},{2,1},{3,2},{4,7},{5,4},{6,5},{7,6},{8,11},{9,8},{10,9... | collective-permute-start | bytes 24584 | tf_op jit(solution)/shard_map/ppermute | solution.py:166
  234.8 7.6 %collective-permute-start.27 = (f32[16,128]{1,0:T(8,128)S(1)}, f32[16,128]{1,0:T(8,128)S(1)}, u32[]{:S(2)}, u32[]{:S(2)}) collective-permute-start(f32[16,128]{1,0:T(8,128)S(1)} %get-tuple-element.90), channel_id=1, source_target_pairs={{0,2},{1,3},{2,0},{3,1},{4,6},{5,7},{6,4},{7,5},{8,10},{9,11},{10,... | collective-permute-start | bytes 24584 | tf_op jit(solution)/shard_map/ppermute | solution.py:166
  235.2 7.2 %collective-permute-start.26 = (f32[16,128]{1,0:T(8,128)S(1)}, f32[16,128]{1,0:T(8,128)S(1)}, u32[]{:S(2)}, u32[]{:S(2)}) collective-permute-start(f32[16,128]{1,0:T(8,128)S(1)} %get-tuple-element.90), channel_id=1, source_target_pairs={{0,1},{1,2},{2,3},{3,0},{4,5},{5,6},{6,7},{7,4},{8,9},{9,10},{10,1... | collective-permute-start | bytes 24584 | tf_op jit(solution)/shard_map/ppermute | solution.py:166
Sparse Core Ops, SparseCore 0:
  10.2 53.4 all-gather.2
  177.8 50.6 all-gather.4
